TPU v7x, 128 devices: a whole 4x4x4 slice. The times are simulated.
128 devices in a mesh: row: 8 (over y, z_hi), col: 16 (over x, z_lo, core).
Axes of the slice: x: 4, y: 4, z: 4 (z_hi: 2, z_lo: 2; z = z_hi * 2 + z_lo), core: 2. Of those that a mesh axis runs over, the one named last changes fastest.
Arguments:
- queries: bfloat16 [64, 3072, 128], P('row', 'col'), may hold values from -48 to 48
- keys: bfloat16 [64, 3072, 128], P('row', 'col'), may hold values from -48 to 48
- values: bfloat16 [64, 3072, 128], P('row', 'col'), may hold values from -6 to 6
- gate_logits: bfloat16 [64, 3072, 128], P('row', 'col'), may hold values from -6 to 6
- out_grad: bfloat16 [64, 3072, 128], P('row', 'col'), may hold values from -96 to 96
- pair_bias: bfloat16 [4, 3072, 3072], P(None, 'col', 'row'), may hold values from -6 to 6
- residue_mask: int32 [3072], replicated, may hold values 0 or 1
- query_weight: bfloat16 [128, 128], replicated, may hold values from -0.5 to 0.5
- pair_cotangent: bfloat16 [64, 3072, 128], P('row', 'col'), may hold values from -6 to 6
- right_proj: bfloat16 [3072, 3072, 128], P('col', 'row'), may hold values from -0.109375 to 0.109375
Outputs:
- grad_queries: bfloat16 [64, 3072, 128], P('row', 'col')
- grad_keys: bfloat16 [64, 3072, 128], P('row', 'col')
- grad_values: bfloat16 [64, 3072, 128], P('row', 'col')
- grad_gate_logits: bfloat16 [64, 3072, 128], P('row', 'col')
- grad_bias: float32 [4, 3072, 3072], P(None, 'col', 'row')
- grad_left: bfloat16 [64, 3072, 128], P('col', 'row')
All inputs are finite; a program needn't handle non-finite values.
Results may differ from a plain program's by a relative error of at most 0.039.
Values may be sent and summed in bfloat16 or wider, within the bound.
No kernel may reach another device: no remote copies, remote signals or barrier semaphores. Data moves between devices by JAX's collectives and lax.ppermute only.
A program may use at most 192 MiB of HBM per device.

v0:
```python
import math

import jax
import jax.numpy as jnp
from jax import lax
from jax.sharding import PartitionSpec as P

big_penalty = 1000000000.0


def row_backward(q_row, k_full, v_full, gate_row, cot_row, bias_plus, score_scale):
    length, channels = q_row.shape
    head_count = bias_plus.shape[0]
    head_size = channels // head_count
    q_heads = q_row.reshape(length, head_count, head_size)
    k_heads = k_full.reshape(k_full.shape[0], head_count, head_size)
    v_heads = v_full.reshape(v_full.shape[0], head_count, head_size)
    scores = (
        jnp.einsum("jhd,khd->hjk", q_heads, k_heads, preferred_element_type=jnp.float32)
        * score_scale
        + bias_plus
    )
    row_top = jnp.max(scores, axis=-1, keepdims=True)
    exponent = jnp.exp(scores - row_top)
    soft_weights = exponent / jnp.sum(exponent, axis=-1, keepdims=True)
    weights_b = soft_weights.astype(jnp.bfloat16)
    attended = jnp.einsum("hjk,khd->jhd", weights_b, v_heads, preferred_element_type=jnp.float32)
    gate_value = jax.nn.sigmoid(gate_row.astype(jnp.float32)).reshape(length, head_count, head_size)
    cot_heads = cot_row.astype(jnp.float32).reshape(length, head_count, head_size)
    gate_grad = (
        (cot_heads * attended * gate_value * (1.0 - gate_value))
        .reshape(length, channels)
        .astype(jnp.bfloat16)
    )
    d_out = (cot_heads * gate_value).astype(jnp.bfloat16)
    d_weights = jnp.einsum("jhd,khd->hjk", d_out, v_heads, preferred_element_type=jnp.float32)
    row_delta = jnp.sum(d_out.astype(jnp.float32) * attended, axis=-1)
    d_scores = soft_weights * (d_weights - jnp.transpose(row_delta)[:, :, None])
    d_scores_b = d_scores.astype(jnp.bfloat16)
    grad_q = (
        (
            jnp.einsum("hjk,khd->jhd", d_scores_b, k_heads, preferred_element_type=jnp.float32)
            * score_scale
        )
        .reshape(length, channels)
        .astype(jnp.bfloat16)
    )
    key_term = (
        jnp.einsum("hjk,jhd->khd", d_scores_b, q_heads, preferred_element_type=jnp.float32)
        * score_scale
    ).reshape(-1, channels)
    value_term = jnp.einsum(
        "hjk,jhd->khd", weights_b, d_out, preferred_element_type=jnp.float32
    ).reshape(-1, channels)
    return (grad_q, gate_grad, key_term, value_term, d_scores)


def local(
    queries,
    keys,
    values,
    gate_logits,
    out_grad,
    pair_bias,
    residue_mask,
    query_weight,
    pair_cotangent,
    right_proj,
):
    channels = queries.shape[2]
    head_count = pair_bias.shape[0]
    score_scale = 1.0 / math.sqrt(channels // head_count)
    bias_whole = lax.all_gather(pair_bias, "row", axis=2, tiled=True)
    penalty = big_penalty * (residue_mask.astype(jnp.float32) - 1.0)
    bias_plus = bias_whole.astype(jnp.float32) + penalty[None, None, :]
    start_total = jnp.zeros(bias_plus.shape, jnp.float32)
    k_whole, v_whole = (
        lax.all_gather(keys, "col", axis=1, tiled=True),
        lax.all_gather(values, "col", axis=1, tiled=True),
    )

    def whole_step(running, band_row):
        q_row, k_full, v_full, gate_row, cot_row = band_row
        grad_q, gate_grad, key_term, value_term, d_scores = row_backward(
            q_row, k_full, v_full, gate_row, cot_row, bias_plus, score_scale
        )
        return (running + d_scores, (grad_q, gate_grad, key_term, value_term))

    score_total, (grad_queries, grad_gates, key_terms, value_terms) = lax.scan(
        whole_step, start_total, (queries, k_whole, v_whole, gate_logits, out_grad)
    )
    key_sums, value_sums = (
        lax.psum_scatter(
            key_terms.astype(jnp.bfloat16), "col", scatter_dimension=1, tiled=True
        ).astype(jnp.float32),
        lax.psum_scatter(
            value_terms.astype(jnp.bfloat16), "col", scatter_dimension=1, tiled=True
        ).astype(jnp.float32),
    )
    grad_keys = key_sums.astype(jnp.bfloat16)
    grad_values = value_sums.astype(jnp.bfloat16)
    grad_bias = lax.psum_scatter(
        score_total.astype(jnp.bfloat16), "row", scatter_dimension=2, tiled=True
    ).astype(jnp.float32)
    flat_grads = grad_queries.reshape(-1, channels)
    carried = (
        pair_cotangent.astype(jnp.float32)
        + jnp.einsum(
            "me,ce->mc", flat_grads, query_weight, preferred_element_type=jnp.float32
        ).reshape(pair_cotangent.shape)
    ).astype(jnp.bfloat16)
    gathered = lax.all_gather(carried, "row", axis=0, tiled=True)
    left_sum = lax.psum_scatter(
        jnp.einsum("ijc,jkc->ikc", gathered, right_proj, preferred_element_type=jnp.float32).astype(
            jnp.bfloat16
        ),
        "col",
        scatter_dimension=0,
        tiled=True,
    )
    return (grad_queries, grad_keys, grad_values, grad_gates, grad_bias, left_sum)


def solution(mesh):
    in_specs = (
        P("row", "col", None),
        P("row", "col", None),
        P("row", "col", None),
        P("row", "col", None),
        P("row", "col", None),
        P(None, "col", "row"),
        P(),
        P(),
        P("row", "col", None),
        P("col", "row", None),
    )
    out_specs = (
        P("row", "col", None),
        P("row", "col", None),
        P("row", "col", None),
        P("row", "col", None),
        P(None, "col", "row"),
        P("col", "row", None),
    )
    return jax.shard_map(local, mesh=mesh, in_specs=in_specs, out_specs=out_specs, check_vma=False)
```

profile of v0, /device:TPU:0, one launch (start us, length us, event | category | flops | bytes accessed | tf_op | source)
XLA Modules:
  0.0 982.1 jit_solution(7346316889384517511)
XLA Ops:
  15.1 81.2 %all-gather.7.cloned.1.call-done = bf16[4,192,3072]{2,1,0:T(8,128)(2,1)} async-done(((bf16[4,192,384]{2,1,0:T(8,128)(2,1)}), bf16[4,192,3072]{2,1,0:T(8,128)(2,1)}) %all-gather.7.cloned.1.call-update) | async-done | bytes 4718608 | tf_op jit(solution)/shard_map/all_gather | solution.py:73
  103.6 36.0 %all-gather.5.cloned.1.call-done = bf16[8,3072,128]{2,0,1:T(8,128)(2,1)} async-done(((bf16[8,192,128]{2,0,1:T(8,128)(2,1)}), bf16[8,3072,128]{2,0,1:T(8,128)(2,1)}) %all-gather.5.cloned.1.call-update) | async-done | bytes 6291472 | tf_op jit(solution)/shard_map/all_gather | solution.py:78
  139.6 9.0 copy.31
  148.6 36.4 %all-gather.9.cloned.1.call-done = bf16[8,3072,128]{2,0,1:T(8,128)(2,1)} async-done(((bf16[8,192,128]{2,0,1:T(8,128)(2,1)}), bf16[8,3072,128]{2,0,1:T(8,128)(2,1)}) %all-gather.9.cloned.1.call-update) | async-done | bytes 6291472 | tf_op jit(solution)/shard_map/all_gather | solution.py:79
  185.0 8.9 copy.34
  194.0 369.2 %while.19 = (s32[]{:T(128)}, f32[4,192,3072]{2,1,0:T(8,128)}, bf16[8,192,128]{1,2,0:T(8,128)(2,1)}, bf16[8,192,128]{2,1,0:T(8,128)(2,1)}, bf16[8,3072,128]{2,1,0...) while((s32[]{:T(128)}, f32[4,192,3072]{2,1,0:T(8,128)}, ...), condition=%wide.region_4.5_spmd.clone, body=%wide.region_0.4_spmd.clone.sunk | while | flops 935487744 | bytes 138396384 | solution.py:89
  239.1 7.7 fusion.63
  262.6 10.9 %select_add_fusion.2 = (f32[4,192,3072]{2,1,0:T(8,128)}, bf16[4,192,3072]{2,1,0:T(8,128)(2,1)S(1)}) fusion(f32[4,192,3072]{2,1,0:T(8,128)} %get-tuple-element.293, pred[]{:T(512)S(6)} %compare.3, f32[4,192]{1,0:T(4,128)S(1)} %bitcast.99, bf16[192,4,32]{0,2,1:T(8,128)(2,1)S(1)} %get-tuple-element.272, bf16[3072,4,32]{0,2,1:T(8,128)(2,1)S(1)} %bitcast.90, ...), kind=kOutput, calls=%fused_computation.1.clone.1 | convolution fusion | flops 165150720 | bytes 33871872 | tf_op jit(solution)/shard_map/while/body/eval_jaxpr/jhd,khd->hjk/dot_general | solution.py:36
  309.2 10.9 %select_add_fusion.2 = (f32[4,192,3072]{2,1,0:T(8,128)}, bf16[4,192,3072]{2,1,0:T(8,128)(2,1)S(1)}) fusion(f32[4,192,3072]{2,1,0:T(8,128)} %get-tuple-element.293, pred[]{:T(512)S(6)} %compare.3, f32[4,192]{1,0:T(4,128)S(1)} %bitcast.99, bf16[192,4,32]{0,2,1:T(8,128)(2,1)S(1)} %get-tuple-element.272, bf16[3072,4,32]{0,2,1:T(8,128)(2,1)S(1)} %bitcast.90, ...), kind=kOutput, calls=%fused_computation.1.clone.1 | convolution fusion | flops 165150720 | bytes 33871872 | tf_op jit(solution)/shard_map/while/body/eval_jaxpr/jhd,khd->hjk/dot_general | solution.py:36
  355.8 10.9 %select_add_fusion.2 = (f32[4,192,3072]{2,1,0:T(8,128)}, bf16[4,192,3072]{2,1,0:T(8,128)(2,1)S(1)}) fusion(f32[4,192,3072]{2,1,0:T(8,128)} %get-tuple-element.293, pred[]{:T(512)S(6)} %compare.3, f32[4,192]{1,0:T(4,128)S(1)} %bitcast.99, bf16[192,4,32]{0,2,1:T(8,128)(2,1)S(1)} %get-tuple-element.272, bf16[3072,4,32]{0,2,1:T(8,128)(2,1)S(1)} %bitcast.90, ...), kind=kOutput, calls=%fused_computation.1.clone.1 | convolution fusion | flops 165150720 | bytes 33871872 | tf_op jit(solution)/shard_map/while/body/eval_jaxpr/jhd,khd->hjk/dot_general | solution.py:36
  402.5 10.9 %select_add_fusion.2 = (f32[4,192,3072]{2,1,0:T(8,128)}, bf16[4,192,3072]{2,1,0:T(8,128)(2,1)S(1)}) fusion(f32[4,192,3072]{2,1,0:T(8,128)} %get-tuple-element.293, pred[]{:T(512)S(6)} %compare.3, f32[4,192]{1,0:T(4,128)S(1)} %bitcast.99, bf16[192,4,32]{0,2,1:T(8,128)(2,1)S(1)} %get-tuple-element.272, bf16[3072,4,32]{0,2,1:T(8,128)(2,1)S(1)} %bitcast.90, ...), kind=kOutput, calls=%fused_computation.1.clone.1 | convolution fusion | flops 165150720 | bytes 33871872 | tf_op jit(solution)/shard_map/while/body/eval_jaxpr/jhd,khd->hjk/dot_general | solution.py:36
  449.1 10.9 %select_add_fusion.2 = (f32[4,192,3072]{2,1,0:T(8,128)}, bf16[4,192,3072]{2,1,0:T(8,128)(2,1)S(1)}) fusion(f32[4,192,3072]{2,1,0:T(8,128)} %get-tuple-element.293, pred[]{:T(512)S(6)} %compare.3, f32[4,192]{1,0:T(4,128)S(1)} %bitcast.99, bf16[192,4,32]{0,2,1:T(8,128)(2,1)S(1)} %get-tuple-element.272, bf16[3072,4,32]{0,2,1:T(8,128)(2,1)S(1)} %bitcast.90, ...), kind=kOutput, calls=%fused_computation.1.clone.1 | convolution fusion | flops 165150720 | bytes 33871872 | tf_op jit(solution)/shard_map/while/body/eval_jaxpr/jhd,khd->hjk/dot_general | solution.py:36
  495.7 10.9 %select_add_fusion.2 = (f32[4,192,3072]{2,1,0:T(8,128)}, bf16[4,192,3072]{2,1,0:T(8,128)(2,1)S(1)}) fusion(f32[4,192,3072]{2,1,0:T(8,128)} %get-tuple-element.293, pred[]{:T(512)S(6)} %compare.3, f32[4,192]{1,0:T(4,128)S(1)} %bitcast.99, bf16[192,4,32]{0,2,1:T(8,128)(2,1)S(1)} %get-tuple-element.272, bf16[3072,4,32]{0,2,1:T(8,128)(2,1)S(1)} %bitcast.90, ...), kind=kOutput, calls=%fused_computation.1.clone.1 | convolution fusion | flops 165150720 | bytes 33871872 | tf_op jit(solution)/shard_map/while/body/eval_jaxpr/jhd,khd->hjk/dot_general | solution.py:36
  542.2 10.9 %select_add_fusion.2 = (f32[4,192,3072]{2,1,0:T(8,128)}, bf16[4,192,3072]{2,1,0:T(8,128)(2,1)S(1)}) fusion(f32[4,192,3072]{2,1,0:T(8,128)} %get-tuple-element.293, pred[]{:T(512)S(6)} %compare.3, f32[4,192]{1,0:T(4,128)S(1)} %bitcast.99, bf16[192,4,32]{0,2,1:T(8,128)(2,1)S(1)} %get-tuple-element.272, bf16[3072,4,32]{0,2,1:T(8,128)(2,1)S(1)} %bitcast.90, ...), kind=kOutput, calls=%fused_computation.1.clone.1 | convolution fusion | flops 165150720 | bytes 33871872 | tf_op jit(solution)/shard_map/while/body/eval_jaxpr/jhd,khd->hjk/dot_general | solution.py:36
  573.9 10.2 %copy.43 = bf16[4,192,3072]{1,0,2:T(4,128)(2,1)} copy(bf16[4,192,3072]{2,1,0:T(8,128)(2,1)} %convert_element_type.91) | data formatting | bytes 9437184
  584.1 11.6 %reshape.80 = bf16[3072,768]{1,0:T(8,128)(2,1)} reshape(bf16[3072,4,192]{2,1,0:T(4,128)(2,1)} %bitcast.91) | data formatting | bytes 9437184
  597.1 24.6 %copy.38 = bf16[192,384,128]{1,0,2:T(8,128)(2,1)} copy(bf16[192,384,128]{2,1,0:T(8,128)(2,1)} %param.21) | data formatting | bytes 37748736 | tf_op args[9]
  621.7 24.6 %all-gather.11.cloned.1.call-done = bf16[64,192,128]{1,0,2:T(8,128)(2,1)} async-done(((bf16[8,192,128]{1,0,2:T(8,128)(2,1)}), bf16[64,192,128]{1,0,2:T(8,128)(2,1)}) %all-gather.11.cloned.1.call-update) | async-done | bytes 3145744 | tf_op jit(solution)/shard_map/all_gather | solution.py:112
  646.3 15.1 %convert_bitcast_fusion = bf16[64,384,128]{1,0,2:T(8,128)(2,1)} fusion(bf16[64,192,128]{1,0,2:T(8,128)(2,1)} %all-gather.11.cloned.1.call-done, bf16[192,384,128]{1,0,2:T(8,128)(2,1)} %copy.38), kind=kOutput, calls=%fused_computation.32 | convolution fusion | flops 1211105280 | bytes 28311552 | tf_op jit(solution)/shard_map/ijc,jkc->ikc/dot_general | solution.py:114
  661.4 9.1 copy.39
  672.5 64.8 %reduce-scatter.13.cloned.1.call-done = bf16[384,768]{1,0:T(8,128)(2,1)} async-done(((bf16[3072,768]{1,0:T(8,128)(2,1)}), bf16[384,768]{1,0:T(8,128)(2,1)}) %reduce-scatter.13.cloned.1.call-update) | async-done | bytes 589840
  741.6 72.6 %reduce-scatter.7.cloned.1.call-done = bf16[8,192,128]{2,1,0:T(8,128)(2,1)} async-done(((bf16[8,3072,128]{2,1,0:T(8,128)(2,1)}), bf16[8,192,128]{2,1,0:T(8,128)(2,1)}) %reduce-scatter.7.cloned.1.call-update) | async-done | bytes 393232 | tf_op jit(solution)/shard_map/reduce_scatter | solution.py:93
  814.2 80.5 %reduce-scatter.9.cloned.1.call-done = bf16[8,192,128]{2,1,0:T(8,128)(2,1)} async-done(((bf16[8,3072,128]{2,1,0:T(8,128)(2,1)}), bf16[8,192,128]{2,1,0:T(8,128)(2,1)}) %reduce-scatter.9.cloned.1.call-update) | async-done | bytes 393232 | tf_op jit(solution)/shard_map/reduce_scatter | solution.py:96
  894.7 80.5 %reduce-scatter.11.cloned.1.call-done = bf16[4,384,128]{2,1,0:T(8,128)(2,1)} async-done(((bf16[64,384,128]{2,1,0:T(8,128)(2,1)}), bf16[4,384,128]{2,1,0:T(8,128)(2,1)}) %reduce-scatter.11.cloned.1.call-update) | async-done | bytes 393232 | tf_op jit(solution)/shard_map/reduce_scatter | solution.py:113
  (238 shorter events, 318.2 us)
Async XLA Ops:
  7.2 556.1 %copy-start = (bf16[128,128]{1,0:T(8,128)(2,1)S(1)}, bf16[128,128]{1,0:T(8,128)(2,1)}, u32[]{:S(2)}) copy-start(bf16[128,128]{1,0:T(8,128)(2,1)} %param.19) | copy-start | bytes 98308
  7.2 89.1 %all-gather.7.cloned.1.call-start = ((), (), s32[]{:S(2)}) async-start(), calls=%async_computation.5 | async-start | bytes 5308416 | tf_op jit(solution)/shard_map/all_gather | solution.py:73
  7.9 131.7 %all-gather.5.cloned.1.call-start = ((), (), s32[]{:S(2)}) async-start(), calls=%async_computation.4 | async-start | bytes 6684672 | tf_op jit(solution)/shard_map/all_gather | solution.py:78
  10.0 175.0 %all-gather.9.cloned.1.call-start = ((), (), s32[]{:S(2)}) async-start(), calls=%async_computation.6 | async-start | bytes 6684672 | tf_op jit(solution)/shard_map/all_gather | solution.py:79
  12.1 634.2 %all-gather.11.cloned.1.call-start = ((), (), s32[]{:S(2)}) async-start(), calls=%async_computation.9 | async-start | bytes 4718592 | tf_op jit(solution)/shard_map/all_gather | solution.py:112
  214.1 4.1 copy-start.1
  226.8 2.2 copy-start.2
  257.1 4.1 copy-start.1
  273.5 2.2 copy-start.2
  303.7 4.1 copy-start.1
  320.1 2.2 copy-start.2
  350.3 4.1 copy-start.1
  366.6 2.2 copy-start.2
  397.0 4.1 copy-start.1
  443.6 4.1 copy-start.1
  459.9 2.2 copy-start.2
  490.2 4.1 copy-start.1
  506.5 2.2 copy-start.2
  536.8 4.1 copy-start.1
  553.1 2.2 copy-start.2
  567.1 170.2 %reduce-scatter.13.cloned.1.call-start = ((), (), s32[]{:S(2)}) async-start(), calls=%async_computation.11 | async-start | bytes 5308416
  595.7 218.5 %reduce-scatter.7.cloned.1.call-start = ((), (), s32[]{:S(2)}) async-start(), calls=%async_computation.7 | async-start | bytes 6684672 | tf_op jit(solution)/shard_map/reduce_scatter | solution.py:93
  596.3 298.4 %reduce-scatter.9.cloned.1.call-start = ((), (), s32[]{:S(2)}) async-start(), calls=%async_computation.8 | async-start | bytes 6684672 | tf_op jit(solution)/shard_map/reduce_scatter | solution.py:96
  597.1 378.2 %reduce-scatter.11.cloned.1.call-start = ((), (), s32[]{:S(2)}) async-start(), calls=%async_computation.10 | async-start | bytes 6684672 | tf_op jit(solution)/shard_map/reduce_scatter | solution.py:113
  (2 other events, 3.3 us)
Sparse Core Ops, SparseCore 0:
  10.2 86.0 all-gather.6
  98.6 40.9 all-gather.4
  141.9 43.1 all-gather.8
  567.2 79.0 all-gather.10
  650.1 87.1 reduce-scatter.12
  740.3 73.9 reduce-scatter.6
  817.4 77.3 reduce-scatter.8
  897.9 77.3 reduce-scatter.10
where the time goes:
time: 989 us; the launch traced here: 982 us
  waiting for transfers between devices  479 us (48%)
  matrix products  241 us (24%)
  local copies, waits for them, and re-layouts  171 us (17%)
  other arithmetic  76.2 us (8%)
  between operations  14.2 us (1%)
    dot_general x8, matrix products, row_backward(): jnp.einsum('jhd,khd->hjk', d_out, v_heads, preferred_element_type=jnp.flo...  83.3 us
    all_gather x1, waiting for transfers between devices, local(): bias_whole = lax.all_gather(pair_bias, 'row', axis=2, tiled=True)  81.2 us
    reduce_scatter x1, waiting for transfers between devices, local(): lax.psum_scatter(jnp.einsum('ijc,jkc->ikc', gathered, right_proj, preferr...  80.5 us
    reduce_scatter x1, waiting for transfers between devices, local(): lax.psum_scatter(value_terms.astype(jnp.bfloat16), 'col', scatter_dimensi...  80.5 us
    unnamed x15, local copies, waits for them, and re-layouts  75.7 us
    reduce_scatter x1, waiting for transfers between devices, local(): lax.psum_scatter(key_terms.astype(jnp.bfloat16), 'col', scatter_dimension...  72.6 us
    unnamed x9, waiting for transfers between devices  66.8 us
    sub x8, matrix products, row_backward(): exponent = jnp.exp(scores - row_top)  61.3 us
  transfers between devices with their start and end apart: 8, of which 8 were waited for; matrix products, arithmetic and copies ran while one was open for 11% of the time, Pallas kernels for 0%

commit v1 on v0

v1 whole, which is shorter than its diff:
```python
import functools
import math

import jax
import jax.numpy as jnp
from jax import lax
from jax.experimental import pallas as pl
from jax.experimental.pallas import tpu as pltpu
from jax.sharding import PartitionSpec as P

F32 = jnp.float32
BF = jnp.bfloat16
NT = (((1,), (1,)), ((), ()))
NN = (((1,), (0,)), ((), ()))
LOG2E = 1.4426950408889634
VMEM_LIMIT = 60 * 1024 * 1024
big_penalty = 1000000000.0


def dot(a, b, dims=NN):
    return lax.dot_general(a, b, dims, preferred_element_type=F32)


def attention_kernel(h0, total_heads, first, last, tile, order_ref, *refs):
    q_ref, kv_ref, g_ref, do_ref, pc_ref, w_ref = refs[:6]
    bias_refs = refs[6:10]
    refs = refs[10:]
    head_start = h0 == 0
    if not first:
        acc_in, refs = refs[0], refs[1:]
    if head_start:
        gq_ref, gg_ref, dkt_out, dvt_out, acc_out = refs[:5]
        refs = refs[5:]
    else:
        gq_in, gg_in, dkt_in, dvt_in = refs[:4]
        gq_ref, gg_ref, dkv_ref, car_ref, acc_out = refs[4:9]
        refs = refs[9:]
    bias_s, s_s, e_s, qt_s, dot_s, dkt_s, dvt_s, gq_s, acc_s = refs
    h = pl.program_id(0)
    i = pl.program_id(1)
    ni, cj, chan = q_ref.shape
    heads = pl.num_programs(0)
    head = chan // total_heads
    n = bias_s.shape[1]
    kb = n // 8
    scale = 1.0 / math.sqrt(head)
    hh = h + h0

    @pl.when(i == 0)
    def _():
        for s in range(8):
            off = pl.multiple_of(order_ref[s] * kb, 128)
            bias_s[:, pl.ds(off, kb)] = bias_refs[s // 2][s % 2, 0].astype(F32) * math.sqrt(head)
        if first:
            acc_s[...] = jnp.zeros(acc_s.shape, F32)
        else:
            acc_s[...] = acc_in[0]

    lane = lax.broadcasted_iota(jnp.int32, (cj, chan), 1)
    mask = (lane >= hh * head) & (lane < (hh + 1) * head)
    q = q_ref[i]
    qh = jnp.where(mask, q, jnp.zeros_like(q))

    @pl.when(h == 0)
    def _():
        qt_s[i] = q.astype(F32).T.astype(BF)
        if head_start:
            gq_s[i] = jnp.zeros((cj, chan), F32)
            gg_ref[i] = jnp.zeros((cj, chan), BF)
        else:
            gq_s[i] = gq_in[i].astype(F32)
            gg_ref[i] = gg_in[i]

    def rows(base, t):
        lo = t * tile
        out = []
        while lo < (t + 1) * tile:
            b, r = lo // cj, lo % cj
            m = min(cj - r, (t + 1) * tile - lo)
            out.append(kv_ref[b, base + i, r : r + m, :])
            lo += m
        return out[0] if len(out) == 1 else jnp.concatenate(out, axis=0)

    def k_rows(t):
        return rows(0, t)

    def v_rows(t):
        return rows(ni, t)

    tiles = n // tile
    m = None
    for t in range(tiles):
        sl = slice(t * tile, (t + 1) * tile)
        s = dot(qh, k_rows(t), NT) + bias_s[:, sl]
        s_s[:, sl] = s
        for u in range(tile // 128):
            p = s[:, u * 128 : (u + 1) * 128]
            m = p if m is None else jnp.maximum(m, p)
    top = jnp.max(m, axis=1, keepdims=True)
    lsum = None
    att = None
    for t in range(tiles):
        sl = slice(t * tile, (t + 1) * tile)
        e = jnp.exp2((s_s[:, sl] - top) * (scale * LOG2E))
        for u in range(tile // 128):
            p = e[:, u * 128 : (u + 1) * 128]
            lsum = p if lsum is None else lsum + p
        eb = e.astype(BF)
        e_s[:, sl] = eb
        a = dot(eb, v_rows(t))
        att = a if att is None else att + a
    linv = 1.0 / jnp.sum(lsum, axis=1, keepdims=True)
    att = att * linv
    gate = jax.nn.sigmoid(g_ref[i].astype(F32))
    cot = do_ref[i].astype(F32)
    gg = (cot * att * gate * (1.0 - gate)).astype(BF)
    gg_ref[i] = jnp.where(mask, gg, gg_ref[i])
    d_out = (cot * gate).astype(BF).astype(F32)
    d_out = jnp.where(mask, d_out, 0.0)
    delta = jnp.sum(d_out * att, axis=1, keepdims=True) * linv
    d_out = d_out * linv
    dob = d_out.astype(BF)
    dot_s[...] = d_out.T.astype(BF)
    hs = pl.ds(pl.multiple_of(hh * head, head), head)
    do_t = dot_s[hs, :]
    q_t = qt_s[i, hs, :]
    ls = pl.ds(pl.multiple_of(h * head, head), head)
    dq = None
    for t in range(tiles):
        sl = slice(t * tile, (t + 1) * tile)
        dp = dot(dob, v_rows(t), NT) - delta
        eb = e_s[:, sl]
        ds = eb.astype(F32) * dp
        acc_s[:, sl] += ds
        dsb = ds.astype(BF)
        a = dot(dsb, k_rows(t))
        dq = a if dq is None else dq + a
        dkt_s[i, ls, sl] = dot(q_t, dsb) * scale
        dvt_s[i, ls, sl] = dot(do_t, eb)
    gq_s[i] = jnp.where(mask, dq * scale, gq_s[i])

    @pl.when(h == heads - 1)
    def _():
        gq = gq_s[i].astype(BF)
        gq_ref[i] = gq
        if head_start:
            dkt_out[i] = dkt_s[i].astype(BF)
            dvt_out[i] = dvt_s[i].astype(BF)
        else:
            car = pc_ref[i].astype(F32) + dot(gq, w_ref[...], NT)
            car_ref[i] = car.T.astype(BF)
            for b in range(n // 384):
                sl = slice(b * 384, (b + 1) * 384)
                for base, old, new in ((0, dkt_in, dkt_s), (ni, dvt_in, dvt_s)):
                    both = jnp.concatenate([old[i, :, sl].astype(F32), new[i, :, sl]], axis=0).T.astype(BF)
                    for c in range(384 // cj):
                        dkv_ref[(384 // cj) * b + c, base + i] = both[c * cj : (c + 1) * cj]

    @pl.when(i == pl.num_programs(1) - 1)
    def _():
        if last:
            for s in range(8):
                off = pl.multiple_of(order_ref[s] * kb, 128)
                acc_out[s, 0] = acc_s[:, pl.ds(off, kb)].astype(BF)
        else:
            acc_out[0] = acc_s[...]


def attention(order, q, kv, g, do, pc, w, biases, acc, earlier, h0, heads, total_heads, last, tile=512):
    ni, cj, chan = q.shape
    nb = kv.shape[0]
    n = nb * cj
    kb = n // 8
    part = heads * (chan // total_heads)
    first = acc is None
    sd = jax.ShapeDtypeStruct

    def whole(*shape):
        return pl.BlockSpec(shape, lambda h, i, r: (0,) * len(shape), pipeline_mode=pl.Buffered(1))

    per_row = whole(ni, cj, chan)
    in_specs = [per_row, whole(nb, 2 * ni, cj, chan), per_row, per_row, per_row, whole(chan, chan)]
    in_specs += [pl.BlockSpec((2, 1, cj, kb), lambda h, i, r: (0, h, 0, 0))] * 4
    ops = [q, kv, g, do, pc, w, *biases]
    if not first:
        in_specs.append(pl.BlockSpec((1, cj, n), lambda h, i, r: (h, 0, 0)))
        ops.append(acc)
    out_specs = [per_row, per_row]
    out_shape = [sd((ni, cj, chan), BF), sd((ni, cj, chan), BF)]
    if h0 == 0:
        out_specs += [whole(ni, part, n), whole(ni, part, n)]
        out_shape += [sd((ni, part, n), BF), sd((ni, part, n), BF)]
    else:
        in_specs += [per_row, per_row, whole(ni, chan - part, n), whole(ni, chan - part, n)]
        ops += earlier
        out_specs += [whole(nb, 2 * ni, cj, chan), whole(ni, chan, cj)]
        out_shape += [sd((nb, 2 * ni, cj, chan), BF), sd((ni, chan, cj), BF)]
    if last:
        out_specs.append(pl.BlockSpec((8, 1, cj, kb), lambda h, i, r: (0, h, 0, 0)))
        out_shape.append(sd((8, heads, cj, kb), BF))
    else:
        out_specs.append(pl.BlockSpec((1, cj, n), lambda h, i, r: (h, 0, 0)))
        out_shape.append(sd((heads, cj, n), F32))
    scratch = [
        pltpu.VMEM((cj, n), F32),
        pltpu.VMEM((cj, n), F32),
        pltpu.VMEM((cj, n), BF),
        pltpu.VMEM((ni, chan, cj), BF),
        pltpu.VMEM((chan, cj), BF),
        pltpu.VMEM((ni, part, n), F32),
        pltpu.VMEM((ni, part, n), F32),
        pltpu.VMEM((ni, cj, chan), F32),
        pltpu.VMEM((cj, n), F32),
    ]
    return pl.pallas_call(
        functools.partial(attention_kernel, h0, total_heads, first, last, tile),
        grid_spec=pltpu.PrefetchScalarGridSpec(
            num_scalar_prefetch=1, grid=(heads, ni), in_specs=in_specs, out_specs=out_specs, scratch_shapes=scratch
        ),
        out_shape=out_shape,
        compiler_params=pltpu.CompilerParams(
            dimension_semantics=("arbitrary", "arbitrary"), vmem_limit_bytes=VMEM_LIMIT
        ),
        cost_estimate=pl.CostEstimate(
            flops=16 * heads * ni * cj * n * chan, bytes_accessed=30_000_000, transcendentals=heads * ni * cj * n
        ),
        name="attention_rows",
    )(order, *ops)


def left_kernel(order_ref, *refs):
    car = refs[:4]
    r_ref, out_ref, l_s, o_s = refs[4:]
    step = pl.program_id(0)
    _, ni, chan, cj = car[0].shape
    cb, _, kk = r_ref.shape
    rows = 8 * ni
    half = ni // 2

    @pl.when(step == 0)
    def _():
        for s in range(8):
            for i in range(ni):
                base = (s * ni + i) * chan
                x = car[s // 2][s % 2, i].astype(F32)
                l_s[0, base : base + chan, :] = x[:, :128]
                l_s[1, base : base + chan, : cj - 128] = x[:, 128:]

    for u in range(cb):
        c = step * cb + u
        a = l_s[0, pl.ds(c, rows, stride=chan), :]
        b = l_s[1, pl.ds(c, rows, stride=chan), :][:, : cj - 128]
        res = dot(jnp.concatenate([a, b], axis=1).astype(BF), r_ref[u])
        for b in range(kk // 128):
            o_s[b, pl.ds(c, rows, stride=chan), :] = res[:, b * 128 : (b + 1) * 128]

    @pl.when(step == pl.num_programs(0) - 1)
    def _():
        for s in range(8):
            for i in range(ni):
                base = (s * ni + i) * chan
                for b in range(kk // 128):
                    out_ref[2 * order_ref[s] + i // half, i % half, b * 128 : (b + 1) * 128, :] = o_s[
                        b, base : base + chan, :
                    ].T.astype(BF)


def left_product(order, cars, right_t, cb=16):
    _, ni, chan, cj = cars[0].shape
    kk = right_t.shape[2]

    def whole(*shape):
        return pl.BlockSpec(shape, lambda t, r: (0,) * len(shape), pipeline_mode=pl.Buffered(1))

    return pl.pallas_call(
        left_kernel,
        grid_spec=pltpu.PrefetchScalarGridSpec(
            num_scalar_prefetch=1,
            grid=(chan // cb,),
            in_specs=[whole(2, ni, chan, cj)] * 4 + [pl.BlockSpec((cb, cj, kk), lambda t, r: (t, 0, 0))],
            out_specs=whole(16, ni // 2, kk, chan),
            scratch_shapes=[
                pltpu.VMEM((2, 8 * ni * chan, 128), F32),
                pltpu.VMEM((kk // 128, 8 * ni * chan, 128), F32),
            ],
        ),
        out_shape=jax.ShapeDtypeStruct((16, ni // 2, kk, chan), BF),
        compiler_params=pltpu.CompilerParams(dimension_semantics=("arbitrary",), vmem_limit_bytes=VMEM_LIMIT),
        cost_estimate=pl.CostEstimate(
            flops=40_000_000_000, bytes_accessed=30_000_000, transcendentals=0
        ),
        name="left_product",
    )(order, *cars, right_t)


def row_shift(x, dy):
    return lax.ppermute(x, "row", [(2 * y + z, 2 * ((y + dy) % 4) + z) for y in range(4) for z in range(2)])


def row_swap(x):
    return lax.ppermute(x, "row", [(r, r ^ 1) for r in range(8)])


def row_pair(x):
    return jnp.stack([x, row_swap(x)])


def row_gather(pair):
    return [pair] + [row_shift(pair, dy) for dy in (1, 2, 3)]


def row_scatter_sum(x):
    total = x[0:2].astype(F32)
    for dy in (1, 2, 3):
        total = total + row_shift(x[2 * dy : 2 * dy + 2], -dy).astype(F32)
    total = total.astype(BF)
    return total[0].astype(F32) + row_swap(total[1]).astype(F32)


def local(
    queries,
    keys,
    values,
    gate_logits,
    out_grad,
    pair_bias,
    residue_mask,
    query_weight,
    pair_cotangent,
    right_proj,
):
    total_heads = pair_bias.shape[0]
    kb = pair_bias.shape[2]
    rb = queries.shape[0]
    row = lax.axis_index("row")
    y, z = row // 2, row % 2
    order = jnp.stack([2 * ((y - s // 2 + 4) % 4) + (z ^ (s % 2)) for s in range(8)]).astype(jnp.int32)
    penalty = big_penalty * (lax.dynamic_slice_in_dim(residue_mask, row * kb, kb).astype(F32) - 1.0)
    bias = (pair_bias.astype(F32) + penalty[None, None, :]).astype(BF)
    hs = total_heads // 2
    pairs = row_pair(bias)
    biases = [row_gather(pairs[:, :hs]), row_gather(pairs[:, hs:])]
    right_t = jnp.transpose(right_proj, (2, 0, 1))

    quarter = rb // 4
    picks = [
        tuple(range(0, quarter)) + tuple(range(2 * quarter, 3 * quarter)),
        tuple(range(quarter, 2 * quarter)) + tuple(range(3 * quarter, rb)),
    ]

    def take(x, ids):
        return jnp.concatenate([x[ids[0] : ids[quarter - 1] + 1], x[ids[quarter] : ids[-1] + 1]])

    gathered = [
        lax.all_gather(jnp.concatenate([take(keys, ids), take(values, ids)]), "col", axis=0) for ids in picks
    ]
    accs = [None, None]
    outs = []
    for part, ids in enumerate(picks):
        rows = [take(a, ids) for a in (queries, gate_logits, out_grad, pair_cotangent)]
        earlier = None
        for half in range(2):
            res = attention(
                order, rows[0], gathered[part], rows[1], rows[2], rows[3], query_weight, biases[half],
                accs[half], earlier, half * hs, hs, total_heads, part == 1,
            )
            earlier = list(res[:4])
            accs[half] = res[4]
        gq, gg, dkv, car = res[:4]
        dkv_sum = lax.psum_scatter(dkv, "col", scatter_dimension=0)
        left = left_product(order, row_gather(row_pair(car)), right_t)
        left_sum = lax.psum_scatter(left, "col", scatter_dimension=0)
        outs.append((gq, gg, dkv_sum[: rb // 2], dkv_sum[rb // 2 :], left_sum))

    def untake(a, b):
        return jnp.concatenate([a[:quarter], b[:quarter], a[quarter:], b[quarter:]])

    gq, gg, dk, dv = [untake(a, b) for a, b in zip(outs[0][:4], outs[1][:4])]
    left = jnp.concatenate([outs[0][4], outs[1][4]])
    grad_bias = jnp.concatenate([row_scatter_sum(a) for a in accs])
    return (gq, dk, dv, gg, grad_bias, left)


def solution(mesh):
    in_specs = (
        P("row", "col", None),
        P("row", "col", None),
        P("row", "col", None),
        P("row", "col", None),
        P("row", "col", None),
        P(None, "col", "row"),
        P(),
        P(),
        P("row", "col", None),
        P("col", "row", None),
    )
    out_specs = (
        P("row", "col", None),
        P("row", "col", None),
        P("row", "col", None),
        P("row", "col", None),
        P(None, "col", "row"),
        P("col", "row", None),
    )
    return jax.shard_map(local, mesh=mesh, in_specs=in_specs, out_specs=out_specs, check_vma=False)
```

time: 989 us -> 556 us (0.56)
  matrix products: 241 us -> 0 us
  waiting for transfers between devices: 479 us -> 276 us
  Pallas kernels: 0 us -> 173 us
  local copies, waits for them, and re-layouts: 171 us -> 34.6 us
  other arithmetic: 76.2 us -> 14.8 us
  starting transfers between devices: 0.5 us -> 38.3 us
    dot_general x42 -> x0, matrix products: 179 us -> none  [the longest x8 83.3 us: row_backward(): jnp.einsum('jhd,khd->hjk', d_out, v_heads, preferred_element_type=jnp.flo...]
    all_gather x4 -> x2, waiting for transfers between devices: 178 us -> 0.01 us  [local(): lax.all_gather(jnp.concatenate([take(keys, ids), take(values, ids)]), 'co...]
    pallas_call x0 -> x6, Pallas kernels: none -> 173 us  [the longest x4 140 us: attention(): pl.pallas_call(functools.partial(attention_kernel, h0, total_heads, first...]
    ppermute x0 -> x23, waiting for transfers between devices: none -> 125 us  [the longest x18 88.7 us: row_shift(): lax.ppermute(x, 'row', [(2 * y + z, 2 * ((y + dy) % 4) + z) for y in rang...]
    reduce_scatter x3 -> x4, waiting for transfers between devices: 234 us -> 150 us  [the longest x2 150 us: local(): dkv_sum = lax.psum_scatter(dkv, 'col', scatter_dimension=0)]
    convert_element_type x11 -> x3, other arithmetic: 67.9 us -> 0.74 us  [the longest x2 0.63 us: row_scatter_sum(): total = total.astype(BF)]
    unnamed x9 -> x6, waiting for transfers between devices: 66.8 us -> 1.11 us
    sub x8 -> x0, matrix products: 61.3 us -> none  [row_backward(): exponent = jnp.exp(scores - row_top)]
  transfers between devices with their start and end apart: 8 -> 29, of which waited for: 8 -> 14; matrix products, arithmetic and copies ran while one was open for 11% -> 7% of each run, Pallas kernels for 0% -> 31%
where the time goes in v1:
time: 556 us; the launch traced here: 551 us
  waiting for transfers between devices  276 us (50%)
  Pallas kernels  173 us (31%)
  starting transfers between devices  38.3 us (7%)
  local copies, waits for them, and re-layouts  34.6 us (6%)
  other arithmetic  14.8 us (3%)
  between operations  14.5 us (3%)
    reduce_scatter x2, waiting for transfers between devices, local(): dkv_sum = lax.psum_scatter(dkv, 'col', scatter_dimension=0)  150 us
    pallas_call x4, Pallas kernels, attention(): pl.pallas_call(functools.partial(attention_kernel, h0, total_heads, first...  140 us
    ppermute x18, waiting for transfers between devices, row_shift(): lax.ppermute(x, 'row', [(2 * y + z, 2 * ((y + dy) % 4) + z) for y in rang...  88.7 us
    ppermute x5, waiting for transfers between devices, row_swap(): return lax.ppermute(x, 'row', [(r, r ^ 1) for r in range(8)])  35.9 us
    pallas_call x2, Pallas kernels, left_product(): pl.pallas_call(left_kernel, grid_spec=pltpu.PrefetchScalarGridSpec(num_sc...  33.6 us
    unnamed x49, local copies, waits for them, and re-layouts  29.9 us
    ppermute x18, starting transfers between devices, row_shift(): lax.ppermute(x, 'row', [(2 * y + z, 2 * ((y + dy) % 4) + z) for y in rang...  21.5 us
    ppermute x5, starting transfers between devices, row_swap(): return lax.ppermute(x, 'row', [(r, r ^ 1) for r in range(8)])  16.5 us
  transfers between devices with their start and end apart: 29, of which 14 were waited for; matrix products, arithmetic and copies ran while one was open for 7% of the time, Pallas kernels for 31%

profile of v1, /device:TPU:0, one launch (start us, length us, event | category | flops | bytes accessed | tf_op | source)
XLA Modules:
  0.0 551.4 jit_solution(5028958326708527958)
XLA Ops:
  11.2 4.0 collective-permute-start
  16.9 18.1 %collective-permute-done = bf16[4,192,384]{2,1,0:T(8,128)(2,1)S(1)} collective-permute-done((bf16[4,192,384]{2,1,0:T(8,128)(2,1)S(1)}, bf16[4,192,384]{2,1,0:T(8,128)(2,1)S(1)}, u32[]{:S(2)}, u32[]{:S(2)}) %collective-permute-start) | collective-permute-done | bytes 589856 | tf_op jit(solution)/shard_map/ppermute | solution.py:301
  44.7 20.0 %collective-permute-done.6.refs_9_ = bf16[2,2,192,384]{3,2,1,0:T(8,128)(2,1)S(1)} collective-permute-done((bf16[2,2,192,384]{3,2,1,0:T(8,128)(2,1)S(1)}, bf16[2,2,192,384]{3,2,1,0:T(8,128)(2,1)S(1)}, u32[]{:S(2)}, u32[]{:S(2)}) %collective-permute-start.6) | collective-permute-done | bytes 589856 | tf_op jit(solution)/shard_map/ppermute | solution.py:297
  65.6 3.3 collective-permute-done.4.refs_7_
  68.9 32.9 %attention_rows.4 = (bf16[4,192,128]{2,1,0:T(8,128)(2,1)}, bf16[4,192,128]{2,1,0:T(8,128)(2,1)}, bf16[4,64,3072]{2,1,0:T(8,128)(2,1)}, bf16[4,64,3072]{2,1,0:T(8,128)(2,1)}, f32[2,192,3072]{2,1,0:T(8,128)}) custom-call(s32[8]{0:T(128)} %stack.62.order_ref, bf16[4,192,128]{2,1,0:T(8,128)(2,1)} %get-tuple-element.98.refs_0_, ...), custom_call_target="tpu_custom_call" | custom-call | flops 9663676416 | bytes 30000000 | tf_op jit(solution)/shard_map/attention_rows/pallas_call | solution.py:215
  102.7 36.7 %attention_rows.5 = (bf16[4,192,128]{2,1,0:T(8,128)(2,1)}, bf16[4,192,128]{2,1,0:T(8,128)(2,1)}, bf16[16,8,192,128]{3,2,1,0:T(8,128)(2,1)}, bf16[4,128,192]{2,1,0:T(8,128)(2,1)}, f32[2,192,3072]{2,1,0:T(8,128)}) custom-call(s32[8]{0:T(128)} %stack.62.order_ref, bf16[4,192,128]{2,1,0:T(8,128)(2,1)} %get-tuple-element.98.refs_0_, ...), custom_call_target="tpu_custom_call" | custom-call | flops 9663676416 | bytes 30000000 | tf_op jit(solution)/shard_map/attention_rows/pallas_call | solution.py:215
  139.3 4.0 collective-permute-start.15
  143.4 6.1 %collective-permute-done.15 = bf16[4,128,192]{2,1,0:T(8,128)(2,1)S(1)} collective-permute-done((bf16[4,128,192]{2,1,0:T(8,128)(2,1)}, bf16[4,128,192]{2,1,0:T(8,128)(2,1)S(1)}, u32[]{:S(2)}, u32[]{:S(2)}) %collective-permute-start.15) | collective-permute-done | bytes 196640 | tf_op jit(solution)/shard_map/ppermute | solution.py:301
  152.7 24.4 %copy.17 = bf16[192,384,128]{1,0,2:T(8,128)(2,1)} copy(bf16[192,384,128]{2,1,0:T(8,128)(2,1)} %param.19) | data formatting | bytes 37748736 | tf_op args[9]
  179.0 16.8 %left_product.2 = bf16[16,2,384,128]{3,2,1,0:T(8,128)(2,1)} custom-call(s32[8]{0:T(128)} %stack.62.order_ref, bf16[2,4,128,192]{3,2,1,0:T(8,128)(2,1)} %copy-done.5, bf16[2,4,128,192]{3,2,1,0:T(8,128)(2,1)} %copy-done.20, bf16[2,4,128,192]{3,2,1,0:T(8,128)(2,1)} %copy-done.19, bf16[2,4,128,192]{3,2,1,0:T(8,128)(2,1)} %copy-done.18, ...), custom_call_target="tpu_custom_call" | custom-call | flops 40000000000 | bytes 30000000 | tf_op jit(solution)/shard_map/left_product/pallas_call | solution.py:275
  196.7 32.9 %attention_rows.6 = (bf16[4,192,128]{2,1,0:T(8,128)(2,1)}, bf16[4,192,128]{2,1,0:T(8,128)(2,1)}, bf16[4,64,3072]{2,1,0:T(8,128)(2,1)}, bf16[4,64,3072]{2,1,0:T(8,128)(2,1)}, bf16[8,2,192,384]{3,2,1,0:T(8,128)(2,1)}) custom-call(s32[8]{0:T(128)} %stack.62.order_ref, bf16[4,192,128]{2,1,0:T(8,128)(2,1)} %get-tuple-element.102.refs_0_, ...), custom_call_target="tpu_custom_call" | custom-call | flops 9663676416 | bytes 30000000 | tf_op jit(solution)/shard_map/attention_rows/pallas_call | solution.py:215
  229.6 37.0 %attention_rows.7 = (bf16[4,192,128]{2,1,0:T(8,128)(2,1)}, bf16[4,192,128]{2,1,0:T(8,128)(2,1)}, bf16[16,8,192,128]{3,2,1,0:T(8,128)(2,1)}, bf16[4,128,192]{2,1,0:T(8,128)(2,1)}, bf16[8,2,192,384]{3,2,1,0:T(8,128)(2,1)}) custom-call(s32[8]{0:T(128)} %stack.62.order_ref, bf16[4,192,128]{2,1,0:T(8,128)(2,1)} %get-tuple-element.102.refs_0_, ...), custom_call_target="tpu_custom_call" | custom-call | flops 9663676416 | bytes 30000000 | tf_op jit(solution)/shard_map/attention_rows/pallas_call | solution.py:215
  266.7 3.3 collective-permute-start.19
  270.0 5.0 collective-permute-done.19
  281.6 17.3 %collective-permute-done.22.refs_3_ = bf16[2,4,128,192]{3,2,1,0:T(8,128)(2,1)S(1)} collective-permute-done((bf16[2,4,128,192]{3,2,1,0:T(8,128)(2,1)S(1)}, bf16[2,4,128,192]{3,2,1,0:T(8,128)(2,1)S(1)}, u32[]{:S(2)}, u32[]{:S(2)}) %collective-permute-start.22) | collective-permute-done | bytes 393248 | tf_op jit(solution)/shard_map/ppermute | solution.py:297
  298.9 3.7 collective-permute-done.20.refs_1_
  303.4 16.8 %left_product.3 = bf16[16,2,384,128]{3,2,1,0:T(8,128)(2,1)} custom-call(s32[8]{0:T(128)} %stack.62.order_ref, bf16[2,4,128,192]{3,2,1,0:T(8,128)(2,1)} %copy-done.6, bf16[2,4,128,192]{3,2,1,0:T(8,128)(2,1)} %copy-done.23, bf16[2,4,128,192]{3,2,1,0:T(8,128)(2,1)} %copy-done.22, bf16[2,4,128,192]{3,2,1,0:T(8,128)(2,1)} %copy-done.21, ...), custom_call_target="tpu_custom_call" | custom-call | flops 40000000000 | bytes 30000000 | tf_op jit(solution)/shard_map/left_product/pallas_call | solution.py:275
  329.0 20.2 %collective-permute-done.11 = bf16[2,2,192,384]{3,2,1,0:T(8,128)(2,1)S(1)} collective-permute-done((bf16[2,2,192,384]{3,2,1,0:T(8,128)(2,1)S(1)}, bf16[2,2,192,384]{3,2,1,0:T(8,128)(2,1)S(1)}, u32[]{:S(2)}, u32[]{:S(2)}) %collective-permute-start.11) | collective-permute-done | bytes 589856 | tf_op jit(solution)/shard_map/ppermute | solution.py:297
  349.9 3.9 collective-permute-done.13
  356.7 7.5 %collective-permute-done.7 = bf16[2,2,192,384]{3,2,1,0:T(8,128)(2,1)S(1)} collective-permute-done((bf16[2,2,192,384]{3,2,1,0:T(8,128)(2,1)S(1)}, bf16[2,2,192,384]{3,2,1,0:T(8,128)(2,1)S(1)}, u32[]{:S(2)}, u32[]{:S(2)}) %collective-permute-start.7) | collective-permute-done | bytes 589856 | tf_op jit(solution)/shard_map/ppermute | solution.py:297
  364.2 12.9 %collective-permute-done.9 = bf16[2,2,192,384]{3,2,1,0:T(8,128)(2,1)S(1)} collective-permute-done((bf16[2,2,192,384]{3,2,1,0:T(8,128)(2,1)S(1)}, bf16[2,2,192,384]{3,2,1,0:T(8,128)(2,1)S(1)}, u32[]{:S(2)}, u32[]{:S(2)}) %collective-permute-start.9) | collective-permute-done | bytes 589856 | tf_op jit(solution)/shard_map/ppermute | solution.py:297
  381.0 6.6 %collective-permute-done.10 = bf16[2,192,384]{2,1,0:T(8,128)(2,1)S(1)} collective-permute-done((bf16[2,192,384]{2,1,0:T(8,128)(2,1)S(1)}, bf16[2,192,384]{2,1,0:T(8,128)(2,1)S(1)}, u32[]{:S(2)}, u32[]{:S(2)}) %collective-permute-start.10) | collective-permute-done | bytes 294944 | tf_op jit(solution)/shard_map/ppermute | solution.py:301
  390.6 71.6 %reduce-scatter.7.cloned.1.call-done = bf16[1,8,192,128]{3,2,1,0:T(8,128)(2,1)} async-done(((bf16[16,8,192,128]{3,2,1,0:T(8,128)(2,1)}), bf16[1,8,192,128]{3,2,1,0:T(8,128)(2,1)}) %reduce-scatter.7.cloned.1.call-update) | async-done | bytes 393232 | tf_op jit(solution)/shard_map/reduce_scatter | solution.py:370
  463.2 78.7 %reduce-scatter.5.cloned.1.call-done = bf16[1,8,192,128]{3,2,1,0:T(8,128)(2,1)} async-done(((bf16[16,8,192,128]{3,2,1,0:T(8,128)(2,1)}), bf16[1,8,192,128]{3,2,1,0:T(8,128)(2,1)}) %reduce-scatter.5.cloned.1.call-update) | async-done | bytes 393232 | tf_op jit(solution)/shard_map/reduce_scatter | solution.py:370
  (133 shorter events, 53.1 us)
Async XLA Ops:
  7.2 61.7 %all-gather.5.cloned.1.call-start = ((), (), s32[]{:S(2)}) async-start(), calls=%async_computation.8 | async-start | bytes 6684672 | tf_op jit(solution)/shard_map/all_gather | solution.py:355
  9.3 187.3 %all-gather.7.cloned.1.call-start = ((), (), s32[]{:S(2)}) async-start(), calls=%async_computation.9 | async-start | bytes 6684672 | tf_op jit(solution)/shard_map/all_gather | solution.py:355
  10.2 378.5 %reduce-scatter.9.cloned.1.call-start = ((), (), s32[]{:S(2)}) async-start(), calls=%async_computation.6 | async-start | bytes 3342336 | tf_op jit(solution)/shard_map/reduce_scatter | solution.py:372
  11.2 23.8 %collective-permute-start = (bf16[4,192,384]{2,1,0:T(8,128)(2,1)S(1)}, bf16[4,192,384]{2,1,0:T(8,128)(2,1)S(1)}, u32[]{:S(2)}, u32[]{:S(2)}) collective-permute-start(bf16[4,192,384]{2,1,0:T(8,128)(2,1)S(1)} %add_convert_fusion.2), channel_id=1, source_target_pairs={{0,16},{16,0},{32,48},{48,32},{64,80},{80,64},{96,112},{112,96},{1... | collective-permute-start | bytes 1769480 | tf_op jit(solution)/shard_map/ppermute | solution.py:301
  35.2 29.5 %collective-permute-start.6 = (bf16[2,2,192,384]{3,2,1,0:T(8,128)(2,1)S(1)}, bf16[2,2,192,384]{3,2,1,0:T(8,128)(2,1)S(1)}, u32[]{:S(2)}, u32[]{:S(2)}) collective-permute-start(bf16[2,2,192,384]{3,2,1,0:T(8,128)(2,1)S(1)} %get-tuple-element.52.refs_6_), channel_id=1, source_target_pairs={{0,96},{16,112},{32,0},{48,16},{64,32},{80,48},{96,64},{112,80},{1... | collective-permute-start | bytes 1769480 | tf_op jit(solution)/shard_map/ppermute | solution.py:297
  38.3 26.4 %collective-permute-start.5 = (bf16[2,2,192,384]{3,2,1,0:T(8,128)(2,1)S(1)}, bf16[2,2,192,384]{3,2,1,0:T(8,128)(2,1)S(1)}, u32[]{:S(2)}, u32[]{:S(2)}) collective-permute-start(bf16[2,2,192,384]{3,2,1,0:T(8,128)(2,1)S(1)} %get-tuple-element.52.refs_6_), channel_id=1, source_target_pairs={{0,64},{16,80},{32,96},{48,112},{64,0},{80,16},{96,32},{112,48},{1... | collective-permute-start | bytes 1769480 | tf_op jit(solution)/shard_map/ppermute | solution.py:297
  38.8 30.1 %collective-permute-start.4 = (bf16[2,2,192,384]{3,2,1,0:T(8,128)(2,1)S(1)}, bf16[2,2,192,384]{3,2,1,0:T(8,128)(2,1)}, u32[]{:S(2)}, u32[]{:S(2)}) collective-permute-start(bf16[2,2,192,384]{3,2,1,0:T(8,128)(2,1)S(1)} %get-tuple-element.52.refs_6_), channel_id=1, source_target_pairs={{0,32},{16,48},{32,64},{48,80},{64,96},{80,112},{96,0},{112,16},{1... | collective-permute-start | bytes 1769480 | tf_op jit(solution)/shard_map/ppermute | solution.py:297
  40.8 61.1 %collective-permute-start.3 = (bf16[2,2,192,384]{3,2,1,0:T(8,128)(2,1)S(1)}, bf16[2,2,192,384]{3,2,1,0:T(8,128)(2,1)S(1)}, u32[]{:S(2)}, u32[]{:S(2)}) collective-permute-start(bf16[2,2,192,384]{3,2,1,0:T(8,128)(2,1)S(1)} %get-tuple-element.53.refs_6_), channel_id=1, source_target_pairs={{0,96},{16,112},{32,0},{48,16},{64,32},{80,48},{96,64},{112,80},{1... | collective-permute-start | bytes 1769480 | tf_op jit(solution)/shard_map/ppermute | solution.py:297
  42.9 59.0 %collective-permute-start.2 = (bf16[2,2,192,384]{3,2,1,0:T(8,128)(2,1)S(1)}, bf16[2,2,192,384]{3,2,1,0:T(8,128)(2,1)}, u32[]{:S(2)}, u32[]{:S(2)}) collective-permute-start(bf16[2,2,192,384]{3,2,1,0:T(8,128)(2,1)S(1)} %get-tuple-element.53.refs_6_), channel_id=1, source_target_pairs={{0,64},{16,80},{32,96},{48,112},{64,0},{80,16},{96,32},{112,48},{1... | collective-permute-start | bytes 1769480 | tf_op jit(solution)/shard_map/ppermute | solution.py:297
  64.8 37.1 %collective-permute-start.1 = (bf16[2,2,192,384]{3,2,1,0:T(8,128)(2,1)S(1)}, bf16[2,2,192,384]{3,2,1,0:T(8,128)(2,1)}, u32[]{:S(2)}, u32[]{:S(2)}) collective-permute-start(bf16[2,2,192,384]{3,2,1,0:T(8,128)(2,1)S(1)} %get-tuple-element.53.refs_6_), channel_id=1, source_target_pairs={{0,32},{16,48},{32,64},{48,80},{64,96},{80,112},{96,0},{112,16},{1... | collective-permute-start | bytes 1769480 | tf_op jit(solution)/shard_map/ppermute | solution.py:297
  150.6 27.3 %collective-permute-start.18 = (bf16[2,4,128,192]{3,2,1,0:T(8,128)(2,1)S(1)}, bf16[2,4,128,192]{3,2,1,0:T(8,128)(2,1)S(1)}, u32[]{:S(2)}, u32[]{:S(2)}) collective-permute-start(bf16[2,4,128,192]{3,2,1,0:T(8,128)(2,1)S(1)} %pad_maximum_fusion.2.refs_0_), channel_id=1, source_target_pairs={{0,96},{16,112},{32,0},{48,16},{64,32},{80,48},{96,64},{112,80},{1... | collective-permute-start | bytes 1179656 | tf_op jit(solution)/shard_map/ppermute | solution.py:297
  150.6 27.2 %collective-permute-start.17 = (bf16[2,4,128,192]{3,2,1,0:T(8,128)(2,1)S(1)}, bf16[2,4,128,192]{3,2,1,0:T(8,128)(2,1)S(1)}, u32[]{:S(2)}, u32[]{:S(2)}) collective-permute-start(bf16[2,4,128,192]{3,2,1,0:T(8,128)(2,1)S(1)} %pad_maximum_fusion.2.refs_0_), channel_id=1, source_target_pairs={{0,64},{16,80},{32,96},{48,112},{64,0},{80,16},{96,32},{112,48},{1... | collective-permute-start | bytes 1179656 | tf_op jit(solution)/shard_map/ppermute | solution.py:297
  151.3 26.6 %collective-permute-start.16 = (bf16[2,4,128,192]{3,2,1,0:T(8,128)(2,1)S(1)}, bf16[2,4,128,192]{3,2,1,0:T(8,128)(2,1)S(1)}, u32[]{:S(2)}, u32[]{:S(2)}) collective-permute-start(bf16[2,4,128,192]{3,2,1,0:T(8,128)(2,1)S(1)} %pad_maximum_fusion.2.refs_0_), channel_id=1, source_target_pairs={{0,32},{16,48},{32,64},{48,80},{64,96},{80,112},{96,0},{112,16},{1... | collective-permute-start | bytes 1179656 | tf_op jit(solution)/shard_map/ppermute | solution.py:297
  195.8 192.9 %reduce-scatter.11.cloned.1.call-start = ((), (), s32[]{:S(2)}) async-start(), calls=%async_computation.7 | async-start | bytes 3342336 | tf_op jit(solution)/shard_map/reduce_scatter | solution.py:372
  276.0 22.8 %collective-permute-start.22 = (bf16[2,4,128,192]{3,2,1,0:T(8,128)(2,1)S(1)}, bf16[2,4,128,192]{3,2,1,0:T(8,128)(2,1)S(1)}, u32[]{:S(2)}, u32[]{:S(2)}) collective-permute-start(bf16[2,4,128,192]{3,2,1,0:T(8,128)(2,1)S(1)} %pad_maximum_fusion.3.refs_0_), channel_id=1, source_target_pairs={{0,96},{16,112},{32,0},{48,16},{64,32},{80,48},{96,64},{112,80},{1... | collective-permute-start | bytes 1179656 | tf_op jit(solution)/shard_map/ppermute | solution.py:297
  320.2 142.0 %reduce-scatter.7.cloned.1.call-start = ((), (), s32[]{:S(2)}) async-start(), calls=%async_computation.5 | async-start | bytes 6684672 | tf_op jit(solution)/shard_map/reduce_scatter | solution.py:370
  320.8 221.1 %reduce-scatter.5.cloned.1.call-start = ((), (), s32[]{:S(2)}) async-start(), calls=%async_computation.4 | async-start | bytes 6684672 | tf_op jit(solution)/shard_map/reduce_scatter | solution.py:370
  322.7 26.5 %collective-permute-start.11 = (bf16[2,2,192,384]{3,2,1,0:T(8,128)(2,1)S(1)}, bf16[2,2,192,384]{3,2,1,0:T(8,128)(2,1)S(1)}, u32[]{:S(2)}, u32[]{:S(2)}) collective-permute-start(bf16[2,2,192,384]{3,2,1,0:T(8,128)(2,1)S(1)} %get-tuple-element.49), channel_id=1, source_target_pairs={{0,96},{16,112},{32,0},{48,16},{64,32},{80,48},{96,64},{112,80},{1... | collective-permute-start | bytes 1769480 | tf_op jit(solution)/shard_map/ppermute | solution.py:297
  323.7 30.1 %collective-permute-start.13 = (bf16[2,2,192,384]{3,2,1,0:T(8,128)(2,1)S(1)}, bf16[2,2,192,384]{3,2,1,0:T(8,128)(2,1)S(1)}, u32[]{:S(2)}, u32[]{:S(2)}) collective-permute-start(bf16[2,2,192,384]{3,2,1,0:T(8,128)(2,1)S(1)} %get-tuple-element.50), channel_id=1, source_target_pairs={{0,32},{16,48},{32,64},{48,80},{64,96},{80,112},{96,0},{112,16},{1... | collective-permute-start | bytes 1769480 | tf_op jit(solution)/shard_map/ppermute | solution.py:297
  324.8 29.1 %collective-permute-start.12 = (bf16[2,2,192,384]{3,2,1,0:T(8,128)(2,1)S(1)}, bf16[2,2,192,384]{3,2,1,0:T(8,128)(2,1)S(1)}, u32[]{:S(2)}, u32[]{:S(2)}) collective-permute-start(bf16[2,2,192,384]{3,2,1,0:T(8,128)(2,1)S(1)} %get-tuple-element.51), channel_id=1, source_target_pairs={{0,64},{16,80},{32,96},{48,112},{64,0},{80,16},{96,32},{112,48},{1... | collective-permute-start | bytes 1769480 | tf_op jit(solution)/shard_map/ppermute | solution.py:297
  326.8 37.4 %collective-permute-start.7 = (bf16[2,2,192,384]{3,2,1,0:T(8,128)(2,1)S(1)}, bf16[2,2,192,384]{3,2,1,0:T(8,128)(2,1)S(1)}, u32[]{:S(2)}, u32[]{:S(2)}) collective-permute-start(bf16[2,2,192,384]{3,2,1,0:T(8,128)(2,1)S(1)} %get-tuple-element.46), channel_id=1, source_target_pairs={{0,96},{16,112},{32,0},{48,16},{64,32},{80,48},{96,64},{112,80},{1... | collective-permute-start | bytes 1769480 | tf_op jit(solution)/shard_map/ppermute | solution.py:297
  328.5 48.7 %collective-permute-start.9 = (bf16[2,2,192,384]{3,2,1,0:T(8,128)(2,1)S(1)}, bf16[2,2,192,384]{3,2,1,0:T(8,128)(2,1)S(1)}, u32[]{:S(2)}, u32[]{:S(2)}) collective-permute-start(bf16[2,2,192,384]{3,2,1,0:T(8,128)(2,1)S(1)} %get-tuple-element.47), channel_id=1, source_target_pairs={{0,32},{16,48},{32,64},{48,80},{64,96},{80,112},{96,0},{112,16},{1... | collective-permute-start | bytes 1769480 | tf_op jit(solution)/shard_map/ppermute | solution.py:297
  349.1 28.0 %collective-permute-start.8 = (bf16[2,2,192,384]{3,2,1,0:T(8,128)(2,1)S(1)}, bf16[2,2,192,384]{3,2,1,0:T(8,128)(2,1)S(1)}, u32[]{:S(2)}, u32[]{:S(2)}) collective-permute-start(bf16[2,2,192,384]{3,2,1,0:T(8,128)(2,1)S(1)} %get-tuple-element.48), channel_id=1, source_target_pairs={{0,64},{16,80},{32,96},{48,112},{64,0},{80,16},{96,32},{112,48},{1... | collective-permute-start | bytes 1769480 | tf_op jit(solution)/shard_map/ppermute | solution.py:297
  354.2 26.8 %collective-permute-start.14 = (bf16[2,192,384]{2,1,0:T(8,128)(2,1)S(1)}, bf16[2,192,384]{2,1,0:T(8,128)(2,1)S(1)}, u32[]{:S(2)}, u32[]{:S(2)}) collective-permute-start(bf16[2,192,384]{2,1,0:T(8,128)(2,1)S(1)} %slice_bitcast_fusion), channel_id=1, source_target_pairs={{0,16},{16,0},{32,48},{48,32},{64,80},{80,64},{96,112},{112,96},{1... | collective-permute-start | bytes 884744 | tf_op jit(solution)/shard_map/ppermute | solution.py:301
  (29 other events, 216.0 us)
Sparse Core Ops, SparseCore 0:
  10.3 50.1 all-gather.4
  62.8 41.5 all-gather.6
  196.0 67.7 reduce-scatter.8
  320.3 65.1 reduce-scatter.10
  387.8 74.3 reduce-scatter.6
  464.4 77.4 reduce-scatter.4

commit v2 on v1

v2 whole, which is shorter than its diff:
```python
import functools
import math

import jax
import jax.numpy as jnp
from jax import lax
from jax.experimental import pallas as pl
from jax.experimental.pallas import tpu as pltpu
from jax.sharding import PartitionSpec as P

F32 = jnp.float32
BF = jnp.bfloat16
NT = (((1,), (1,)), ((), ()))
NN = (((1,), (0,)), ((), ()))
LOG2E = 1.4426950408889634
VMEM_LIMIT = 60 * 1024 * 1024
big_penalty = 1000000000.0


def dot(a, b, dims=NN):
    return lax.dot_general(a, b, dims, preferred_element_type=F32)


def attention_kernel(h0, heads, total_heads, first, last, tile, order_ref, cols_ref, *refs):
    q_ref, k_ref, v_ref, g_ref, do_ref, pc_ref, w_ref = refs[:7]
    bias_refs = refs[7:11]
    refs = refs[11:]
    head_start = h0 == 0
    if not first:
        acc_in, refs = refs[0], refs[1:]
    if head_start:
        gq_ref, gg_ref, dkt_out, dvt_out, acc_out = refs[:5]
        refs = refs[5:]
    else:
        gq_in, gg_in, dkt_in, dvt_in = refs[:4]
        gq_ref, gg_ref, keep_ref, send_ref, car_ref, acc_out = refs[4:10]
        refs = refs[10:]
    bias_s, s_s, e_s, t_s = refs[:4]
    refs = refs[4:]
    if not head_start:
        dkt_s, dvt_s, kv_s = refs[:3]
        refs = refs[3:]
    acc_s = acc_out
    if last:
        acc_s = refs[0]
        refs = refs[1:]
    i = pl.program_id(0)
    _, cj, chan = q_ref.shape
    head = chan // total_heads
    n = bias_s.shape[2]
    kb = n // 8
    scale = 1.0 / math.sqrt(head)
    tiles = n // tile
    fetch = None
    if not first:
        fetch = pltpu.make_async_copy(acc_in, acc_s, refs[0])

    @pl.when(i == 0)
    def _():
        if first:
            acc_s[...] = jnp.zeros(acc_s.shape, F32)
        else:
            fetch.start()
        for h in range(heads):
            for s in range(8):
                off = pl.multiple_of(order_ref[s] * kb, 128)
                bias_s[h, :, pl.ds(off, kb)] = bias_refs[s // 2][s % 2, h].astype(F32) * math.sqrt(head)

    def rows(ref, t):
        lo = t * tile
        out = []
        while lo < (t + 1) * tile:
            b, r = lo // cj, lo % cj
            m = min(cj - r, (t + 1) * tile - lo)
            out.append(ref[b, 0, r : r + m, :])
            lo += m
        return out[0] if len(out) == 1 else jnp.concatenate(out, axis=0)

    def lanes(h):
        lane = lax.broadcasted_iota(jnp.int32, (cj, chan), 1)
        return (lane >= (h0 + h) * head) & (lane < (h0 + h + 1) * head)

    def part(h):
        return slice((h0 + h) * head, (h0 + h + 1) * head)

    q = q_ref[0]
    q_t = q.astype(F32).T.astype(BF)
    tops = []
    for h in range(heads):
        qh = jnp.where(lanes(h), q, jnp.zeros_like(q))
        m = None
        for t in range(tiles):
            sl = slice(t * tile, (t + 1) * tile)
            s = dot(qh, rows(k_ref, t), NT) + bias_s[h, :, sl]
            s_s[h, :, sl] = s
            for u in range(tile // 128):
                p = s[:, u * 128 : (u + 1) * 128]
                m = p if m is None else jnp.maximum(m, p)
        tops.append(jnp.max(m, axis=1, keepdims=True))
    gate = jax.nn.sigmoid(g_ref[0].astype(F32))
    cot = do_ref[0].astype(F32)
    d_all = (cot * gate).astype(BF).astype(F32)
    gfac = cot * gate * (1.0 - gate)
    att_all = None
    stats = []
    for h in range(heads):
        lsum = None
        att = None
        for t in range(tiles):
            sl = slice(t * tile, (t + 1) * tile)
            e = jnp.exp2((s_s[h, :, sl] - tops[h]) * (scale * LOG2E))
            for u in range(tile // 128):
                p = e[:, u * 128 : (u + 1) * 128]
                lsum = p if lsum is None else lsum + p
            eb = e.astype(BF)
            e_s[h, :, sl] = eb
            a = dot(eb, rows(v_ref, t))
            att = a if att is None else att + a
        linv = 1.0 / jnp.sum(lsum, axis=1, keepdims=True)
        att = jnp.where(lanes(h), att * linv, 0.0)
        att_all = att if att_all is None else att_all + att
        delta = jnp.sum(d_all * att, axis=1, keepdims=True) * linv
        d_out = jnp.where(lanes(h), d_all * linv, 0.0)
        stats.append((delta, d_out.astype(BF)))
        t_s[h] = d_out.T.astype(BF)
    gg = gfac * att_all
    if not head_start:
        gg = gg + gg_in[0].astype(F32)
    gg_ref[0] = gg.astype(BF)

    if not first:

        @pl.when(i == 0)
        def _():
            fetch.wait()

    dq_all = None if head_start else gq_in[0].astype(F32)
    for h in range(heads):
        delta, dob = stats[h]
        out = slice(h * head, (h + 1) * head)
        do_t = t_s[h, part(h), :]
        dq = None
        for t in range(tiles):
            sl = slice(t * tile, (t + 1) * tile)
            dp = dot(dob, rows(v_ref, t), NT) - delta
            eb = e_s[h, :, sl]
            ds = eb.astype(F32) * dp
            acc_s[h, :, sl] += ds
            dsb = ds.astype(BF)
            a = dot(dsb, rows(k_ref, t))
            dq = a if dq is None else dq + a
            dk = dot(q_t[part(h), :], dsb) * scale
            dv = dot(do_t, eb)
            if head_start:
                dkt_out[0, out, sl] = dk.astype(BF)
                dvt_out[0, out, sl] = dv.astype(BF)
            else:
                dkt_s[out, sl] = dk
                dvt_s[out, sl] = dv
        dq = jnp.where(lanes(h), dq * scale, 0.0)
        dq_all = dq if dq_all is None else dq_all + dq
    gq = dq_all.astype(BF)
    gq_ref[0] = gq
    if not head_start:
        car = pc_ref[0].astype(F32) + dot(gq, w_ref[...], NT)
        car_ref[0] = car.T.astype(BF)
        for b in range(n // 384):
            sl = slice(b * 384, (b + 1) * 384)
            for j, old, new in ((0, dkt_in, dkt_s), (1, dvt_in, dvt_s)):
                both = jnp.concatenate([old[0, :, sl].astype(F32), new[:, sl]], axis=0).T.astype(BF)
                for c in range(384 // cj):
                    kv_s[(384 // cj) * b + c, j] = both[c * cj : (c + 1) * cj]
        half = n // cj // 2
        for r in range(half):
            keep_ref[r, 0] = kv_s[cols_ref[r]]
            send_ref[r, 0] = kv_s[cols_ref[half + r]]

    if last:

        @pl.when(i == pl.num_programs(0) - 1)
        def _():
            for h in range(heads):
                for s in range(8):
                    off = pl.multiple_of(s * kb, 128)
                    acc_out[s, h] = acc_s[h, :, pl.ds(off, kb)].astype(BF)


def attention(order, cols, q, kv, g, do, pc, w, biases, acc, earlier, h0, heads, total_heads, last, tile=3072):
    ni, cj, chan = q.shape
    nb = kv.shape[0]
    n = nb * cj
    kb = n // 8
    part = heads * (chan // total_heads)
    first = acc is None
    sd = jax.ShapeDtypeStruct

    def whole(*shape):
        return pl.BlockSpec(shape, lambda i, *r: (0,) * len(shape), pipeline_mode=pl.Buffered(1))

    per_row = pl.BlockSpec((1, cj, chan), lambda i, *r: (i, 0, 0))
    per_t = pl.BlockSpec((1, part, n), lambda i, *r: (i, 0, 0))
    k_spec = pl.BlockSpec((nb, 1, cj, chan), lambda i, *r: (0, i, 0, 0))
    v_spec = pl.BlockSpec((nb, 1, cj, chan), lambda i, *r: (0, ni + i, 0, 0))
    in_specs = [per_row, k_spec, v_spec, per_row, per_row, per_row, whole(chan, chan)]
    in_specs += [whole(2, heads, cj, kb)] * 4
    ops = [q, kv, kv, g, do, pc, w, *biases]
    if not first:
        in_specs.append(pl.BlockSpec(memory_space=pl.ANY))
        ops.append(acc)
    out_specs = [per_row, per_row]
    out_shape = [sd((ni, cj, chan), BF), sd((ni, cj, chan), BF)]
    scratch = [
        pltpu.VMEM((heads, cj, n), F32),
        pltpu.VMEM((heads, cj, n), F32),
        pltpu.VMEM((heads, cj, n), BF),
        pltpu.VMEM((heads, chan, cj), BF),
    ]
    if h0 == 0:
        out_specs += [per_t, per_t]
        out_shape += [sd((ni, part, n), BF), sd((ni, part, n), BF)]
    else:
        in_specs += [per_row, per_row, per_t, per_t]
        ops += earlier
        half = nb // 2
        kv_out = pl.BlockSpec((half, 1, 2, cj, chan), lambda i, *r: (0, i, 0, 0, 0))
        out_specs += [kv_out, kv_out, pl.BlockSpec((1, chan, cj), lambda i, *r: (i, 0, 0))]
        out_shape += [sd((half, ni, 2, cj, chan), BF), sd((half, ni, 2, cj, chan), BF), sd((ni, chan, cj), BF)]
        scratch += [pltpu.VMEM((part, n), F32), pltpu.VMEM((part, n), F32), pltpu.VMEM((nb, 2, cj, chan), BF)]
    if last:
        out_specs.append(whole(8, heads, cj, kb))
        out_shape.append(sd((8, heads, cj, kb), BF))
        scratch.append(pltpu.VMEM((heads, cj, n), F32))
    else:
        out_specs.append(whole(heads, cj, n))
        out_shape.append(sd((heads, cj, n), F32))
    if not first:
        scratch.append(pltpu.SemaphoreType.DMA(()))
    return pl.pallas_call(
        functools.partial(attention_kernel, h0, heads, total_heads, first, last, tile),
        grid_spec=pltpu.PrefetchScalarGridSpec(
            num_scalar_prefetch=2, grid=(ni,), in_specs=in_specs, out_specs=out_specs, scratch_shapes=scratch
        ),
        out_shape=out_shape,
        compiler_params=pltpu.CompilerParams(dimension_semantics=("arbitrary",), vmem_limit_bytes=VMEM_LIMIT),
        cost_estimate=pl.CostEstimate(
            flops=16 * heads * ni * cj * n * chan, bytes_accessed=30_000_000, transcendentals=heads * ni * cj * n
        ),
        name="attention_rows",
    )(order, cols, *ops)


def left_kernel(order_ref, cols_ref, *refs):
    car = refs[:4]
    r_ref, keep_ref, send_ref, l_s, o_s = refs[4:]
    step = pl.program_id(0)
    _, ni, chan, cj = car[0].shape
    cb, _, kk = r_ref.shape
    rows = 8 * ni
    half = ni // 2

    @pl.when(step == 0)
    def _():
        for s in range(8):
            for i in range(ni):
                at = pl.ds(pl.multiple_of((order_ref[s] * ni + i) * chan, chan), chan)
                x = car[s // 2][s % 2, i].astype(F32)
                l_s[0, at, :] = x[:, :128]
                l_s[1, at, : cj - 128] = x[:, 128:]

    for u in range(cb):
        c = step * cb + u
        a = l_s[0, pl.ds(c, rows, stride=chan), :]
        b = l_s[1, pl.ds(c, rows, stride=chan), :][:, : cj - 128]
        res = dot(jnp.concatenate([a, b], axis=1).astype(BF), r_ref[u])
        for b in range(kk // 128):
            o_s[b, pl.ds(c, rows, stride=chan), :] = res[:, b * 128 : (b + 1) * 128]

    @pl.when(step == pl.num_programs(0) - 1)
    def _():
        for r in range(8):
            for ref, col in ((keep_ref, cols_ref[r]), (send_ref, cols_ref[8 + r])):
                for i in range(half):
                    at = pl.ds(pl.multiple_of((col * half + i) * chan, chan), chan)
                    for b in range(kk // 128):
                        ref[r, i, b * 128 : (b + 1) * 128, :] = o_s[b, at, :].T.astype(BF)


def left_product(order, cols, cars, right_t, cb=16):
    _, ni, chan, cj = cars[0].shape
    kk = right_t.shape[2]

    def whole(*shape):
        return pl.BlockSpec(shape, lambda t, *r: (0,) * len(shape), pipeline_mode=pl.Buffered(1))

    return pl.pallas_call(
        left_kernel,
        grid_spec=pltpu.PrefetchScalarGridSpec(
            num_scalar_prefetch=2,
            grid=(chan // cb,),
            in_specs=[whole(2, ni, chan, cj)] * 4 + [pl.BlockSpec((cb, cj, kk), lambda t, *r: (t, 0, 0))],
            out_specs=[whole(8, ni // 2, kk, chan)] * 2,
            scratch_shapes=[
                pltpu.VMEM((2, 8 * ni * chan, 128), F32),
                pltpu.VMEM((kk // 128, 8 * ni * chan, 128), F32),
            ],
        ),
        out_shape=[jax.ShapeDtypeStruct((8, ni // 2, kk, chan), BF)] * 2,
        compiler_params=pltpu.CompilerParams(dimension_semantics=("arbitrary",), vmem_limit_bytes=VMEM_LIMIT),
        cost_estimate=pl.CostEstimate(
            flops=40_000_000_000, bytes_accessed=30_000_000, transcendentals=0
        ),
        name="left_product",
    )(order, cols, *cars, right_t)


def row_shift(x, dy):
    return lax.ppermute(x, "row", [(2 * y + z, 2 * ((y + dy) % 4) + z) for y in range(4) for z in range(2)])


def row_swap(x):
    return lax.ppermute(x, "row", [(r, r ^ 1) for r in range(8)])


def row_pair(x):
    return jnp.stack([x, row_swap(x)])


def row_gather(pair):
    return [pair] + [row_shift(pair, dy) for dy in (1, 2, 3)]


def row_sides(pair):
    return [row_shift(pair, 1), row_shift(pair, 3)]


def row_far(pair, side):
    back, on = side
    far = jnp.stack([row_shift(on[0], 3), row_shift(back[1], 1)])
    return [pair, back, far, on]


def add_all(parts):
    return sum(p.astype(F32) for p in parts).astype(BF)


def core_swap(send):
    return lax.ppermute(send, "col", [(c, c ^ 1) for c in range(16)])


def add_pair(a, b):
    return (a.astype(F32) + b.astype(F32)).astype(BF)


def core_sum(keep, send):
    return add_pair(keep, core_swap(send))


def x_shift(part, dx):
    return lax.ppermute(part[2 * dx : 2 * dx + 2], "col", [(c, (c + 4 * dx) % 16) for c in range(16)])


def z_swap(total):
    return lax.ppermute(total[1], "col", [(c, c ^ 2) for c in range(16)])


def z_sum(total):
    return add_pair(total[0], z_swap(total))


def after(x, *done):
    return lax.optimization_barrier((x, done))[0]


def local(
    queries,
    keys,
    values,
    gate_logits,
    out_grad,
    pair_bias,
    residue_mask,
    query_weight,
    pair_cotangent,
    right_proj,
):
    total_heads = pair_bias.shape[0]
    kb = pair_bias.shape[2]
    rb = queries.shape[0]
    row = lax.axis_index("row")
    y, z = row // 2, row % 2
    order = jnp.stack([2 * ((y - s // 2 + 4) % 4) + (z ^ (s % 2)) for s in range(8)]).astype(jnp.int32)
    col = lax.axis_index("col")
    x, zl, core = col // 4, (col // 2) % 2, col % 2
    cols = jnp.stack(
        [((x + r % 8 // 2) % 4) * 4 + (zl ^ (r % 2)) * 2 + (core ^ (r // 8)) for r in range(16)]
    ).astype(jnp.int32)
    penalty = big_penalty * (lax.dynamic_slice_in_dim(residue_mask, row * kb, kb).astype(F32) - 1.0)
    bias = (pair_bias.astype(F32) + penalty[None, None, :]).astype(BF)
    hs = total_heads // 2
    pairs = row_pair(bias)
    biases = [row_gather(pairs[:, :hs]), row_gather(pairs[:, hs:])]
    right_t = jnp.transpose(right_proj, (2, 0, 1))

    quarter = rb // 4
    picks = [
        tuple(range(0, quarter)) + tuple(range(2 * quarter, 3 * quarter)),
        tuple(range(quarter, 2 * quarter)) + tuple(range(3 * quarter, rb)),
    ]

    def take(x, ids):
        return jnp.concatenate([x[ids[0] : ids[quarter - 1] + 1], x[ids[quarter] : ids[-1] + 1]])

    gathered = [
        lax.all_gather(jnp.concatenate([take(keys, ids), take(values, ids)]), "col", axis=0) for ids in picks
    ]
    order, right_t = lax.optimization_barrier((order, right_t))
    small = [[take(a, ids) for a in (queries, gate_logits, out_grad, pair_cotangent)] for ids in picks]

    def attend(part, half, acc, earlier, order):
        q, g, do, pc = small[part]
        return attention(
            order, cols, q, gathered[part], g, do, pc, query_weight, biases[half],
            acc, earlier, half * hs, hs, total_heads, part == 1,
        )

    a = attend(0, 0, None, None, order)
    b = attend(0, 1, None, list(a[:4]), order)
    gq0, gg0, keep, send, car0 = b[:5]
    part0 = core_sum(keep, send)
    pair0 = row_pair(car0)
    order_c, part0, pair0 = lax.optimization_barrier((order, part0, pair0))
    near0 = [x_shift(part0, 1), x_shift(part0, 3)]
    side0 = row_sides(pair0)
    c = attend(1, 0, a[-1], None, order_c)
    near0, side0 = after((near0, side0), c[0])
    total0 = add_all([part0[0:2]] + near0)
    order_d, total0, side0 = lax.optimization_barrier((order, total0, side0))
    far0 = x_shift(part0, 2)
    cars0 = row_far(pair0, side0)
    d = attend(1, 1, b[-1], list(c[:4]), order_d)
    gq1, gg1, keep, send, car1 = d[:5]
    far0, cars0 = after((far0, cars0), gq1)
    total0 = add_all([total0, far0])
    order_l, total0, cars0, car1, send = lax.optimization_barrier((order, total0, cars0, car1, send))
    swap1 = row_swap(car1)
    got1 = core_swap(send)
    got_z0 = z_swap(total0)
    left0 = left_product(order_l, cols, cars0, right_t)
    swap1, got1, got_z0, left0 = lax.optimization_barrier((swap1, got1, got_z0, left0))
    dkv0 = add_pair(total0[0], got_z0)
    part1 = add_pair(keep, got1)
    pair1 = jnp.stack([car1, swap1])
    pair1, part1, left0 = lax.optimization_barrier((pair1, part1, left0))
    side1 = row_sides(pair1)
    got_l0 = core_swap(left0[1])
    near1 = [x_shift(part1, 1)]
    side1, got_l0 = lax.optimization_barrier((side1, got_l0))
    cars1 = row_far(pair1, side1)
    near1.append(x_shift(after(part1, got_l0), 3))
    far1 = x_shift(after(part1, cars1), 2)
    left1 = left_product(after(order, cars1), cols, cars1, right_t)
    near1, far1 = after((near1, far1), left1)
    part_l0 = add_pair(left0[0], after(got_l0, left1))
    total1 = add_all([part1[0:2], near1[0], near1[1], far1])
    total1, part_l0, left1 = lax.optimization_barrier((total1, part_l0, left1))
    dkv1 = z_sum(total1)
    part_l1 = core_sum(*left1)
    sums = [add_all([p[0:2], x_shift(p, 1), x_shift(p, 3), x_shift(p, 2)]) for p in (part_l0, part_l1)]
    left = z_sum(jnp.concatenate(sums, axis=1))
    bias_sum = [lax.psum_scatter(t[-1], "row", scatter_dimension=0).astype(F32) for t in (c, d)]

    def untake(a, b):
        return jnp.concatenate([a[:quarter], b[:quarter], a[quarter:], b[quarter:]])

    gq, gg = untake(gq0, gq1), untake(gg0, gg1)
    dk, dv = untake(dkv0[:, 0], dkv1[:, 0]), untake(dkv0[:, 1], dkv1[:, 1])
    return (gq, dk, dv, gg, jnp.concatenate(bias_sum), left)


def solution(mesh):
    in_specs = (
        P("row", "col", None),
        P("row", "col", None),
        P("row", "col", None),
        P("row", "col", None),
        P("row", "col", None),
        P(None, "col", "row"),
        P(),
        P(),
        P("row", "col", None),
        P("col", "row", None),
    )
    out_specs = (
        P("row", "col", None),
        P("row", "col", None),
        P("row", "col", None),
        P("row", "col", None),
        P(None, "col", "row"),
        P("col", "row", None),
    )
    return jax.shard_map(local, mesh=mesh, in_specs=in_specs, out_specs=out_specs, check_vma=False)
```

time: 556 us -> 401 us (0.72)
  waiting for transfers between devices: 276 us -> 119 us
  Pallas kernels: 173 us -> 134 us
  other arithmetic: 14.8 us -> 34.1 us
  starting transfers between devices: 38.3 us -> 53.1 us
  local copies, waits for them, and re-layouts: 34.6 us -> 42.2 us
    reduce_scatter x4 -> x2, waiting for transfers between devices: 150 us -> 21.2 us  [local(): lax.psum_scatter(t[-1], 'row', scatter_dimension=0).astype(F32)]
    ppermute x0 -> x19, waiting for transfers between devices: none -> 48.6 us  [the longest x12 42.1 us: x_shift(): lax.ppermute(part[2 * dx:2 * dx + 2], 'col', [(c, (c + 4 * dx) % 16) for...]
    ppermute x18 -> x14, waiting for transfers between devices: 88.7 us -> 40.7 us  [row_shift(): lax.ppermute(x, 'row', [(2 * y + z, 2 * ((y + dy) % 4) + z) for y in rang...]
    pallas_call x4, Pallas kernels: 140 us -> 99.5 us  [attention(): pl.pallas_call(functools.partial(attention_kernel, h0, heads, total_heads...]
    ppermute x5 -> x3, waiting for transfers between devices: 35.9 us -> 8.36 us  [row_swap(): return lax.ppermute(x, 'row', [(r, r ^ 1) for r in range(8)])]
    ppermute x0 -> x19, starting transfers between devices: none -> 18.9 us  [the longest x12 17 us: x_shift(): lax.ppermute(part[2 * dx:2 * dx + 2], 'col', [(c, (c + 4 * dx) % 16) for...]
    convert_element_type x2 -> x12, other arithmetic: 0.63 us -> 17.8 us  [the longest x7 10.4 us: add_pair(): return (a.astype(F32) + b.astype(F32)).astype(BF)]
    ppermute x5 -> x3, starting transfers between devices: 16.5 us -> 6.01 us  [row_swap(): return lax.ppermute(x, 'row', [(r, r ^ 1) for r in range(8)])]
  transfers between devices with their start and end apart: 29 -> 40, of which waited for: 14 -> 17; matrix products, arithmetic and copies ran while one was open for 7% -> 18% of each run, Pallas kernels for 31% -> 34%
where the time goes in v2:
time: 401 us; the launch traced here: 396 us
  Pallas kernels  134 us (33%)
  waiting for transfers between devices  119 us (30%)
  starting transfers between devices  53.1 us (13%)
  local copies, waits for them, and re-layouts  42.2 us (11%)
  other arithmetic  34.1 us (9%)
  between operations  14.5 us (4%)
    pallas_call x4, Pallas kernels, attention(): pl.pallas_call(functools.partial(attention_kernel, h0, heads, total_heads...  99.5 us
    ppermute x12, waiting for transfers between devices, x_shift(): lax.ppermute(part[2 * dx:2 * dx + 2], 'col', [(c, (c + 4 * dx) % 16) for...  42.1 us
    ppermute x14, waiting for transfers between devices, row_shift(): lax.ppermute(x, 'row', [(2 * y + z, 2 * ((y + dy) % 4) + z) for y in rang...  40.7 us
    pallas_call x2, Pallas kernels, left_product(): pl.pallas_call(left_kernel, grid_spec=pltpu.PrefetchScalarGridSpec(num_sc...  34 us
    ppermute x14, starting transfers between devices, row_shift(): lax.ppermute(x, 'row', [(2 * y + z, 2 * ((y + dy) % 4) + z) for y in rang...  28 us
    unnamed x51, local copies, waits for them, and re-layouts  27.7 us
    reduce_scatter x2, waiting for transfers between devices, local(): lax.psum_scatter(t[-1], 'row', scatter_dimension=0).astype(F32)  21.2 us
    ppermute x12, starting transfers between devices, x_shift(): lax.ppermute(part[2 * dx:2 * dx + 2], 'col', [(c, (c + 4 * dx) % 16) for...  17 us
  transfers between devices with their start and end apart: 40, of which 17 were waited for; matrix products, arithmetic and copies ran while one was open for 18% of the time, Pallas kernels for 34%

profile of v2, /device:TPU:0, one launch (start us, length us, event | category | flops | bytes accessed | tf_op | source)
XLA Modules:
  0.0 396.5 jit_solution(2194406373930454034)
XLA Ops:
  11.2 4.0 %collective-permute-start = (bf16[4,192,384]{2,1,0:T(8,128)(2,1)S(1)}, bf16[4,192,384]{2,1,0:T(8,128)(2,1)S(1)}, u32[]{:S(2)}, u32[]{:S(2)}) collective-permute-start(bf16[4,192,384]{2,1,0:T(8,128)(2,1)S(1)} %add_convert_fusion.7), channel_id=1, source_target_pairs={{0,16},{16,0},{32,48},{48,32},{64,80},{80,64},{96,112},{112,96},{1... | collective-permute-start | bytes 1769480 | tf_op jit(solution)/shard_map/ppermute | solution.py:321
  15.2 24.5 %copy.22 = bf16[192,384,128]{1,0,2:T(8,128)(2,1)} copy(bf16[192,384,128]{2,1,0:T(8,128)(2,1)} %param.19) | data formatting | bytes 37748736 | tf_op args[9]
  50.4 10.6 %collective-permute-done.4.refs_8_ = bf16[2,2,192,384]{3,2,1,0:T(8,128)(2,1)S(1)} collective-permute-done((bf16[2,2,192,384]{3,2,1,0:T(8,128)(2,1)S(1)}, bf16[2,2,192,384]{3,2,1,0:T(8,128)(2,1)S(1)}, u32[]{:S(2)}, u32[]{:S(2)}) %collective-permute-start.4) | collective-permute-done | bytes 589856 | tf_op jit(solution)/shard_map/ppermute | solution.py:317
  61.7 11.8 %collective-permute-done.5.refs_9_ = bf16[2,2,192,384]{3,2,1,0:T(8,128)(2,1)S(1)} collective-permute-done((bf16[2,2,192,384]{3,2,1,0:T(8,128)(2,1)S(1)}, bf16[2,2,192,384]{3,2,1,0:T(8,128)(2,1)S(1)}, u32[]{:S(2)}, u32[]{:S(2)}) %collective-permute-start.5) | collective-permute-done | bytes 589856 | tf_op jit(solution)/shard_map/ppermute | solution.py:317
  74.4 23.3 %attention_rows.4 = (bf16[4,192,128]{2,1,0:T(8,128)(2,1)}, bf16[4,192,128]{2,1,0:T(8,128)(2,1)}, bf16[4,64,3072]{2,1,0:T(8,128)(2,1)}, bf16[4,64,3072]{2,1,0:T(8,128)(2,1)}, f32[2,192,3072]{2,1,0:T(8,128)}) custom-call(s32[8]{0:T(128)} %stack.131.order_ref, s32[16]{0:T(128)} %stack.148.cols_ref, bf16[4,192,128]{2,1,0:T(8,128)(2,1)} %get-tuple-element.211.refs_0_, ...), custom_call_target="tpu_custom_call" | custom-call | flops 9663676416 | bytes 30000000 | tf_op jit(solution)/shard_map/attention_rows/pallas_call | solution.py:238
  98.8 25.6 %attention_rows.5 = (bf16[4,192,128]{2,1,0:T(8,128)(2,1)}, bf16[4,192,128]{2,1,0:T(8,128)(2,1)}, bf16[8,4,2,192,128]{4,3,2,1,0:T(8,128)(2,1)}, bf16[8,4,2,192,12...) custom-call(s32[8]{0:T(128)} %stack.131.order_ref, s32[16]{0:T(128)} %stack.148.cols_ref, ...), custom_call_target="tpu_custom_call" | custom-call | flops 9663676416 | bytes 30000000 | tf_op jit(solution)/shard_map/attention_rows/pallas_call | solution.py:238
  129.2 8.4 %collective-permute-done.8 = bf16[4,128,192]{2,1,0:T(8,128)(2,1)S(1)} collective-permute-done((bf16[4,128,192]{2,1,0:T(8,128)(2,1)S(1)}, bf16[4,128,192]{2,1,0:T(8,128)(2,1)S(1)}, u32[]{:S(2)}, u32[]{:S(2)}) %collective-permute-start.8) | collective-permute-done | bytes 196640 | tf_op jit(solution)/shard_map/ppermute | solution.py:321
  139.6 11.1 %collective-permute-start.11 = (bf16[2,4,128,192]{3,2,1,0:T(8,128)(2,1)}, bf16[2,4,128,192]{3,2,1,0:T(8,128)(2,1)}, u32[]{:S(2)}, u32[]{:S(2)}) collective-permute-start(bf16[2,4,128,192]{3,2,1,0:T(8,128)(2,1)} %pad_maximum_fusion.1.refs_0_), channel_id=1, source_target_pairs={{0,32},{16,48},{32,64},{48,80},{64,96},{80,112},{96,0},{112,16},{1... | collective-permute-start | bytes 1179656 | tf_op jit(solution)/shard_map/ppermute | solution.py:317
  157.4 24.2 %attention_rows.6 = (bf16[4,192,128]{2,1,0:T(8,128)(2,1)}, bf16[4,192,128]{2,1,0:T(8,128)(2,1)}, bf16[4,64,3072]{2,1,0:T(8,128)(2,1)}, bf16[4,64,3072]{2,1,0:T(8,128)(2,1)}, bf16[8,2,192,384]{3,2,1,0:T(8,128)(2,1)}) custom-call(s32[8]{0:T(128)} %stack.131.order_ref, s32[16]{0:T(128)} %stack.148.cols_ref, bf16[4,192,128]{2,1,0:T(8,128)(2,1)} %get-tuple-element.215.refs_0_, ...), custom_call_target="tpu_custom_call" | custom-call | flops 9663676416 | bytes 30000000 | tf_op jit(solution)/shard_map/attention_rows/pallas_call | solution.py:238
  181.7 6.8 %collective-permute-done.10 = bf16[2,4,2,192,128]{4,3,1,2,0:T(8,128)(2,1)} collective-permute-done((bf16[2,4,2,192,128]{4,3,1,2,0:T(8,128)(2,1)}, bf16[2,4,2,192,128]{4,3,1,2,0:T(8,128)(2,1)}, u32[]{:S(2)}, u32[]{:S(2)}) %collective-permute-start.10) | collective-permute-done | bytes 786464 | tf_op jit(solution)/shard_map/ppermute | solution.py:359
  188.5 3.4 collective-permute-done.9
  198.8 26.4 %attention_rows.7 = (bf16[4,192,128]{2,1,0:T(8,128)(2,1)}, bf16[4,192,128]{2,1,0:T(8,128)(2,1)}, bf16[8,4,2,192,128]{4,3,2,1,0:T(8,128)(2,1)}, bf16[8,4,2,192,12...) custom-call(s32[8]{0:T(128)} %stack.131.order_ref, s32[16]{0:T(128)} %stack.148.cols_ref, ...), custom_call_target="tpu_custom_call" | custom-call | flops 9663676416 | bytes 30000000 | tf_op jit(solution)/shard_map/attention_rows/pallas_call | solution.py:238
  230.4 17.0 %left_product.2 = (bf16[8,2,384,128]{3,2,1,0:T(8,128)(2,1)}, bf16[8,2,384,128]{3,2,1,0:T(8,128)(2,1)}) custom-call(s32[8]{0:T(128)} %stack.131.order_ref, s32[16]{0:T(128)} %stack.148.cols_ref, bf16[2,4,128,192]{3,2,1,0:T(8,128)(2,1)} %pad_maximum_fusion.1.refs_0_, bf16[2,4,128,192]{3,2,1,0:T(8,128)(2,1)} %collective-permute-done.11.refs_1_, ...), custom_call_target="tpu_custom_call" | custom-call | flops 40000000000 | bytes 30000000 | tf_op jit(solution)/shard_map/left_product/pallas_call | solution.py:295
  249.8 4.2 %add_convert_fusion = bf16[8,4,2,192,128]{4,3,2,1,0:T(8,128)(2,1)S(1)} fusion(bf16[8,4,2,192,128]{4,3,2,1,0:T(8,128)(2,1)} %copy-done.2, bf16[8,4,2,192,128]{4,3,2,1,0:T(8,128)(2,1)} %get-tuple-element.128), kind=kLoop, calls=%fused_computation | loop fusion | flops 6291456 | bytes 9437184 | tf_op jit(solution)/shard_map/convert_element_type | solution.py:351
  257.5 12.5 %collective-permute-done.20.refs_1_ = bf16[2,4,128,192]{3,2,1,0:T(8,128)(2,1)} collective-permute-done((bf16[2,4,128,192]{3,2,1,0:T(8,128)(2,1)}, bf16[2,4,128,192]{3,2,1,0:T(8,128)(2,1)}, u32[]{:S(2)}, u32[]{:S(2)}) %collective-permute-start.20) | collective-permute-done | bytes 393248 | tf_op jit(solution)/shard_map/ppermute | solution.py:317
  281.5 5.5 %collective-permute-done.25 = bf16[4,128,192]{2,1,0:T(8,128)(2,1)S(1)} collective-permute-done((bf16[4,128,192]{2,1,0:T(8,128)(2,1)S(1)}, bf16[4,128,192]{2,1,0:T(8,128)(2,1)S(1)}, u32[]{:S(2)}, u32[]{:S(2)}) %collective-permute-start.25) | collective-permute-done | bytes 196640 | tf_op jit(solution)/shard_map/ppermute | solution.py:317
  289.0 16.9 %left_product.3 = (bf16[8,2,384,128]{3,2,1,0:T(8,128)(2,1)}, bf16[8,2,384,128]{3,2,1,0:T(8,128)(2,1)}) custom-call(s32[8]{0:T(128)} %stack.131.order_ref, s32[16]{0:T(128)} %stack.148.cols_ref, bf16[2,4,128,192]{3,2,1,0:T(8,128)(2,1)} %pad_maximum_fusion.3.refs_0_, bf16[2,4,128,192]{3,2,1,0:T(8,128)(2,1)} %collective-permute-done.20.refs_1_, ...), custom_call_target="tpu_custom_call" | custom-call | flops 40000000000 | bytes 30000000 | tf_op jit(solution)/shard_map/left_product/pallas_call | solution.py:295
  305.9 3.6 add_convert_fusion.3
  309.5 4.5 %collective-permute-done.19 = bf16[2,4,2,192,128]{4,3,2,1,0:T(8,128)(2,1)} collective-permute-done((bf16[2,4,2,192,128]{4,3,2,1,0:T(8,128)(2,1)}, bf16[2,4,2,192,128]{4,3,2,1,0:T(8,128)(2,1)}, u32[]{:S(2)}, u32[]{:S(2)}) %collective-permute-start.19) | collective-permute-done | bytes 786464 | tf_op jit(solution)/shard_map/ppermute | solution.py:359
  319.2 21.2 %reduce-scatter.5.cloned.1.call-done = bf16[1,2,192,384]{3,2,1,0:T(8,128)(2,1)} async-done(((bf16[8,2,192,384]{3,2,1,0:T(8,128)(2,1)}), bf16[1,2,192,384]{3,2,1,0:T(8,128)(2,1)}) %reduce-scatter.5.cloned.1.call-update) | async-done | bytes 294928 | tf_op jit(solution)/shard_map/reduce_scatter | solution.py:470
  349.7 13.7 %collective-permute-done.28 = bf16[2,2,384,128]{3,2,1,0:T(8,128)(2,1)S(1)} collective-permute-done((bf16[2,2,384,128]{3,2,1,0:T(8,128)(2,1)S(1)}, bf16[2,2,384,128]{3,2,1,0:T(8,128)(2,1)S(1)}, u32[]{:S(2)}, u32[]{:S(2)}) %collective-permute-start.28) | collective-permute-done | bytes 393248 | tf_op jit(solution)/shard_map/ppermute | solution.py:359
  366.5 5.4 %collective-permute-done.32 = bf16[2,2,384,128]{3,2,1,0:T(8,128)(2,1)S(1)} collective-permute-done((bf16[2,2,384,128]{3,2,1,0:T(8,128)(2,1)S(1)}, bf16[2,2,384,128]{3,2,1,0:T(8,128)(2,1)S(1)}, u32[]{:S(2)}, u32[]{:S(2)}) %collective-permute-start.32) | collective-permute-done | bytes 393248 | tf_op jit(solution)/shard_map/ppermute | solution.py:359
  371.9 6.3 %collective-permute-done.33 = bf16[2,2,384,128]{3,2,1,0:T(8,128)(2,1)S(1)} collective-permute-done((bf16[2,2,384,128]{3,2,1,0:T(8,128)(2,1)S(1)}, bf16[2,2,384,128]{3,2,1,0:T(8,128)(2,1)S(1)}, u32[]{:S(2)}, u32[]{:S(2)}) %collective-permute-start.33) | collective-permute-done | bytes 393248 | tf_op jit(solution)/shard_map/ppermute | solution.py:359
  382.4 6.5 %collective-permute-done.35 = bf16[4,384,128]{2,1,0:T(8,128)(2,1)S(1)} collective-permute-done((bf16[4,384,128]{2,1,0:T(8,128)(2,1)S(1)}, bf16[4,384,128]{2,1,0:T(8,128)(2,1)S(1)}, u32[]{:S(2)}, u32[]{:S(2)}) %collective-permute-start.35) | collective-permute-done | bytes 393248 | tf_op jit(solution)/shard_map/ppermute | solution.py:363
  (175 shorter events, 84.4 us)
Async XLA Ops:
  7.2 67.2 %all-gather.5.cloned.1.call-start = ((), (), s32[]{:S(2)}) async-start(), calls=%async_computation.4 | async-start | bytes 6684672 | tf_op jit(solution)/shard_map/all_gather | solution.py:414
  9.3 148.1 %all-gather.7.cloned.1.call-start = ((), (), s32[]{:S(2)}) async-start(), calls=%async_computation.5 | async-start | bytes 6684672 | tf_op jit(solution)/shard_map/all_gather | solution.py:414
  10.2 309.0 %reduce-scatter.3.cloned.1.call-start = ((), (), s32[]{:S(2)}) async-start(), calls=%async_computation.2 | async-start | bytes 2654208 | tf_op jit(solution)/shard_map/reduce_scatter | solution.py:470
  11.2 30.8 %collective-permute-start = (bf16[4,192,384]{2,1,0:T(8,128)(2,1)S(1)}, bf16[4,192,384]{2,1,0:T(8,128)(2,1)S(1)}, u32[]{:S(2)}, u32[]{:S(2)}) collective-permute-start(bf16[4,192,384]{2,1,0:T(8,128)(2,1)S(1)} %add_convert_fusion.7), channel_id=1, source_target_pairs={{0,16},{16,0},{32,48},{48,32},{64,80},{80,64},{96,112},{112,96},{1... | collective-permute-start | bytes 1769480 | tf_op jit(solution)/shard_map/ppermute | solution.py:321
  43.8 29.8 %collective-permute-start.5 = (bf16[2,2,192,384]{3,2,1,0:T(8,128)(2,1)S(1)}, bf16[2,2,192,384]{3,2,1,0:T(8,128)(2,1)S(1)}, u32[]{:S(2)}, u32[]{:S(2)}) collective-permute-start(bf16[2,2,192,384]{3,2,1,0:T(8,128)(2,1)S(1)} %get-tuple-element.165.refs_7_), channel_id=1, source_target_pairs={{0,64},{16,80},{32,96},{48,112},{64,0},{80,16},{96,32},{112,48},{1... | collective-permute-start | bytes 1769480 | tf_op jit(solution)/shard_map/ppermute | solution.py:317
  46.7 27.7 %collective-permute-start.6 = (bf16[2,2,192,384]{3,2,1,0:T(8,128)(2,1)S(1)}, bf16[2,2,192,384]{3,2,1,0:T(8,128)(2,1)}, u32[]{:S(2)}, u32[]{:S(2)}) collective-permute-start(bf16[2,2,192,384]{3,2,1,0:T(8,128)(2,1)S(1)} %get-tuple-element.165.refs_7_), channel_id=1, source_target_pairs={{0,96},{16,112},{32,0},{48,16},{64,32},{80,48},{96,64},{112,80},{1... | collective-permute-start | bytes 1769480 | tf_op jit(solution)/shard_map/ppermute | solution.py:317
  48.9 48.8 %collective-permute-start.1 = (bf16[2,2,192,384]{3,2,1,0:T(8,128)(2,1)S(1)}, bf16[2,2,192,384]{3,2,1,0:T(8,128)(2,1)S(1)}, u32[]{:S(2)}, u32[]{:S(2)}) collective-permute-start(bf16[2,2,192,384]{3,2,1,0:T(8,128)(2,1)S(1)} %get-tuple-element.166.refs_7_), channel_id=1, source_target_pairs={{0,32},{16,48},{32,64},{48,80},{64,96},{80,112},{96,0},{112,16},{1... | collective-permute-start | bytes 1769480 | tf_op jit(solution)/shard_map/ppermute | solution.py:317
  49.6 48.2 %collective-permute-start.2 = (bf16[2,2,192,384]{3,2,1,0:T(8,128)(2,1)S(1)}, bf16[2,2,192,384]{3,2,1,0:T(8,128)(2,1)S(1)}, u32[]{:S(2)}, u32[]{:S(2)}) collective-permute-start(bf16[2,2,192,384]{3,2,1,0:T(8,128)(2,1)S(1)} %get-tuple-element.166.refs_7_), channel_id=1, source_target_pairs={{0,64},{16,80},{32,96},{48,112},{64,0},{80,16},{96,32},{112,48},{1... | collective-permute-start | bytes 1769480 | tf_op jit(solution)/shard_map/ppermute | solution.py:317
  61.0 36.8 %collective-permute-start.3 = (bf16[2,2,192,384]{3,2,1,0:T(8,128)(2,1)S(1)}, bf16[2,2,192,384]{3,2,1,0:T(8,128)(2,1)}, u32[]{:S(2)}, u32[]{:S(2)}) collective-permute-start(bf16[2,2,192,384]{3,2,1,0:T(8,128)(2,1)S(1)} %get-tuple-element.166.refs_7_), channel_id=1, source_target_pairs={{0,96},{16,112},{32,0},{48,16},{64,32},{80,48},{96,64},{112,80},{1... | collective-permute-start | bytes 1769480 | tf_op jit(solution)/shard_map/ppermute | solution.py:317
  139.6 42.1 %collective-permute-start.11 = (bf16[2,4,128,192]{3,2,1,0:T(8,128)(2,1)}, bf16[2,4,128,192]{3,2,1,0:T(8,128)(2,1)}, u32[]{:S(2)}, u32[]{:S(2)}) collective-permute-start(bf16[2,4,128,192]{3,2,1,0:T(8,128)(2,1)} %pad_maximum_fusion.1.refs_0_), channel_id=1, source_target_pairs={{0,32},{16,48},{32,64},{48,80},{64,96},{80,112},{96,0},{112,16},{1... | collective-permute-start | bytes 1179656 | tf_op jit(solution)/shard_map/ppermute | solution.py:317
  150.7 31.0 %collective-permute-start.12 = (bf16[2,4,128,192]{3,2,1,0:T(8,128)(2,1)}, bf16[2,4,128,192]{3,2,1,0:T(8,128)(2,1)}, u32[]{:S(2)}, u32[]{:S(2)}) collective-permute-start(bf16[2,4,128,192]{3,2,1,0:T(8,128)(2,1)} %pad_maximum_fusion.1.refs_0_), channel_id=1, source_target_pairs={{0,96},{16,112},{32,0},{48,16},{64,32},{80,48},{96,64},{112,80},{1... | collective-permute-start | bytes 1179656 | tf_op jit(solution)/shard_map/ppermute | solution.py:317
  152.2 36.3 %collective-permute-start.10 = (bf16[2,4,2,192,128]{4,3,1,2,0:T(8,128)(2,1)}, bf16[2,4,2,192,128]{4,3,1,2,0:T(8,128)(2,1)}, u32[]{:S(2)}, u32[]{:S(2)}) collective-permute-start(bf16[2,4,2,192,128]{4,3,1,2,0:T(8,128)(2,1)} %get-tuple-element.157), channel_id=1, source_target_pairs={{0,12},{1,13},{2,14},{3,15},{4,0},{5,1},{6,2},{7,3},{8,4},{9,5},{1... | collective-permute-start | bytes 2359304 | tf_op jit(solution)/shard_map/ppermute | solution.py:359
  155.1 36.8 %collective-permute-start.9 = (bf16[2,4,2,192,128]{4,3,1,2,0:T(8,128)(2,1)}, bf16[2,4,2,192,128]{4,3,1,2,0:T(8,128)(2,1)}, u32[]{:S(2)}, u32[]{:S(2)}) collective-permute-start(bf16[2,4,2,192,128]{4,3,1,2,0:T(8,128)(2,1)} %get-tuple-element.158), channel_id=1, source_target_pairs={{0,4},{1,5},{2,6},{3,7},{4,8},{5,9},{6,10},{7,11},{8,12},{9,13},{1... | collective-permute-start | bytes 2359304 | tf_op jit(solution)/shard_map/ppermute | solution.py:359
  155.1 71.1 %collective-permute-start.13 = (bf16[2,4,2,192,128]{4,3,1,2,0:T(8,128)(2,1)}, bf16[2,4,2,192,128]{4,3,1,2,0:T(8,128)(2,1)}, u32[]{:S(2)}, u32[]{:S(2)}) collective-permute-start(bf16[2,4,2,192,128]{4,3,1,2,0:T(8,128)(2,1)} %get-tuple-element.156), channel_id=1, source_target_pairs={{0,8},{1,9},{2,10},{3,11},{4,12},{5,13},{6,14},{7,15},{8,0},{9,1},... | collective-permute-start | bytes 2359304 | tf_op jit(solution)/shard_map/ppermute | solution.py:359
  181.6 158.8 %reduce-scatter.5.cloned.1.call-start = ((), (), s32[]{:S(2)}) async-start(), calls=%async_computation.3 | async-start | bytes 2654208 | tf_op jit(solution)/shard_map/reduce_scatter | solution.py:470
  195.5 29.8 %collective-permute-start.14 = (bf16[4,128,192]{2,1,0:T(8,128)(2,1)S(1)}, bf16[4,128,192]{2,1,0:T(8,128)(2,1)S(1)}, u32[]{:S(2)}, u32[]{:S(2)}) collective-permute-start(bf16[4,128,192]{2,1,0:T(8,128)(2,1)S(1)} %slice_bitcast_fusion.5), channel_id=1, source_target_pairs={{0,96},{16,112},{32,0},{48,16},{64,32},{80,48},{96,64},{112,80},{1... | collective-permute-start | bytes 589832 | tf_op jit(solution)/shard_map/ppermute | solution.py:317
  196.6 28.7 %collective-permute-start.15 = (bf16[4,128,192]{2,1,0:T(8,128)(2,1)S(1)}, bf16[4,128,192]{2,1,0:T(8,128)(2,1)S(1)}, u32[]{:S(2)}, u32[]{:S(2)}) collective-permute-start(bf16[4,128,192]{2,1,0:T(8,128)(2,1)S(1)} %slice_bitcast_fusion.4), channel_id=1, source_target_pairs={{0,32},{16,48},{32,64},{48,80},{64,96},{80,112},{96,0},{112,16},{1... | collective-permute-start | bytes 589832 | tf_op jit(solution)/shard_map/ppermute | solution.py:317
  277.2 36.9 %collective-permute-start.19 = (bf16[2,4,2,192,128]{4,3,2,1,0:T(8,128)(2,1)}, bf16[2,4,2,192,128]{4,3,2,1,0:T(8,128)(2,1)}, u32[]{:S(2)}, u32[]{:S(2)}) collective-permute-start(bf16[2,4,2,192,128]{4,3,2,1,0:T(8,128)(2,1)} %slice.281), channel_id=1, source_target_pairs={{0,4},{1,5},{2,6},{3,7},{4,8},{5,9},{6,10},{7,11},{8,12},{9,13},{1... | collective-permute-start | bytes 2359304 | tf_op jit(solution)/shard_map/ppermute | solution.py:359
  278.2 36.1 %collective-permute-start.23 = (bf16[2,4,2,192,128]{4,3,2,1,0:T(8,128)(2,1)}, bf16[2,4,2,192,128]{4,3,2,1,0:T(8,128)(2,1)}, u32[]{:S(2)}, u32[]{:S(2)}) collective-permute-start(bf16[2,4,2,192,128]{4,3,2,1,0:T(8,128)(2,1)} %slice.282), channel_id=1, source_target_pairs={{0,12},{1,13},{2,14},{3,15},{4,0},{5,1},{6,2},{7,3},{8,4},{9,5},{1... | collective-permute-start | bytes 2359304 | tf_op jit(solution)/shard_map/ppermute | solution.py:359
  289.0 25.4 %collective-permute-start.26 = (bf16[2,4,2,192,128]{4,3,2,1,0:T(8,128)(2,1)}, bf16[2,4,2,192,128]{4,3,2,1,0:T(8,128)(2,1)}, u32[]{:S(2)}, u32[]{:S(2)}) collective-permute-start(bf16[2,4,2,192,128]{4,3,2,1,0:T(8,128)(2,1)} %slice.285), channel_id=1, source_target_pairs={{0,8},{1,9},{2,10},{3,11},{4,12},{5,13},{6,14},{7,15},{8,0},{9,1},... | collective-permute-start | bytes 2359304 | tf_op jit(solution)/shard_map/ppermute | solution.py:359
  317.4 31.1 %collective-permute-start.31 = (bf16[8,2,384,128]{3,2,1,0:T(8,128)(2,1)}, bf16[8,2,384,128]{3,2,1,0:T(8,128)(2,1)S(1)}, u32[]{:S(2)}, u32[]{:S(2)}) collective-permute-start(bf16[8,2,384,128]{3,2,1,0:T(8,128)(2,1)} %get-tuple-element.155), channel_id=1, source_target_pairs={{0,1},{1,0},{2,3},{3,2},{4,5},{5,4},{6,7},{7,6},{8,9},{9,8},{10,11... | collective-permute-start | bytes 4718600 | tf_op jit(solution)/shard_map/ppermute | solution.py:347
  342.6 20.8 %collective-permute-start.28 = (bf16[2,2,384,128]{3,2,1,0:T(8,128)(2,1)S(1)}, bf16[2,2,384,128]{3,2,1,0:T(8,128)(2,1)S(1)}, u32[]{:S(2)}, u32[]{:S(2)}) collective-permute-start(bf16[2,2,384,128]{3,2,1,0:T(8,128)(2,1)S(1)} %get-tuple-element.159), channel_id=1, source_target_pairs={{0,4},{1,5},{2,6},{3,7},{4,8},{5,9},{6,10},{7,11},{8,12},{9,13},{1... | collective-permute-start | bytes 1179656 | tf_op jit(solution)/shard_map/ppermute | solution.py:359
  344.2 22.1 %collective-permute-start.29 = (bf16[2,2,384,128]{3,2,1,0:T(8,128)(2,1)S(1)}, bf16[2,2,384,128]{3,2,1,0:T(8,128)(2,1)S(1)}, u32[]{:S(2)}, u32[]{:S(2)}) collective-permute-start(bf16[2,2,384,128]{3,2,1,0:T(8,128)(2,1)S(1)} %get-tuple-element.161), channel_id=1, source_target_pairs={{0,12},{1,13},{2,14},{3,15},{4,0},{5,1},{6,2},{7,3},{8,4},{9,5},{1... | collective-permute-start | bytes 1179656 | tf_op jit(solution)/shard_map/ppermute | solution.py:359
  349.0 22.9 %collective-permute-start.32 = (bf16[2,2,384,128]{3,2,1,0:T(8,128)(2,1)S(1)}, bf16[2,2,384,128]{3,2,1,0:T(8,128)(2,1)S(1)}, u32[]{:S(2)}, u32[]{:S(2)}) collective-permute-start(bf16[2,2,384,128]{3,2,1,0:T(8,128)(2,1)S(1)} %get-tuple-element.162), channel_id=1, source_target_pairs={{0,4},{1,5},{2,6},{3,7},{4,8},{5,9},{6,10},{7,11},{8,12},{9,13},{1... | collective-permute-start | bytes 1179656 | tf_op jit(solution)/shard_map/ppermute | solution.py:359
  (41 other events, 497.1 us)
Sparse Core Ops, SparseCore 0:
  10.3 50.1 all-gather.4
  62.7 41.5 all-gather.6
  181.7 76.7 reduce-scatter.2
  262.7 77.6 reduce-scatter.4

commit v3 on v2

--- a/solution.py
+++ b/solution.py
@@ -23,8 +23,8 @@
 
 def attention_kernel(h0, heads, total_heads, first, last, tile, order_ref, cols_ref, *refs):
     q_ref, k_ref, v_ref, g_ref, do_ref, pc_ref, w_ref = refs[:7]
-    bias_refs = refs[7:11]
-    refs = refs[11:]
+    bias_refs = refs[7:15]
+    refs = refs[15:]
     head_start = h0 == 0
     if not first:
         acc_in, refs = refs[0], refs[1:]
@@ -64,7 +64,7 @@
         for h in range(heads):
             for s in range(8):
                 off = pl.multiple_of(order_ref[s] * kb, 128)
-                bias_s[h, :, pl.ds(off, kb)] = bias_refs[s // 2][s % 2, h].astype(F32) * math.sqrt(head)
+                bias_s[h, :, pl.ds(off, kb)] = bias_refs[s][0, h].astype(F32) * math.sqrt(head)
 
     def rows(ref, t):
         lo = t * tile
@@ -181,7 +181,7 @@
         def _():
             for h in range(heads):
                 for s in range(8):
-                    off = pl.multiple_of(s * kb, 128)
+                    off = pl.multiple_of((s if head_start else order_ref[s]) * kb, 128)
                     acc_out[s, h] = acc_s[h, :, pl.ds(off, kb)].astype(BF)
 
 
@@ -202,8 +202,10 @@
     k_spec = pl.BlockSpec((nb, 1, cj, chan), lambda i, *r: (0, i, 0, 0))
     v_spec = pl.BlockSpec((nb, 1, cj, chan), lambda i, *r: (0, ni + i, 0, 0))
     in_specs = [per_row, k_spec, v_spec, per_row, per_row, per_row, whole(chan, chan)]
-    in_specs += [whole(2, heads, cj, kb)] * 4
-    ops = [q, kv, kv, g, do, pc, w, *biases]
+    in_specs += [
+        pl.BlockSpec((1, heads, cj, kb), lambda i, *r, z=z: (z, 0, 0, 0), pipeline_mode=pl.Buffered(1)) for _, z in biases
+    ]
+    ops = [q, kv, kv, g, do, pc, w, *(block for block, _ in biases)]
     if not first:
         in_specs.append(pl.BlockSpec(memory_space=pl.ANY))
         ops.append(acc)
@@ -250,10 +252,10 @@
 
 
 def left_kernel(order_ref, cols_ref, *refs):
-    car = refs[:4]
-    r_ref, keep_ref, send_ref, l_s, o_s = refs[4:]
+    car = refs[:8]
+    r_ref, keep_ref, send_ref, l_s, o_s = refs[8:]
     step = pl.program_id(0)
-    _, ni, chan, cj = car[0].shape
+    ni, chan, cj = car[0].shape
     cb, _, kk = r_ref.shape
     rows = 8 * ni
     half = ni // 2
@@ -263,7 +265,7 @@
         for s in range(8):
             for i in range(ni):
                 at = pl.ds(pl.multiple_of((order_ref[s] * ni + i) * chan, chan), chan)
-                x = car[s // 2][s % 2, i].astype(F32)
+                x = car[s][i].astype(F32)
                 l_s[0, at, :] = x[:, :128]
                 l_s[1, at, : cj - 128] = x[:, 128:]
 
@@ -286,7 +288,7 @@
 
 
 def left_product(order, cols, cars, right_t, cb=16):
-    _, ni, chan, cj = cars[0].shape
+    ni, chan, cj = cars[0].shape
     kk = right_t.shape[2]
 
     def whole(*shape):
@@ -297,7 +299,7 @@
         grid_spec=pltpu.PrefetchScalarGridSpec(
             num_scalar_prefetch=2,
             grid=(chan // cb,),
-            in_specs=[whole(2, ni, chan, cj)] * 4 + [pl.BlockSpec((cb, cj, kk), lambda t, *r: (t, 0, 0))],
+            in_specs=[whole(ni, chan, cj)] * 8 + [pl.BlockSpec((cb, cj, kk), lambda t, *r: (t, 0, 0))],
             out_specs=[whole(8, ni // 2, kk, chan)] * 2,
             scratch_shapes=[
                 pltpu.VMEM((2, 8 * ni * chan, 128), F32),
@@ -321,22 +323,16 @@
     return lax.ppermute(x, "row", [(r, r ^ 1) for r in range(8)])
 
 
-def row_pair(x):
-    return jnp.stack([x, row_swap(x)])
-
-
-def row_gather(pair):
-    return [pair] + [row_shift(pair, dy) for dy in (1, 2, 3)]
-
-
-def row_sides(pair):
-    return [row_shift(pair, 1), row_shift(pair, 3)]
-
-
-def row_far(pair, side):
-    back, on = side
-    far = jnp.stack([row_shift(on[0], 3), row_shift(back[1], 1)])
-    return [pair, back, far, on]
+def row_shifts(x):
+    return [row_shift(x, dy) for dy in (1, 2, 3)]
+
+
+def row_order(own, swapped, own_shifts, swapped_shifts):
+    return [block for pair in zip([own] + own_shifts, [swapped] + swapped_shifts) for block in pair]
+
+
+def row_parts(x):
+    return [x[0:2]] + [row_shift(x[2 * dy : 2 * dy + 2], -dy) for dy in (1, 2, 3)]
 
 
 def add_all(parts):
@@ -349,10 +345,6 @@
 
 def add_pair(a, b):
     return (a.astype(F32) + b.astype(F32)).astype(BF)
-
-
-def core_sum(keep, send):
-    return add_pair(keep, core_swap(send))
 
 
 def x_shift(part, dx):
@@ -397,9 +389,15 @@
     penalty = big_penalty * (lax.dynamic_slice_in_dim(residue_mask, row * kb, kb).astype(F32) - 1.0)
     bias = (pair_bias.astype(F32) + penalty[None, None, :]).astype(BF)
     hs = total_heads // 2
-    pairs = row_pair(bias)
-    biases = [row_gather(pairs[:, :hs]), row_gather(pairs[:, hs:])]
-    right_t = jnp.transpose(right_proj, (2, 0, 1))
+    bias_swap = row_swap(bias)
+    first_shifts = row_shifts(bias[:hs])
+    right_t = jnp.transpose(after(right_proj, bias_swap), (2, 0, 1))
+    early = row_order(bias[:hs], bias_swap[:hs], first_shifts, row_shifts(bias_swap[:hs]))
+    late = after(jnp.stack([bias[hs:], bias_swap[hs:]]), early)
+    biases = [
+        [(block[None], 0) for block in early],
+        [(pair, z) for pair in [late] + row_shifts(late) for z in range(2)],
+    ]
 
     quarter = rb // 4
     picks = [
@@ -426,55 +424,53 @@
     a = attend(0, 0, None, None, order)
     b = attend(0, 1, None, list(a[:4]), order)
     gq0, gg0, keep, send, car0 = b[:5]
-    part0 = core_sum(keep, send)
-    pair0 = row_pair(car0)
-    order_c, part0, pair0 = lax.optimization_barrier((order, part0, pair0))
+    got0, swap0, own0 = core_swap(send), row_swap(car0), row_shifts(car0)
+    c = attend(1, 0, a[-1], None, after(order, gq0))
+    got0, swap0, own0 = after((got0, swap0, own0), c[0])
+    part0 = add_pair(keep, got0)
+    part0, swap0 = lax.optimization_barrier((part0, swap0))
     near0 = [x_shift(part0, 1), x_shift(part0, 3)]
-    side0 = row_sides(pair0)
-    c = attend(1, 0, a[-1], None, order_c)
-    near0, side0 = after((near0, side0), c[0])
+    swapped0 = row_shifts(swap0)
+    d = attend(1, 1, b[-1], list(c[:4]), after(order, part0, c[0]))
+    gq1, gg1, keep, send, car1 = d[:5]
+    near0, swapped0 = after((near0, swapped0), gq1)
     total0 = add_all([part0[0:2]] + near0)
-    order_d, total0, side0 = lax.optimization_barrier((order, total0, side0))
+    order_l, car1, send = lax.optimization_barrier((order, car1, send))
     far0 = x_shift(part0, 2)
-    cars0 = row_far(pair0, side0)
-    d = attend(1, 1, b[-1], list(c[:4]), order_d)
-    gq1, gg1, keep, send, car1 = d[:5]
-    far0, cars0 = after((far0, cars0), gq1)
+    swap1, own1, got1 = row_swap(car1), row_shifts(car1), core_swap(send)
+    left0 = left_product(order_l, cols, row_order(car0, swap0, own0, swapped0), right_t)
+    far0, swap1, own1, got1, left0 = lax.optimization_barrier((far0, swap1, own1, got1, left0))
+    part1 = add_pair(keep, got1)
+    swapped1 = row_shifts(swap1)
     total0 = add_all([total0, far0])
-    order_l, total0, cars0, car1, send = lax.optimization_barrier((order, total0, cars0, car1, send))
-    swap1 = row_swap(car1)
-    got1 = core_swap(send)
-    got_z0 = z_swap(total0)
-    left0 = left_product(order_l, cols, cars0, right_t)
-    swap1, got1, got_z0, left0 = lax.optimization_barrier((swap1, got1, got_z0, left0))
+    part1, total0 = lax.optimization_barrier((part1, total0))
+    near1 = [x_shift(part1, 1), x_shift(part1, 3)]
+    got_l0 = core_swap(left0[1])
+    swapped1, got_l0, total0, part1, bias1 = lax.optimization_barrier((swapped1, got_l0, total0, part1, d[-1]))
+    bias1 = row_parts(bias1)
+    part_l0 = add_pair(left0[0], got_l0)
+    far1, got_z0 = x_shift(part1, 2), z_swap(total0)
+    left1 = left_product(after(order, swapped1, near1), cols, row_order(car1, swap1, own1, swapped1), right_t)
+    far1, got_z0, bias1 = after((far1, got_z0, bias1), left1)
+    part_l0, left1 = lax.optimization_barrier((part_l0, left1))
     dkv0 = add_pair(total0[0], got_z0)
-    part1 = add_pair(keep, got1)
-    pair1 = jnp.stack([car1, swap1])
-    pair1, part1, left0 = lax.optimization_barrier((pair1, part1, left0))
-    side1 = row_sides(pair1)
-    got_l0 = core_swap(left0[1])
-    near1 = [x_shift(part1, 1)]
-    side1, got_l0 = lax.optimization_barrier((side1, got_l0))
-    cars1 = row_far(pair1, side1)
-    near1.append(x_shift(after(part1, got_l0), 3))
-    far1 = x_shift(after(part1, cars1), 2)
-    left1 = left_product(after(order, cars1), cols, cars1, right_t)
-    near1, far1 = after((near1, far1), left1)
-    part_l0 = add_pair(left0[0], after(got_l0, left1))
-    total1 = add_all([part1[0:2], near1[0], near1[1], far1])
-    total1, part_l0, left1 = lax.optimization_barrier((total1, part_l0, left1))
-    dkv1 = z_sum(total1)
-    part_l1 = core_sum(*left1)
-    sums = [add_all([p[0:2], x_shift(p, 1), x_shift(p, 3), x_shift(p, 2)]) for p in (part_l0, part_l1)]
-    left = z_sum(jnp.concatenate(sums, axis=1))
-    bias_sum = [lax.psum_scatter(t[-1], "row", scatter_dimension=0).astype(F32) for t in (c, d)]
+    got_l1 = core_swap(left1[1])
+    sum_l0 = add_all([part_l0[0:2]] + [x_shift(part_l0, dx) for dx in (1, 3, 2)])
+    dkv1 = z_sum(add_all([part1[0:2], far1] + near1))
+    part_l1 = add_pair(left1[0], got_l1)
+    bias1 = add_all(bias1)
+    bias_z = row_swap(bias1[1])
+    sum_l1 = add_all([part_l1[0:2]] + [x_shift(part_l1, dx) for dx in (1, 3, 2)])
+    left = z_sum(jnp.concatenate([sum_l0, sum_l1], axis=1))
+    bias0 = after(lax.psum_scatter(c[-1], "row", scatter_dimension=0), left)
+    grad_bias = jnp.concatenate([bias0.astype(F32), bias1[0].astype(F32) + bias_z.astype(F32)])
 
     def untake(a, b):
         return jnp.concatenate([a[:quarter], b[:quarter], a[quarter:], b[quarter:]])
 
     gq, gg = untake(gq0, gq1), untake(gg0, gg1)
     dk, dv = untake(dkv0[:, 0], dkv1[:, 0]), untake(dkv0[:, 1], dkv1[:, 1])
-    return (gq, dk, dv, gg, jnp.concatenate(bias_sum), left)
+    return (gq, dk, dv, gg, grad_bias, left)
 
 
 def solution(mesh):

time: 401 us -> 383 us (0.955)
  waiting for transfers between devices: 119 us -> 81.7 us
  starting transfers between devices: 53.1 us -> 71.3 us
    optimization_barrier x0 -> x1, local copies, waits for them, and re-layouts: none -> 24.6 us  [after(): return lax.optimization_barrier((x, done))[0]]
    reduce_scatter x2 -> x1, waiting for transfers between devices: 21.2 us -> 0.01 us  [local(): bias0 = after(lax.psum_scatter(c[-1], 'row', scatter_dimension=0), left)]
    unnamed x51 -> x66, local copies, waits for them, and re-layouts: 27.7 us -> 8.13 us
    ppermute x14 -> x24, waiting for transfers between devices: 40.7 us -> 25.3 us  [row_shift(): lax.ppermute(x, 'row', [(2 * y + z, 2 * ((y + dy) % 4) + z) for y in rang...]
    ppermute x12, waiting for transfers between devices: 42.1 us -> 28.1 us  [x_shift(): lax.ppermute(part[2 * dx:2 * dx + 2], 'col', [(c, (c + 4 * dx) % 16) for...]
    ppermute x14 -> x24, starting transfers between devices: 28 us -> 37.5 us  [row_shift(): lax.ppermute(x, 'row', [(2 * y + z, 2 * ((y + dy) % 4) + z) for y in rang...]
    ppermute x3 -> x4, starting transfers between devices: 6.01 us -> 13.3 us  [row_swap(): return lax.ppermute(x, 'row', [(r, r ^ 1) for r in range(8)])]
    ppermute x3, waiting for transfers between devices: 6.46 us -> 13.3 us  [z_swap(): return lax.ppermute(total[1], 'col', [(c, c ^ 2) for c in range(16)])]
  transfers between devices with their start and end apart: 40 -> 50, of which waited for: 17 -> 12; matrix products, arithmetic and copies ran while one was open for 18% -> 16% of each run, Pallas kernels for 34% -> 35%
where the time goes in v3:
time: 383 us; the launch traced here: 378 us
  Pallas kernels  133 us (35%)
  waiting for transfers between devices  81.7 us (21%)
  starting transfers between devices  71.3 us (19%)
  local copies, waits for them, and re-layouts  45.8 us (12%)
  other arithmetic  30.8 us (8%)
  between operations  14.9 us (4%)
    pallas_call x4, Pallas kernels, attention(): pl.pallas_call(functools.partial(attention_kernel, h0, heads, total_heads...  99.6 us
    ppermute x24, starting transfers between devices, row_shift(): lax.ppermute(x, 'row', [(2 * y + z, 2 * ((y + dy) % 4) + z) for y in rang...  37.5 us
    pallas_call x2, Pallas kernels, left_product(): pl.pallas_call(left_kernel, grid_spec=pltpu.PrefetchScalarGridSpec(num_sc...  33.8 us
    ppermute x12, waiting for transfers between devices, x_shift(): lax.ppermute(part[2 * dx:2 * dx + 2], 'col', [(c, (c + 4 * dx) % 16) for...  28.1 us
    ppermute x24, waiting for transfers between devices, row_shift(): lax.ppermute(x, 'row', [(2 * y + z, 2 * ((y + dy) % 4) + z) for y in rang...  25.3 us
    optimization_barrier x1, local copies, waits for them, and re-layouts, after(): return lax.optimization_barrier((x, done))[0]  24.6 us
    ppermute x12, starting transfers between devices, x_shift(): lax.ppermute(part[2 * dx:2 * dx + 2], 'col', [(c, (c + 4 * dx) % 16) for...  18.3 us
    ppermute x4, waiting for transfers between devices, row_swap(): return lax.ppermute(x, 'row', [(r, r ^ 1) for r in range(8)])  14.9 us
  transfers between devices with their start and end apart: 50, of which 12 were waited for; matrix products, arithmetic and copies ran while one was open for 16% of the time, Pallas kernels for 35%

profile of v3, /device:TPU:0, one launch (start us, length us, event | category | flops | bytes accessed | tf_op | source)
XLA Modules:
  0.0 378.0 jit_solution(7092654620597533357)
XLA Ops:
  11.2 4.0 %collective-permute-start = (bf16[4,192,384]{2,1,0:T(8,128)(2,1)S(1)}, bf16[4,192,384]{2,1,0:T(8,128)(2,1)S(1)}, u32[]{:S(2)}, u32[]{:S(2)}) collective-permute-start(bf16[4,192,384]{2,1,0:T(8,128)(2,1)S(1)} %add_convert_fusion.8), channel_id=1, source_target_pairs={{0,16},{16,0},{32,48},{48,32},{64,80},{80,64},{96,112},{112,96},{1... | collective-permute-start | bytes 1769480 | tf_op jit(solution)/shard_map/ppermute | solution.py:323
  23.4 11.7 %collective-permute-done = bf16[4,192,384]{2,1,0:T(8,128)(2,1)S(1)} collective-permute-done((bf16[4,192,384]{2,1,0:T(8,128)(2,1)S(1)}, bf16[4,192,384]{2,1,0:T(8,128)(2,1)S(1)}, u32[]{:S(2)}, u32[]{:S(2)}) %collective-permute-start) | collective-permute-done | bytes 589856 | tf_op jit(solution)/shard_map/ppermute | solution.py:323
  44.5 24.6 %copy.22 = bf16[192,384,128]{1,0,2:T(8,128)(2,1)} copy(bf16[192,384,128]{2,1,0:T(8,128)(2,1)} %param.19) | data formatting | bytes 37748736 | tf_op jit(solution)/shard_map/optimization_barrier | solution.py:363
  74.6 23.5 %attention_rows.4 = (bf16[4,192,128]{2,1,0:T(8,128)(2,1)}, bf16[4,192,128]{2,1,0:T(8,128)(2,1)}, bf16[4,64,3072]{2,1,0:T(8,128)(2,1)}, bf16[4,64,3072]{2,1,0:T(8,128)(2,1)}, f32[2,192,3072]{2,1,0:T(8,128)}) custom-call(s32[8]{0:T(128)} %stack.95.order_ref, s32[16]{0:T(128)} %stack.112.cols_ref, bf16[4,192,128]{2,1,0:T(8,128)(2,1)} %get-tuple-element.221.refs_0_, ...), custom_call_target="tpu_custom_call" | custom-call | flops 9663676416 | bytes 30000000 | tf_op jit(solution)/shard_map/attention_rows/pallas_call | solution.py:240
  99.3 25.6 %attention_rows.5 = (bf16[4,192,128]{2,1,0:T(8,128)(2,1)}, bf16[4,192,128]{2,1,0:T(8,128)(2,1)}, bf16[8,4,2,192,128]{4,3,2,1,0:T(8,128)(2,1)}, bf16[8,4,2,192,12...) custom-call(s32[8]{0:T(128)} %stack.95.order_ref, s32[16]{0:T(128)} %stack.112.cols_ref, ...), custom_call_target="tpu_custom_call" | custom-call | flops 9663676416 | bytes 30000000 | tf_op jit(solution)/shard_map/attention_rows/pallas_call | solution.py:240
  128.9 3.9 %collective-permute-start.11 = (bf16[4,128,192]{2,1,0:T(8,128)(2,1)}, bf16[4,128,192]{2,1,0:T(8,128)(2,1)S(1)}, u32[]{:S(2)}, u32[]{:S(2)}) collective-permute-start(bf16[4,128,192]{2,1,0:T(8,128)(2,1)} %get-tuple-element.91.refs_0_), channel_id=1, source_target_pairs={{0,16},{16,0},{32,48},{48,32},{64,80},{80,64},{96,112},{112,96},{1... | collective-permute-start | bytes 589832 | tf_op jit(solution)/shard_map/ppermute | solution.py:323
  137.6 24.2 %attention_rows.6 = (bf16[4,192,128]{2,1,0:T(8,128)(2,1)}, bf16[4,192,128]{2,1,0:T(8,128)(2,1)}, bf16[4,64,3072]{2,1,0:T(8,128)(2,1)}, bf16[4,64,3072]{2,1,0:T(8,128)(2,1)}, bf16[8,2,192,384]{3,2,1,0:T(8,128)(2,1)}) custom-call(s32[8]{0:T(128)} %stack.95.order_ref, s32[16]{0:T(128)} %stack.112.cols_ref, bf16[4,192,128]{2,1,0:T(8,128)(2,1)} %get-tuple-element.225.refs_0_, ...), custom_call_target="tpu_custom_call" | custom-call | flops 9663676416 | bytes 30000000 | tf_op jit(solution)/shard_map/attention_rows/pallas_call | solution.py:240
  162.6 4.0 %add_convert_fusion.1 = bf16[8,4,2,192,128]{4,3,1,2,0:T(8,128)(2,1)S(1)} fusion(bf16[8,4,2,192,128]{4,3,1,2,0:T(8,128)(2,1)} %collective-permute-done.10, bf16[8,4,2,192,128]{4,3,2,1,0:T(8,128)(2,1)} %get-tuple-element.89), kind=kLoop, calls=%fused_computation.1 | loop fusion | flops 6291456 | bytes 9437184 | tf_op jit(solution)/shard_map/convert_element_type | solution.py:347
  172.5 3.4 collective-permute-start.22
  175.9 26.3 %attention_rows.7 = (bf16[4,192,128]{2,1,0:T(8,128)(2,1)}, bf16[4,192,128]{2,1,0:T(8,128)(2,1)}, bf16[8,4,2,192,128]{4,3,2,1,0:T(8,128)(2,1)}, bf16[8,4,2,192,12...) custom-call(s32[8]{0:T(128)} %stack.95.order_ref, s32[16]{0:T(128)} %stack.112.cols_ref, ...), custom_call_target="tpu_custom_call" | custom-call | flops 9663676416 | bytes 30000000 | tf_op jit(solution)/shard_map/attention_rows/pallas_call | solution.py:240
  207.2 3.2 collective-permute-done.16.refs_1_
  212.3 16.9 %left_product.2 = (bf16[8,2,384,128]{3,2,1,0:T(8,128)(2,1)}, bf16[8,2,384,128]{3,2,1,0:T(8,128)(2,1)}) custom-call(s32[8]{0:T(128)} %stack.95.order_ref, s32[16]{0:T(128)} %stack.112.cols_ref, bf16[4,128,192]{2,1,0:T(8,128)(2,1)} %get-tuple-element.91.refs_0_, bf16[4,128,192]{2,1,0:T(8,128)(2,1)} %copy-done.28, ...), custom_call_target="tpu_custom_call" | custom-call | flops 40000000000 | bytes 30000000 | tf_op jit(solution)/shard_map/left_product/pallas_call | solution.py:297
  231.1 4.2 %add_convert_fusion = bf16[8,4,2,192,128]{4,3,2,1,0:T(8,128)(2,1)S(1)} fusion(bf16[8,4,2,192,128]{4,3,2,1,0:T(8,128)(2,1)} %copy-done.1, bf16[8,4,2,192,128]{4,3,2,1,0:T(8,128)(2,1)} %get-tuple-element.121), kind=kLoop, calls=%fused_computation | loop fusion | flops 6291456 | bytes 9437184 | tf_op jit(solution)/shard_map/convert_element_type | solution.py:347
  246.6 11.8 %collective-permute-done.26.refs_3_ = bf16[4,128,192]{2,1,0:T(8,128)(2,1)S(1)} collective-permute-done((bf16[4,128,192]{2,1,0:T(8,128)(2,1)}, bf16[4,128,192]{2,1,0:T(8,128)(2,1)S(1)}, u32[]{:S(2)}, u32[]{:S(2)}) %collective-permute-start.26) | collective-permute-done | bytes 196640 | tf_op jit(solution)/shard_map/ppermute | solution.py:319
  260.1 7.0 %collective-permute-done.28.refs_7_ = bf16[4,128,192]{2,1,0:T(8,128)(2,1)} collective-permute-done((bf16[4,128,192]{2,1,0:T(8,128)(2,1)}, bf16[4,128,192]{2,1,0:T(8,128)(2,1)}, u32[]{:S(2)}, u32[]{:S(2)}) %collective-permute-start.28) | collective-permute-done | bytes 196640 | tf_op jit(solution)/shard_map/ppermute | solution.py:319
  267.1 3.5 add_convert_fusion.3
  270.5 17.0 %left_product.3 = (bf16[8,2,384,128]{3,2,1,0:T(8,128)(2,1)}, bf16[8,2,384,128]{3,2,1,0:T(8,128)(2,1)}) custom-call(s32[8]{0:T(128)} %stack.95.order_ref, s32[16]{0:T(128)} %stack.112.cols_ref, bf16[4,128,192]{2,1,0:T(8,128)(2,1)} %get-tuple-element.106.refs_0_, bf16[4,128,192]{2,1,0:T(8,128)(2,1)} %copy-done.27, ...), custom_call_target="tpu_custom_call" | custom-call | flops 40000000000 | bytes 30000000 | tf_op jit(solution)/shard_map/left_product/pallas_call | solution.py:297
  293.0 3.6 collective-permute-start.30
  298.9 19.5 %collective-permute-done.38 = bf16[2,2,384,128]{3,2,1,0:T(8,128)(2,1)S(1)} collective-permute-done((bf16[2,2,384,128]{3,2,1,0:T(8,128)(2,1)S(1)}, bf16[2,2,384,128]{3,2,1,0:T(8,128)(2,1)S(1)}, u32[]{:S(2)}, u32[]{:S(2)}) %collective-permute-start.38) | collective-permute-done | bytes 393248 | tf_op jit(solution)/shard_map/ppermute | solution.py:351
  324.5 5.2 %collective-permute-done.31 = bf16[4,2,192,128]{3,2,0,1:T(8,128)(2,1)S(1)} collective-permute-done((bf16[4,2,192,128]{3,2,0,1:T(8,128)(2,1)S(1)}, bf16[4,2,192,128]{3,2,0,1:T(8,128)(2,1)S(1)}, u32[]{:S(2)}, u32[]{:S(2)}) %collective-permute-start.31) | collective-permute-done | bytes 393248 | tf_op jit(solution)/shard_map/ppermute | solution.py:355
  329.9 6.2 %collective-permute-done.34 = bf16[2,2,192,384]{3,2,1,0:T(8,128)(2,1)S(1)} collective-permute-done((bf16[2,2,192,384]{3,2,1,0:T(8,128)(2,1)S(1)}, bf16[2,2,192,384]{3,2,1,0:T(8,128)(2,1)S(1)}, u32[]{:S(2)}, u32[]{:S(2)}) %collective-permute-start.34) | collective-permute-done | bytes 589856 | tf_op jit(solution)/shard_map/ppermute | solution.py:319
  336.4 5.3 %collective-permute-start.46 = (bf16[2,192,384]{2,1,0:T(8,128)(2,1)S(1)}, bf16[2,192,384]{2,1,0:T(8,128)(2,1)S(1)}, u32[]{:S(2)}, u32[]{:S(2)}) collective-permute-start(bf16[2,192,384]{2,1,0:T(8,128)(2,1)S(1)} %slice_bitcast_fusion.3), channel_id=1, source_target_pairs={{0,16},{16,0},{32,48},{48,32},{64,80},{80,64},{96,112},{112,96},{1... | collective-permute-start | bytes 884744 | tf_op jit(solution)/shard_map/ppermute | solution.py:323
  351.6 8.4 %collective-permute-done.42 = bf16[2,2,384,128]{3,2,1,0:T(8,128)(2,1)S(1)} collective-permute-done((bf16[2,2,384,128]{3,2,1,0:T(8,128)(2,1)S(1)}, bf16[2,2,384,128]{3,2,1,0:T(8,128)(2,1)S(1)}, u32[]{:S(2)}, u32[]{:S(2)}) %collective-permute-start.42) | collective-permute-done | bytes 393248 | tf_op jit(solution)/shard_map/ppermute | solution.py:351
  362.6 5.5 %collective-permute-done.45 = bf16[4,384,128]{2,1,0:T(8,128)(2,1)S(1)} collective-permute-done((bf16[4,384,128]{2,1,0:T(8,128)(2,1)S(1)}, bf16[4,384,128]{2,1,0:T(8,128)(2,1)S(1)}, u32[]{:S(2)}, u32[]{:S(2)}) %collective-permute-start.45) | collective-permute-done | bytes 393248 | tf_op jit(solution)/shard_map/ppermute | solution.py:355
  (206 shorter events, 94.6 us)
Async XLA Ops:
  7.2 67.5 %all-gather.5.cloned.1.call-start = ((), (), s32[]{:S(2)}) async-start(), calls=%async_computation.2 | async-start | bytes 6684672 | tf_op jit(solution)/shard_map/all_gather | solution.py:412
  9.3 128.3 %all-gather.7.cloned.1.call-start = ((), (), s32[]{:S(2)}) async-start(), calls=%async_computation.3 | async-start | bytes 6684672 | tf_op jit(solution)/shard_map/all_gather | solution.py:412
  10.2 358.8 %reduce-scatter.2.cloned.1.call-start = ((), (), s32[]{:S(2)}) async-start(), calls=%async_computation.1 | async-start | bytes 2654208 | tf_op jit(solution)/shard_map/reduce_scatter | solution.py:465
  17.6 51.5 %collective-permute-start.3 = (bf16[2,192,384]{2,1,0:T(8,128)(2,1)S(1)}, bf16[2,192,384]{2,1,0:T(8,128)(2,1)}, u32[]{:S(2)}, u32[]{:S(2)}) collective-permute-start(bf16[2,192,384]{2,1,0:T(8,128)(2,1)S(1)} %get-tuple-element.175), channel_id=1, source_target_pairs={{0,64},{16,80},{32,96},{48,112},{64,0},{80,16},{96,32},{112,48},{1... | collective-permute-start | bytes 884744 | tf_op jit(solution)/shard_map/ppermute | solution.py:319
  20.5 48.6 %collective-permute-start.5 = (bf16[2,192,384]{2,1,0:T(8,128)(2,1)S(1)}, bf16[2,192,384]{2,1,0:T(8,128)(2,1)}, u32[]{:S(2)}, u32[]{:S(2)}) collective-permute-start(bf16[2,192,384]{2,1,0:T(8,128)(2,1)S(1)} %get-tuple-element.175), channel_id=1, source_target_pairs={{0,96},{16,112},{32,0},{48,16},{64,32},{80,48},{96,64},{112,80},{1... | collective-permute-start | bytes 884744 | tf_op jit(solution)/shard_map/ppermute | solution.py:319
  35.9 33.3 %collective-permute-start.2 = (bf16[2,192,384]{2,1,0:T(8,128)(2,1)S(1)}, bf16[2,192,384]{2,1,0:T(8,128)(2,1)S(1)}, u32[]{:S(2)}, u32[]{:S(2)}) collective-permute-start(bf16[2,192,384]{2,1,0:T(8,128)(2,1)S(1)} %get-tuple-element.172), channel_id=1, source_target_pairs={{0,32},{16,48},{32,64},{48,80},{64,96},{80,112},{96,0},{112,16},{1... | collective-permute-start | bytes 884744 | tf_op jit(solution)/shard_map/ppermute | solution.py:319
  37.3 31.9 %collective-permute-start.4 = (bf16[2,192,384]{2,1,0:T(8,128)(2,1)S(1)}, bf16[2,192,384]{2,1,0:T(8,128)(2,1)S(1)}, u32[]{:S(2)}, u32[]{:S(2)}) collective-permute-start(bf16[2,192,384]{2,1,0:T(8,128)(2,1)S(1)} %get-tuple-element.172), channel_id=1, source_target_pairs={{0,64},{16,80},{32,96},{48,112},{64,0},{80,16},{96,32},{112,48},{1... | collective-permute-start | bytes 884744 | tf_op jit(solution)/shard_map/ppermute | solution.py:319
  40.3 28.8 %collective-permute-start.6 = (bf16[2,192,384]{2,1,0:T(8,128)(2,1)S(1)}, bf16[2,192,384]{2,1,0:T(8,128)(2,1)S(1)}, u32[]{:S(2)}, u32[]{:S(2)}) collective-permute-start(bf16[2,192,384]{2,1,0:T(8,128)(2,1)S(1)} %get-tuple-element.172), channel_id=1, source_target_pairs={{0,96},{16,112},{32,0},{48,16},{64,32},{80,48},{96,64},{112,80},{1... | collective-permute-start | bytes 884744 | tf_op jit(solution)/shard_map/ppermute | solution.py:319
  70.0 28.1 %collective-permute-start.7 = (bf16[2,2,192,384]{3,2,1,0:T(8,128)(2,1)S(1)}, bf16[2,2,192,384]{3,2,1,0:T(8,128)(2,1)S(1)}, u32[]{:S(2)}, u32[]{:S(2)}) collective-permute-start(bf16[2,2,192,384]{3,2,1,0:T(8,128)(2,1)S(1)} %pad_maximum_fusion.1.refs_7_.refs_8_), channel_id=1, source_target_pairs={{0,32},{16,48},{32,64},{48,80},{64,96},{80,112},{96,0},{112,16},{1... | collective-permute-start | bytes 1769480 | tf_op jit(solution)/shard_map/ppermute | solution.py:319
  127.2 34.7 %collective-permute-start.10 = (bf16[8,4,2,192,128]{4,3,1,2,0:T(8,128)(2,1)S(1)}, bf16[8,4,2,192,128]{4,3,1,2,0:T(8,128)(2,1)}, u32[]{:S(2)}, u32[]{:S(2)}) collective-permute-start(bf16[8,4,2,192,128]{4,3,1,2,0:T(8,128)(2,1)S(1)} %copy.24), channel_id=1, source_target_pairs={{0,1},{1,0},{2,3},{3,2},{4,5},{5,4},{6,7},{7,6},{8,9},{9,8},{10,11... | collective-permute-start | bytes 9437192 | tf_op jit(solution)/shard_map/ppermute | solution.py:343
  128.9 32.9 %collective-permute-start.11 = (bf16[4,128,192]{2,1,0:T(8,128)(2,1)}, bf16[4,128,192]{2,1,0:T(8,128)(2,1)S(1)}, u32[]{:S(2)}, u32[]{:S(2)}) collective-permute-start(bf16[4,128,192]{2,1,0:T(8,128)(2,1)} %get-tuple-element.91.refs_0_), channel_id=1, source_target_pairs={{0,16},{16,0},{32,48},{48,32},{64,80},{80,64},{96,112},{112,96},{1... | collective-permute-start | bytes 589832 | tf_op jit(solution)/shard_map/ppermute | solution.py:323
  132.8 29.1 %collective-permute-start.12 = (bf16[4,128,192]{2,1,0:T(8,128)(2,1)}, bf16[4,128,192]{2,1,0:T(8,128)(2,1)}, u32[]{:S(2)}, u32[]{:S(2)}) collective-permute-start(bf16[4,128,192]{2,1,0:T(8,128)(2,1)} %get-tuple-element.91.refs_0_), channel_id=1, source_target_pairs={{0,32},{16,48},{32,64},{48,80},{64,96},{80,112},{96,0},{112,16},{1... | collective-permute-start | bytes 589832 | tf_op jit(solution)/shard_map/ppermute | solution.py:319
  132.9 29.0 %collective-permute-start.13 = (bf16[4,128,192]{2,1,0:T(8,128)(2,1)}, bf16[4,128,192]{2,1,0:T(8,128)(2,1)}, u32[]{:S(2)}, u32[]{:S(2)}) collective-permute-start(bf16[4,128,192]{2,1,0:T(8,128)(2,1)} %get-tuple-element.91.refs_0_), channel_id=1, source_target_pairs={{0,64},{16,80},{32,96},{48,112},{64,0},{80,16},{96,32},{112,48},{1... | collective-permute-start | bytes 589832 | tf_op jit(solution)/shard_map/ppermute | solution.py:319
  168.3 33.9 %collective-permute-start.23 = (bf16[4,128,192]{2,1,0:T(8,128)(2,1)S(1)}, bf16[4,128,192]{2,1,0:T(8,128)(2,1)S(1)}, u32[]{:S(2)}, u32[]{:S(2)}) collective-permute-start(bf16[4,128,192]{2,1,0:T(8,128)(2,1)S(1)} %copy-done.29), channel_id=1, source_target_pairs={{0,32},{16,48},{32,64},{48,80},{64,96},{80,112},{96,0},{112,16},{1... | collective-permute-start | bytes 589832 | tf_op jit(solution)/shard_map/ppermute | solution.py:319
  168.3 34.0 %collective-permute-start.24 = (bf16[4,128,192]{2,1,0:T(8,128)(2,1)S(1)}, bf16[4,128,192]{2,1,0:T(8,128)(2,1)S(1)}, u32[]{:S(2)}, u32[]{:S(2)}) collective-permute-start(bf16[4,128,192]{2,1,0:T(8,128)(2,1)S(1)} %copy-done.29), channel_id=1, source_target_pairs={{0,64},{16,80},{32,96},{48,112},{64,0},{80,16},{96,32},{112,48},{1... | collective-permute-start | bytes 589832 | tf_op jit(solution)/shard_map/ppermute | solution.py:319
  169.8 32.6 %collective-permute-start.25 = (bf16[4,128,192]{2,1,0:T(8,128)(2,1)S(1)}, bf16[4,128,192]{2,1,0:T(8,128)(2,1)}, u32[]{:S(2)}, u32[]{:S(2)}) collective-permute-start(bf16[4,128,192]{2,1,0:T(8,128)(2,1)S(1)} %copy-done.29), channel_id=1, source_target_pairs={{0,96},{16,112},{32,0},{48,16},{64,32},{80,48},{96,64},{112,80},{1... | collective-permute-start | bytes 589832 | tf_op jit(solution)/shard_map/ppermute | solution.py:319
  172.5 32.1 %collective-permute-start.21 = (bf16[2,4,2,192,128]{4,3,1,2,0:T(8,128)(2,1)S(1)}, bf16[2,4,2,192,128]{4,3,1,2,0:T(8,128)(2,1)S(1)}, u32[]{:S(2)}, u32[]{:S(2)}) collective-permute-start(bf16[2,4,2,192,128]{4,3,1,2,0:T(8,128)(2,1)S(1)} %get-tuple-element.159), channel_id=1, source_target_pairs={{0,4},{1,5},{2,6},{3,7},{4,8},{5,9},{6,10},{7,11},{8,12},{9,13},{1... | collective-permute-start | bytes 2359304 | tf_op jit(solution)/shard_map/ppermute | solution.py:351
  172.5 34.6 %collective-permute-start.22 = (bf16[2,4,2,192,128]{4,3,1,2,0:T(8,128)(2,1)S(1)}, bf16[2,4,2,192,128]{4,3,1,2,0:T(8,128)(2,1)}, u32[]{:S(2)}, u32[]{:S(2)}) collective-permute-start(bf16[2,4,2,192,128]{4,3,1,2,0:T(8,128)(2,1)S(1)} %get-tuple-element.158), channel_id=1, source_target_pairs={{0,12},{1,13},{2,14},{3,15},{4,0},{5,1},{6,2},{7,3},{8,4},{9,5},{1... | collective-permute-start | bytes 2359304 | tf_op jit(solution)/shard_map/ppermute | solution.py:351
  229.5 37.6 %collective-permute-start.29 = (bf16[8,2,384,128]{3,2,1,0:T(8,128)(2,1)}, bf16[8,2,384,128]{3,2,1,0:T(8,128)(2,1)}, u32[]{:S(2)}, u32[]{:S(2)}) collective-permute-start(bf16[8,2,384,128]{3,2,1,0:T(8,128)(2,1)} %get-tuple-element.120), channel_id=1, source_target_pairs={{0,1},{1,0},{2,3},{3,2},{4,5},{5,4},{6,7},{7,6},{8,9},{9,8},{10,11... | collective-permute-start | bytes 4718600 | tf_op jit(solution)/shard_map/ppermute | solution.py:343
  288.8 29.5 %collective-permute-start.38 = (bf16[2,2,384,128]{3,2,1,0:T(8,128)(2,1)S(1)}, bf16[2,2,384,128]{3,2,1,0:T(8,128)(2,1)S(1)}, u32[]{:S(2)}, u32[]{:S(2)}) collective-permute-start(bf16[2,2,384,128]{3,2,1,0:T(8,128)(2,1)S(1)} %get-tuple-element.165), channel_id=1, source_target_pairs={{0,4},{1,5},{2,6},{3,7},{4,8},{5,9},{6,10},{7,11},{8,12},{9,13},{1... | collective-permute-start | bytes 1179656 | tf_op jit(solution)/shard_map/ppermute | solution.py:351
  288.9 31.7 %collective-permute-start.39 = (bf16[2,2,384,128]{3,2,1,0:T(8,128)(2,1)S(1)}, bf16[2,2,384,128]{3,2,1,0:T(8,128)(2,1)S(1)}, u32[]{:S(2)}, u32[]{:S(2)}) collective-permute-start(bf16[2,2,384,128]{3,2,1,0:T(8,128)(2,1)S(1)} %get-tuple-element.167), channel_id=1, source_target_pairs={{0,12},{1,13},{2,14},{3,15},{4,0},{5,1},{6,2},{7,3},{8,4},{9,5},{1... | collective-permute-start | bytes 1179656 | tf_op jit(solution)/shard_map/ppermute | solution.py:351
  292.9 28.8 %collective-permute-start.40 = (bf16[2,2,384,128]{3,2,1,0:T(8,128)(2,1)S(1)}, bf16[2,2,384,128]{3,2,1,0:T(8,128)(2,1)S(1)}, u32[]{:S(2)}, u32[]{:S(2)}) collective-permute-start(bf16[2,2,384,128]{3,2,1,0:T(8,128)(2,1)S(1)} %get-tuple-element.166), channel_id=1, source_target_pairs={{0,8},{1,9},{2,10},{3,11},{4,12},{5,13},{6,14},{7,15},{8,0},{9,1},... | collective-permute-start | bytes 1179656 | tf_op jit(solution)/shard_map/ppermute | solution.py:351
  293.0 43.1 %collective-permute-start.30 = (bf16[2,4,2,192,128]{4,3,2,1,0:T(8,128)(2,1)S(1)}, bf16[2,4,2,192,128]{4,3,2,1,0:T(8,128)(2,1)S(1)}, u32[]{:S(2)}, u32[]{:S(2)}) collective-permute-start(bf16[2,4,2,192,128]{4,3,2,1,0:T(8,128)(2,1)S(1)} %slice.291), channel_id=1, source_target_pairs={{0,8},{1,9},{2,10},{3,11},{4,12},{5,13},{6,14},{7,15},{8,0},{9,1},... | collective-permute-start | bytes 2359304 | tf_op jit(solution)/shard_map/ppermute | solution.py:351
  296.9 32.7 %collective-permute-start.32 = (bf16[2,2,192,384]{3,2,1,0:T(8,128)(2,1)S(1)}, bf16[2,2,192,384]{3,2,1,0:T(8,128)(2,1)S(1)}, u32[]{:S(2)}, u32[]{:S(2)}) collective-permute-start(bf16[2,2,192,384]{3,2,1,0:T(8,128)(2,1)S(1)} %get-tuple-element.163), channel_id=1, source_target_pairs={{0,96},{16,112},{32,0},{48,16},{64,32},{80,48},{96,64},{112,80},{1... | collective-permute-start | bytes 1769480 | tf_op jit(solution)/shard_map/ppermute | solution.py:319
  (59 other events, 638.8 us)
Sparse Core Ops, SparseCore 0:
  10.3 50.1 all-gather.4
  62.8 41.5 all-gather.6
  243.3 75.2 reduce-scatter.1

commit v4 on v3

--- a/solution.py
+++ b/solution.py
@@ -21,7 +21,7 @@
     return lax.dot_general(a, b, dims, preferred_element_type=F32)
 
 
-def attention_kernel(h0, heads, total_heads, first, last, tile, order_ref, cols_ref, *refs):
+def attention_kernel(h0, heads, total_heads, first, last, tile, order_ref, *refs):
     q_ref, k_ref, v_ref, g_ref, do_ref, pc_ref, w_ref = refs[:7]
     bias_refs = refs[7:15]
     refs = refs[15:]
@@ -33,13 +33,13 @@
         refs = refs[5:]
     else:
         gq_in, gg_in, dkt_in, dvt_in = refs[:4]
-        gq_ref, gg_ref, keep_ref, send_ref, car_ref, acc_out = refs[4:10]
-        refs = refs[10:]
+        gq_ref, gg_ref, dkv_ref, car_ref, acc_out = refs[4:9]
+        refs = refs[9:]
     bias_s, s_s, e_s, t_s = refs[:4]
     refs = refs[4:]
     if not head_start:
-        dkt_s, dvt_s, kv_s = refs[:3]
-        refs = refs[3:]
+        dkt_s, dvt_s = refs[:2]
+        refs = refs[2:]
     acc_s = acc_out
     if last:
         acc_s = refs[0]
@@ -169,11 +169,7 @@
             for j, old, new in ((0, dkt_in, dkt_s), (1, dvt_in, dvt_s)):
                 both = jnp.concatenate([old[0, :, sl].astype(F32), new[:, sl]], axis=0).T.astype(BF)
                 for c in range(384 // cj):
-                    kv_s[(384 // cj) * b + c, j] = both[c * cj : (c + 1) * cj]
-        half = n // cj // 2
-        for r in range(half):
-            keep_ref[r, 0] = kv_s[cols_ref[r]]
-            send_ref[r, 0] = kv_s[cols_ref[half + r]]
+                    dkv_ref[(384 // cj) * b + c, j] = both[c * cj : (c + 1) * cj]
 
     if last:
 
@@ -181,11 +177,11 @@
         def _():
             for h in range(heads):
                 for s in range(8):
-                    off = pl.multiple_of((s if head_start else order_ref[s]) * kb, 128)
+                    off = pl.multiple_of(order_ref[s] * kb, 128)
                     acc_out[s, h] = acc_s[h, :, pl.ds(off, kb)].astype(BF)
 
 
-def attention(order, cols, q, kv, g, do, pc, w, biases, acc, earlier, h0, heads, total_heads, last, tile=3072):
+def attention(order, q, kv, g, do, pc, w, biases, acc, earlier, h0, heads, total_heads, last, tile=3072):
     ni, cj, chan = q.shape
     nb = kv.shape[0]
     n = nb * cj
@@ -223,11 +219,10 @@
     else:
         in_specs += [per_row, per_row, per_t, per_t]
         ops += earlier
-        half = nb // 2
-        kv_out = pl.BlockSpec((half, 1, 2, cj, chan), lambda i, *r: (0, i, 0, 0, 0))
-        out_specs += [kv_out, kv_out, pl.BlockSpec((1, chan, cj), lambda i, *r: (i, 0, 0))]
-        out_shape += [sd((half, ni, 2, cj, chan), BF), sd((half, ni, 2, cj, chan), BF), sd((ni, chan, cj), BF)]
-        scratch += [pltpu.VMEM((part, n), F32), pltpu.VMEM((part, n), F32), pltpu.VMEM((nb, 2, cj, chan), BF)]
+        kv_out = pl.BlockSpec((nb, 2, cj, chan), lambda i, *r: (0, i, 0, 0))
+        out_specs += [kv_out, pl.BlockSpec((1, chan, cj), lambda i, *r: (i, 0, 0))]
+        out_shape += [sd((nb, 2 * ni, cj, chan), BF), sd((ni, chan, cj), BF)]
+        scratch += [pltpu.VMEM((part, n), F32), pltpu.VMEM((part, n), F32)]
     if last:
         out_specs.append(whole(8, heads, cj, kb))
         out_shape.append(sd((8, heads, cj, kb), BF))
@@ -240,7 +235,7 @@
     return pl.pallas_call(
         functools.partial(attention_kernel, h0, heads, total_heads, first, last, tile),
         grid_spec=pltpu.PrefetchScalarGridSpec(
-            num_scalar_prefetch=2, grid=(ni,), in_specs=in_specs, out_specs=out_specs, scratch_shapes=scratch
+            num_scalar_prefetch=1, grid=(ni,), in_specs=in_specs, out_specs=out_specs, scratch_shapes=scratch
         ),
         out_shape=out_shape,
         compiler_params=pltpu.CompilerParams(dimension_semantics=("arbitrary",), vmem_limit_bytes=VMEM_LIMIT),
@@ -248,16 +243,16 @@
             flops=16 * heads * ni * cj * n * chan, bytes_accessed=30_000_000, transcendentals=heads * ni * cj * n
         ),
         name="attention_rows",
-    )(order, cols, *ops)
-
-
-def left_kernel(order_ref, cols_ref, *refs):
+    )(order, *ops)
+
+
+def left_kernel(rows, order_ref, cols_ref, *refs):
     car = refs[:8]
     r_ref, keep_ref, send_ref, l_s, o_s = refs[8:]
     step = pl.program_id(0)
-    ni, chan, cj = car[0].shape
+    _, _, chan, cj = car[0].shape
     cb, _, kk = r_ref.shape
-    rows = 8 * ni
+    ni = len(rows)
     half = ni // 2
 
     @pl.when(step == 0)
@@ -265,17 +260,17 @@
         for s in range(8):
             for i in range(ni):
                 at = pl.ds(pl.multiple_of((order_ref[s] * ni + i) * chan, chan), chan)
-                x = car[s][i].astype(F32)
+                x = car[s][0, rows[i]].astype(F32)
                 l_s[0, at, :] = x[:, :128]
                 l_s[1, at, : cj - 128] = x[:, 128:]
 
     for u in range(cb):
         c = step * cb + u
-        a = l_s[0, pl.ds(c, rows, stride=chan), :]
-        b = l_s[1, pl.ds(c, rows, stride=chan), :][:, : cj - 128]
+        a = l_s[0, pl.ds(c, 8 * ni, stride=chan), :]
+        b = l_s[1, pl.ds(c, 8 * ni, stride=chan), :][:, : cj - 128]
         res = dot(jnp.concatenate([a, b], axis=1).astype(BF), r_ref[u])
         for b in range(kk // 128):
-            o_s[b, pl.ds(c, rows, stride=chan), :] = res[:, b * 128 : (b + 1) * 128]
+            o_s[b, pl.ds(c, 8 * ni, stride=chan), :] = res[:, b * 128 : (b + 1) * 128]
 
     @pl.when(step == pl.num_programs(0) - 1)
     def _():
@@ -287,19 +282,25 @@
                         ref[r, i, b * 128 : (b + 1) * 128, :] = o_s[b, at, :].T.astype(BF)
 
 
-def left_product(order, cols, cars, right_t, cb=16):
-    ni, chan, cj = cars[0].shape
+def left_product(order, cols, pairs, right_t, rows, cb=16):
+    _, total, chan, cj = pairs[0].shape
+    ni = len(rows)
     kk = right_t.shape[2]
 
     def whole(*shape):
         return pl.BlockSpec(shape, lambda t, *r: (0,) * len(shape), pipeline_mode=pl.Buffered(1))
 
+    cars = [
+        pl.BlockSpec((1, total, chan, cj), lambda t, *r, z=z: (z, 0, 0, 0), pipeline_mode=pl.Buffered(1))
+        for _ in pairs
+        for z in range(2)
+    ]
     return pl.pallas_call(
-        left_kernel,
+        functools.partial(left_kernel, rows),
         grid_spec=pltpu.PrefetchScalarGridSpec(
             num_scalar_prefetch=2,
             grid=(chan // cb,),
-            in_specs=[whole(ni, chan, cj)] * 8 + [pl.BlockSpec((cb, cj, kk), lambda t, *r: (t, 0, 0))],
+            in_specs=cars + [pl.BlockSpec((cb, cj, kk), lambda t, *r: (t, 0, 0))],
             out_specs=[whole(8, ni // 2, kk, chan)] * 2,
             scratch_shapes=[
                 pltpu.VMEM((2, 8 * ni * chan, 128), F32),
@@ -308,11 +309,9 @@
         ),
         out_shape=[jax.ShapeDtypeStruct((8, ni // 2, kk, chan), BF)] * 2,
         compiler_params=pltpu.CompilerParams(dimension_semantics=("arbitrary",), vmem_limit_bytes=VMEM_LIMIT),
-        cost_estimate=pl.CostEstimate(
-            flops=40_000_000_000, bytes_accessed=30_000_000, transcendentals=0
-        ),
+        cost_estimate=pl.CostEstimate(flops=40_000_000_000, bytes_accessed=30_000_000, transcendentals=0),
         name="left_product",
-    )(order, cols, *cars, right_t)
+    )(order, cols, *(pair for pair in pairs for _ in range(2)), right_t)
 
 
 def row_shift(x, dy):
@@ -391,7 +390,7 @@
     hs = total_heads // 2
     bias_swap = row_swap(bias)
     first_shifts = row_shifts(bias[:hs])
-    right_t = jnp.transpose(after(right_proj, bias_swap), (2, 0, 1))
+    bias_swap, right_t = lax.optimization_barrier((bias_swap, jnp.transpose(right_proj, (2, 0, 1))))
     early = row_order(bias[:hs], bias_swap[:hs], first_shifts, row_shifts(bias_swap[:hs]))
     late = after(jnp.stack([bias[hs:], bias_swap[hs:]]), early)
     biases = [
@@ -411,65 +410,61 @@
     gathered = [
         lax.all_gather(jnp.concatenate([take(keys, ids), take(values, ids)]), "col", axis=0) for ids in picks
     ]
-    order, right_t = lax.optimization_barrier((order, right_t))
     small = [[take(a, ids) for a in (queries, gate_logits, out_grad, pair_cotangent)] for ids in picks]
 
     def attend(part, half, acc, earlier, order):
         q, g, do, pc = small[part]
         return attention(
-            order, cols, q, gathered[part], g, do, pc, query_weight, biases[half],
+            order, q, gathered[part], g, do, pc, query_weight, biases[half],
             acc, earlier, half * hs, hs, total_heads, part == 1,
         )
 
     a = attend(0, 0, None, None, order)
     b = attend(0, 1, None, list(a[:4]), order)
-    gq0, gg0, keep, send, car0 = b[:5]
-    got0, swap0, own0 = core_swap(send), row_swap(car0), row_shifts(car0)
+    gq0, gg0, dkv, car0 = b[:4]
+    sum0 = lax.psum_scatter(dkv, "col", scatter_dimension=0)
+    swap0 = row_swap(car0)
     c = attend(1, 0, a[-1], None, after(order, gq0))
-    got0, swap0, own0 = after((got0, swap0, own0), c[0])
-    part0 = add_pair(keep, got0)
-    part0, swap0 = lax.optimization_barrier((part0, swap0))
-    near0 = [x_shift(part0, 1), x_shift(part0, 3)]
-    swapped0 = row_shifts(swap0)
-    d = attend(1, 1, b[-1], list(c[:4]), after(order, part0, c[0]))
-    gq1, gg1, keep, send, car1 = d[:5]
-    near0, swapped0 = after((near0, swapped0), gq1)
-    total0 = add_all([part0[0:2]] + near0)
-    order_l, car1, send = lax.optimization_barrier((order, car1, send))
-    far0 = x_shift(part0, 2)
-    swap1, own1, got1 = row_swap(car1), row_shifts(car1), core_swap(send)
-    left0 = left_product(order_l, cols, row_order(car0, swap0, own0, swapped0), right_t)
-    far0, swap1, own1, got1, left0 = lax.optimization_barrier((far0, swap1, own1, got1, left0))
-    part1 = add_pair(keep, got1)
-    swapped1 = row_shifts(swap1)
-    total0 = add_all([total0, far0])
-    part1, total0 = lax.optimization_barrier((part1, total0))
-    near1 = [x_shift(part1, 1), x_shift(part1, 3)]
-    got_l0 = core_swap(left0[1])
-    swapped1, got_l0, total0, part1, bias1 = lax.optimization_barrier((swapped1, got_l0, total0, part1, d[-1]))
+    swap0, bias0 = lax.optimization_barrier((after(swap0, c[0]), c[-1]))
+    pair0 = jnp.stack([car0, swap0])
+    pairs0 = [pair0] + row_shifts(pair0)
+    bias0 = row_parts(bias0)
+    d = attend(1, 1, b[-1], list(c[:4]), after(order, pair0, c[0]))
+    gq1, gg1, dkv, car1 = d[:4]
+    sum1 = lax.psum_scatter(after(dkv, sum0), "col", scatter_dimension=0)
+    pairs0, near0 = after((pairs0, bias0[1:4:2]), gq1)
+    order_l, car1 = lax.optimization_barrier((order, car1))
+    swap1 = row_swap(car1)
+    left_a = left_product(after(order_l, pairs0), cols, pairs0, right_t, (0, 2))
+    swap1, left_a = lax.optimization_barrier((swap1, left_a))
+    pair1 = jnp.stack([car1, swap1])
+    pairs1 = [pair1] + row_shifts(pair1)
+    got_a = core_swap(left_a[1])
+    left_b = left_product(after(order_l, pair1, left_a, sum0), cols, pairs0, right_t, (1, 3))
+    far0, got_a, left_b, pairs1 = lax.optimization_barrier((bias0[2], got_a, left_b, pairs1))
+    bias0 = add_all([bias0[0], far0] + list(near0))
+    got_b = core_swap(left_b[1])
+    pairs1, got_b, bias1 = lax.optimization_barrier((pairs1, got_b, d[-1]))
+    part_l0 = jnp.concatenate([add_pair(left_a[0], got_a), add_pair(left_b[0], got_b)], axis=1)
+    shifts_l0 = [x_shift(part_l0, dx) for dx in (1, 3, 2)]
     bias1 = row_parts(bias1)
-    part_l0 = add_pair(left0[0], got_l0)
-    far1, got_z0 = x_shift(part1, 2), z_swap(total0)
-    left1 = left_product(after(order, swapped1, near1), cols, row_order(car1, swap1, own1, swapped1), right_t)
-    far1, got_z0, bias1 = after((far1, got_z0, bias1), left1)
-    part_l0, left1 = lax.optimization_barrier((part_l0, left1))
-    dkv0 = add_pair(total0[0], got_z0)
-    got_l1 = core_swap(left1[1])
-    sum_l0 = add_all([part_l0[0:2]] + [x_shift(part_l0, dx) for dx in (1, 3, 2)])
-    dkv1 = z_sum(add_all([part1[0:2], far1] + near1))
-    part_l1 = add_pair(left1[0], got_l1)
-    bias1 = add_all(bias1)
-    bias_z = row_swap(bias1[1])
+    left_c = left_product(after(order, pairs1, part_l0), cols, pairs1, right_t, (0, 1, 2, 3))
+    shifts_l0, bias1[1], bias1[3], left_c = lax.optimization_barrier((shifts_l0, bias1[1], bias1[3], left_c))
+    got_c = core_swap(left_c[1])
+    sum_l0 = add_all([part_l0[0:2]] + shifts_l0)
+    part_l1 = add_pair(left_c[0], after(got_c, sum_l0))
     sum_l1 = add_all([part_l1[0:2]] + [x_shift(part_l1, dx) for dx in (1, 3, 2)])
     left = z_sum(jnp.concatenate([sum_l0, sum_l1], axis=1))
-    bias0 = after(lax.psum_scatter(c[-1], "row", scatter_dimension=0), left)
-    grad_bias = jnp.concatenate([bias0.astype(F32), bias1[0].astype(F32) + bias_z.astype(F32)])
+    bias1 = add_all(after(bias1, part_l1))
+    bias_keep, bias_send = [jnp.concatenate([bias0[z], bias1[z]]) for z in range(2)]
+    grad_bias = bias_keep.astype(F32) + row_swap(bias_send).astype(F32)
+    sum0, sum1 = after((sum0, sum1), left)
 
     def untake(a, b):
         return jnp.concatenate([a[:quarter], b[:quarter], a[quarter:], b[quarter:]])
 
     gq, gg = untake(gq0, gq1), untake(gg0, gg1)
-    dk, dv = untake(dkv0[:, 0], dkv1[:, 0]), untake(dkv0[:, 1], dkv1[:, 1])
+    dk, dv = untake(sum0[::2], sum1[::2]), untake(sum0[1::2], sum1[1::2])
     return (gq, dk, dv, gg, grad_bias, left)
 
 

time: 383 us -> 336 us (0.88)
  waiting for transfers between devices: 81.7 us -> 55.7 us
  other arithmetic: 30.8 us -> 18.9 us
  Pallas kernels: 133 us -> 144 us
  starting transfers between devices: 71.3 us -> 60.3 us
  local copies, waits for them, and re-layouts: 45.8 us -> 36.5 us
    optimization_barrier x1 -> x0, local copies, waits for them, and re-layouts: 24.6 us -> none  [after(): return lax.optimization_barrier((x, done))[0]]
    ppermute x12 -> x6, waiting for transfers between devices: 28.1 us -> 10.2 us  [x_shift(): lax.ppermute(part[2 * dx:2 * dx + 2], 'col', [(c, (c + 4 * dx) % 16) for...]
    unnamed x66 -> x55, local copies, waits for them, and re-layouts: 8.13 us -> 25.8 us
    ppermute x4, waiting for transfers between devices: 14.9 us -> 1.54 us  [row_swap(): return lax.ppermute(x, 'row', [(r, r ^ 1) for r in range(8)])]
    convert_element_type x7 -> x4, other arithmetic: 13.2 us -> 1.69 us  [add_pair(): return (a.astype(F32) + b.astype(F32)).astype(BF)]
    pallas_call x2 -> x3, Pallas kernels: 33.8 us -> 45.2 us  [left_product(): pl.pallas_call(functools.partial(left_kernel, rows), grid_spec=pltpu.Pref...]
    ppermute x24 -> x21, waiting for transfers between devices: 25.3 us -> 34.2 us  [row_shift(): lax.ppermute(x, 'row', [(2 * y + z, 2 * ((y + dy) % 4) + z) for y in rang...]
    ppermute x24 -> x21, starting transfers between devices: 37.5 us -> 30 us  [row_shift(): lax.ppermute(x, 'row', [(2 * y + z, 2 * ((y + dy) % 4) + z) for y in rang...]
  transfers between devices with their start and end apart: 50 -> 39, of which waited for: 12 -> 11; matrix products, arithmetic and copies ran while one was open for 16% -> 15% of each run, Pallas kernels for 35% -> 44%
where the time goes in v4:
time: 336 us; the launch traced here: 330 us
  Pallas kernels  144 us (43%)
  starting transfers between devices  60.3 us (18%)
  waiting for transfers between devices  55.7 us (17%)
  local copies, waits for them, and re-layouts  36.5 us (11%)
  other arithmetic  18.9 us (6%)
  between operations  14.8 us (4%)
    pallas_call x4, Pallas kernels, attention(): pl.pallas_call(functools.partial(attention_kernel, h0, heads, total_heads...  98.8 us
    pallas_call x3, Pallas kernels, left_product(): pl.pallas_call(functools.partial(left_kernel, rows), grid_spec=pltpu.Pref...  45.2 us
    ppermute x21, waiting for transfers between devices, row_shift(): lax.ppermute(x, 'row', [(2 * y + z, 2 * ((y + dy) % 4) + z) for y in rang...  34.2 us
    ppermute x21, starting transfers between devices, row_shift(): lax.ppermute(x, 'row', [(2 * y + z, 2 * ((y + dy) % 4) + z) for y in rang...  30 us
    unnamed x55, local copies, waits for them, and re-layouts  25.8 us
    ppermute x6, starting transfers between devices, x_shift(): lax.ppermute(part[2 * dx:2 * dx + 2], 'col', [(c, (c + 4 * dx) % 16) for...  17 us
    ppermute x4, starting transfers between devices, row_swap(): return lax.ppermute(x, 'row', [(r, r ^ 1) for r in range(8)])  12.8 us
    ppermute x6, waiting for transfers between devices, x_shift(): lax.ppermute(part[2 * dx:2 * dx + 2], 'col', [(c, (c + 4 * dx) % 16) for...  10.2 us
  transfers between devices with their start and end apart: 39, of which 11 were waited for; matrix products, arithmetic and copies ran while one was open for 15% of the time, Pallas kernels for 44%

profile of v4, /device:TPU:0, one launch (start us, length us, event | category | flops | bytes accessed | tf_op | source)
XLA Modules:
  0.0 330.1 jit_solution(1947343606980983001)
XLA Ops:
  11.2 4.0 %collective-permute-start = (bf16[4,192,384]{2,1,0:T(8,128)(2,1)S(1)}, bf16[4,192,384]{2,1,0:T(8,128)(2,1)S(1)}, u32[]{:S(2)}, u32[]{:S(2)}) collective-permute-start(bf16[4,192,384]{2,1,0:T(8,128)(2,1)S(1)} %add_convert_fusion.5), channel_id=1, source_target_pairs={{0,16},{16,0},{32,48},{48,32},{64,80},{80,64},{96,112},{112,96},{1... | collective-permute-start | bytes 1769480 | tf_op jit(solution)/shard_map/ppermute | solution.py:322
  17.7 2.9 collective-permute-start.3
  22.2 24.7 %copy.17 = bf16[192,384,128]{1,0,2:T(8,128)(2,1)} copy(bf16[192,384,128]{2,1,0:T(8,128)(2,1)} %param.19) | data formatting | bytes 37748736 | tf_op args[9]
  53.5 9.5 %collective-permute-done.2 = bf16[2,192,384]{2,1,0:T(8,128)(2,1)S(1)} collective-permute-done((bf16[2,192,384]{2,1,0:T(8,128)(2,1)}, bf16[2,192,384]{2,1,0:T(8,128)(2,1)S(1)}, u32[]{:S(2)}, u32[]{:S(2)}) %collective-permute-start.2) | collective-permute-done | bytes 294944 | tf_op jit(solution)/shard_map/ppermute | solution.py:318
  64.3 3.6 %collective-permute-start.8 = (bf16[2,2,192,384]{3,2,1,0:T(8,128)(2,1)S(1)}, bf16[2,2,192,384]{3,2,1,0:T(8,128)(2,1)S(1)}, u32[]{:S(2)}, u32[]{:S(2)}) collective-permute-start(bf16[2,2,192,384]{3,2,1,0:T(8,128)(2,1)S(1)} %pad_maximum_fusion.1.refs_7_.refs_8_), channel_id=1, source_target_pairs={{0,64},{16,80},{32,96},{48,112},{64,0},{80,16},{96,32},{112,48},{1... | collective-permute-start | bytes 1769480 | tf_op jit(solution)/shard_map/ppermute | solution.py:318
  68.4 23.5 %attention_rows.4 = (bf16[4,192,128]{2,1,0:T(8,128)(2,1)}, bf16[4,192,128]{2,1,0:T(8,128)(2,1)}, bf16[4,64,3072]{2,1,0:T(8,128)(2,1)}, bf16[4,64,3072]{2,1,0:T(8,128)(2,1)}, f32[2,192,3072]{2,1,0:T(8,128)}) custom-call(s32[8]{0:T(128)} %stack.113.order_ref, bf16[4,192,128]{2,1,0:T(8,128)(2,1)} %get-tuple-element.231.refs_0_, ...), custom_call_target="tpu_custom_call" | custom-call | flops 9663676416 | bytes 30000000 | tf_op jit(solution)/shard_map/attention_rows/pallas_call | solution.py:235
  94.7 24.9 %attention_rows.5 = (bf16[4,192,128]{2,1,0:T(8,128)(2,1)}, bf16[4,192,128]{2,1,0:T(8,128)(2,1)}, bf16[16,8,192,128]{3,2,1,0:T(8,128)(2,1)}, bf16[4,128,192]{2,1,0:T(8,128)(2,1)}, f32[2,192,3072]{2,1,0:T(8,128)}) custom-call(s32[8]{0:T(128)} %stack.113.order_ref, bf16[4,192,128]{2,1,0:T(8,128)(2,1)} %get-tuple-element.231.refs_0_, ...), custom_call_target="tpu_custom_call" | custom-call | flops 9663676416 | bytes 30000000 | tf_op jit(solution)/shard_map/attention_rows/pallas_call | solution.py:235
  122.3 24.5 %attention_rows.6 = (bf16[4,192,128]{2,1,0:T(8,128)(2,1)}, bf16[4,192,128]{2,1,0:T(8,128)(2,1)}, bf16[4,64,3072]{2,1,0:T(8,128)(2,1)}, bf16[4,64,3072]{2,1,0:T(8,128)(2,1)}, bf16[8,2,192,384]{3,2,1,0:T(8,128)(2,1)}) custom-call(s32[8]{0:T(128)} %stack.113.order_ref, bf16[4,192,128]{2,1,0:T(8,128)(2,1)} %get-tuple-element.235.refs_0_, ...), custom_call_target="tpu_custom_call" | custom-call | flops 9663676416 | bytes 30000000 | tf_op jit(solution)/shard_map/attention_rows/pallas_call | solution.py:235
  147.5 2.9 collective-permute-start.13
  154.4 25.9 %attention_rows.7 = (bf16[4,192,128]{2,1,0:T(8,128)(2,1)}, bf16[4,192,128]{2,1,0:T(8,128)(2,1)}, bf16[16,8,192,128]{3,2,1,0:T(8,128)(2,1)}, bf16[4,128,192]{2,1,0:T(8,128)(2,1)}, bf16[8,2,192,384]{3,2,1,0:T(8,128)(2,1)}) custom-call(s32[8]{0:T(128)} %stack.113.order_ref, bf16[4,192,128]{2,1,0:T(8,128)(2,1)} %get-tuple-element.235.refs_0_, ...), custom_call_target="tpu_custom_call" | custom-call | flops 9663676416 | bytes 30000000 | tf_op jit(solution)/shard_map/attention_rows/pallas_call | solution.py:235
  180.4 3.7 %collective-permute-start.11 = (bf16[4,128,192]{2,1,0:T(8,128)(2,1)}, bf16[4,128,192]{2,1,0:T(8,128)(2,1)}, u32[]{:S(2)}, u32[]{:S(2)}) collective-permute-start(bf16[4,128,192]{2,1,0:T(8,128)(2,1)} %get-tuple-element.107), channel_id=1, source_target_pairs={{0,16},{16,0},{32,48},{48,32},{64,80},{80,64},{96,112},{112,96},{1... | collective-permute-start | bytes 589832 | tf_op jit(solution)/shard_map/ppermute | solution.py:322
  184.0 2.6 collective-permute-start.17
  186.7 14.0 %left_product.3 = (bf16[8,1,384,128]{3,2,1,0:T(8,128)(2,1)}, bf16[8,1,384,128]{3,2,1,0:T(8,128)(2,1)}) custom-call(s32[8]{0:T(128)} %stack.113.order_ref, s32[16]{0:T(128)} %stack.136.cols_ref, bf16[2,4,128,192]{3,2,1,0:T(8,128)(2,1)} %copy-done.11, bf16[2,4,128,192]{3,2,1,0:T(8,128)(2,1)} %copy-done.11, bf16[2,4,128,192]{3,2,1,0:T(8,128)(2,1)} %copy-done.24, ...), custom_call_target="tpu_custom_call" | custom-call | flops 40000000000 | bytes 30000000 | tf_op jit(solution)/shard_map/left_product/pallas_call | solution.py:298
  202.5 2.8 collective-permute-start.20
  205.6 14.2 %left_product.4 = (bf16[8,1,384,128]{3,2,1,0:T(8,128)(2,1)}, bf16[8,1,384,128]{3,2,1,0:T(8,128)(2,1)}) custom-call(s32[8]{0:T(128)} %stack.113.order_ref, s32[16]{0:T(128)} %stack.136.cols_ref, bf16[2,4,128,192]{3,2,1,0:T(8,128)(2,1)} %copy-done.11, bf16[2,4,128,192]{3,2,1,0:T(8,128)(2,1)} %copy-done.11, bf16[2,4,128,192]{3,2,1,0:T(8,128)(2,1)} %copy-done.24, ...), custom_call_target="tpu_custom_call" | custom-call | flops 40000000000 | bytes 30000000 | tf_op jit(solution)/shard_map/left_product/pallas_call | solution.py:298
  219.8 8.4 %collective-permute-done.20.refs_4_.refs_5_ = bf16[2,4,128,192]{3,2,1,0:T(8,128)(2,1)} collective-permute-done((bf16[2,4,128,192]{3,2,1,0:T(8,128)(2,1)S(1)}, bf16[2,4,128,192]{3,2,1,0:T(8,128)(2,1)}, u32[]{:S(2)}, u32[]{:S(2)}) %collective-permute-start.20) | collective-permute-done | bytes 393248 | tf_op jit(solution)/shard_map/ppermute | solution.py:318
  235.6 2.4 collective-permute-start.24
  239.5 17.0 %left_product.5 = (bf16[8,2,384,128]{3,2,1,0:T(8,128)(2,1)}, bf16[8,2,384,128]{3,2,1,0:T(8,128)(2,1)}) custom-call(s32[8]{0:T(128)} %stack.113.order_ref, s32[16]{0:T(128)} %stack.136.cols_ref, bf16[2,4,128,192]{3,2,1,0:T(8,128)(2,1)} %copy-done.12, bf16[2,4,128,192]{3,2,1,0:T(8,128)(2,1)} %copy-done.12, ...), custom_call_target="tpu_custom_call" | custom-call | flops 40000000000 | bytes 30000000 | tf_op jit(solution)/shard_map/left_product/pallas_call | solution.py:298
  264.8 13.7 %collective-permute-done.33 = bf16[2,2,192,384]{3,2,1,0:T(8,128)(2,1)S(1)} collective-permute-done((bf16[2,2,192,384]{3,2,1,0:T(8,128)(2,1)S(1)}, bf16[2,2,192,384]{3,2,1,0:T(8,128)(2,1)S(1)}, u32[]{:S(2)}, u32[]{:S(2)}) %collective-permute-start.33) | collective-permute-done | bytes 589856 | tf_op jit(solution)/shard_map/ppermute | solution.py:318
  278.6 9.8 %collective-permute-start.29 = (bf16[2,2,384,128]{3,2,1,0:T(8,128)(2,1)S(1)}, bf16[2,2,384,128]{3,2,1,0:T(8,128)(2,1)S(1)}, u32[]{:S(2)}, u32[]{:S(2)}) collective-permute-start(bf16[2,2,384,128]{3,2,1,0:T(8,128)(2,1)S(1)} %get-tuple-element.167), channel_id=1, source_target_pairs={{0,4},{1,5},{2,6},{3,7},{4,8},{5,9},{6,10},{7,11},{8,12},{9,13},{1... | collective-permute-start | bytes 1179656 | tf_op jit(solution)/shard_map/ppermute | solution.py:350
  292.3 5.0 %collective-permute-start.34 = (bf16[4,192,384]{2,1,0:T(8,128)(2,1)S(1)}, bf16[4,192,384]{2,1,0:T(8,128)(2,1)S(1)}, u32[]{:S(2)}, u32[]{:S(2)}) collective-permute-start(bf16[4,192,384]{2,1,0:T(8,128)(2,1)S(1)} %pad_maximum_fusion.2), channel_id=1, source_target_pairs={{0,16},{16,0},{32,48},{48,32},{64,80},{80,64},{96,112},{112,96},{1... | collective-permute-start | bytes 1769480 | tf_op jit(solution)/shard_map/ppermute | solution.py:322
  298.0 2.5 collective-permute-done.30
  300.5 6.9 %collective-permute-done.31 = bf16[2,2,384,128]{3,2,1,0:T(8,128)(2,1)S(1)} collective-permute-done((bf16[2,2,384,128]{3,2,1,0:T(8,128)(2,1)S(1)}, bf16[2,2,384,128]{3,2,1,0:T(8,128)(2,1)S(1)}, u32[]{:S(2)}, u32[]{:S(2)}) %collective-permute-start.31) | collective-permute-done | bytes 393248 | tf_op jit(solution)/shard_map/ppermute | solution.py:350
  312.2 7.5 %collective-permute-done.32 = bf16[4,384,128]{2,1,0:T(8,128)(2,1)S(1)} collective-permute-done((bf16[4,384,128]{2,1,0:T(8,128)(2,1)S(1)}, bf16[4,384,128]{2,1,0:T(8,128)(2,1)S(1)}, u32[]{:S(2)}, u32[]{:S(2)}) %collective-permute-start.32) | collective-permute-done | bytes 393248 | tf_op jit(solution)/shard_map/ppermute | solution.py:354
  (171 shorter events, 58.5 us)
Async XLA Ops:
  7.2 61.2 %all-gather.5.cloned.1.call-start = ((), (), s32[]{:S(2)}) async-start(), calls=%async_computation.4 | async-start | bytes 6684672 | tf_op jit(solution)/shard_map/all_gather | solution.py:411
  9.3 112.9 %all-gather.7.cloned.1.call-start = ((), (), s32[]{:S(2)}) async-start(), calls=%async_computation.5 | async-start | bytes 6684672 | tf_op jit(solution)/shard_map/all_gather | solution.py:411
  10.2 195.3 %reduce-scatter.3.cloned.1.call-start = ((), (), s32[]{:S(2)}) async-start(), calls=%async_computation.2 | async-start | bytes 6684672 | tf_op jit(solution)/shard_map/reduce_scatter | solution.py:425
  11.2 35.6 %collective-permute-start = (bf16[4,192,384]{2,1,0:T(8,128)(2,1)S(1)}, bf16[4,192,384]{2,1,0:T(8,128)(2,1)S(1)}, u32[]{:S(2)}, u32[]{:S(2)}) collective-permute-start(bf16[4,192,384]{2,1,0:T(8,128)(2,1)S(1)} %add_convert_fusion.5), channel_id=1, source_target_pairs={{0,16},{16,0},{32,48},{48,32},{64,80},{80,64},{96,112},{112,96},{1... | collective-permute-start | bytes 1769480 | tf_op jit(solution)/shard_map/ppermute | solution.py:322
  16.2 33.1 %collective-permute-start.1 = (bf16[2,192,384]{2,1,0:T(8,128)(2,1)}, bf16[2,192,384]{2,1,0:T(8,128)(2,1)}, u32[]{:S(2)}, u32[]{:S(2)}) collective-permute-start(bf16[2,192,384]{2,1,0:T(8,128)(2,1)} %get-tuple-element.181), channel_id=1, source_target_pairs={{0,32},{16,48},{32,64},{48,80},{64,96},{80,112},{96,0},{112,16},{1... | collective-permute-start | bytes 884744 | tf_op jit(solution)/shard_map/ppermute | solution.py:318
  17.7 35.7 %collective-permute-start.3 = (bf16[2,192,384]{2,1,0:T(8,128)(2,1)}, bf16[2,192,384]{2,1,0:T(8,128)(2,1)}, u32[]{:S(2)}, u32[]{:S(2)}) collective-permute-start(bf16[2,192,384]{2,1,0:T(8,128)(2,1)} %get-tuple-element.181), channel_id=1, source_target_pairs={{0,64},{16,80},{32,96},{48,112},{64,0},{80,16},{96,32},{112,48},{1... | collective-permute-start | bytes 884744 | tf_op jit(solution)/shard_map/ppermute | solution.py:318
  20.6 32.9 %collective-permute-start.5 = (bf16[2,192,384]{2,1,0:T(8,128)(2,1)}, bf16[2,192,384]{2,1,0:T(8,128)(2,1)}, u32[]{:S(2)}, u32[]{:S(2)}) collective-permute-start(bf16[2,192,384]{2,1,0:T(8,128)(2,1)} %get-tuple-element.181), channel_id=1, source_target_pairs={{0,96},{16,112},{32,0},{48,16},{64,32},{80,48},{96,64},{112,80},{1... | collective-permute-start | bytes 884744 | tf_op jit(solution)/shard_map/ppermute | solution.py:318
  63.7 28.1 %collective-permute-start.7 = (bf16[2,2,192,384]{3,2,1,0:T(8,128)(2,1)S(1)}, bf16[2,2,192,384]{3,2,1,0:T(8,128)(2,1)S(1)}, u32[]{:S(2)}, u32[]{:S(2)}) collective-permute-start(bf16[2,2,192,384]{3,2,1,0:T(8,128)(2,1)S(1)} %pad_maximum_fusion.1.refs_7_.refs_8_), channel_id=1, source_target_pairs={{0,32},{16,48},{32,64},{48,80},{64,96},{80,112},{96,0},{112,16},{1... | collective-permute-start | bytes 1769480 | tf_op jit(solution)/shard_map/ppermute | solution.py:318
  64.3 29.4 %collective-permute-start.8 = (bf16[2,2,192,384]{3,2,1,0:T(8,128)(2,1)S(1)}, bf16[2,2,192,384]{3,2,1,0:T(8,128)(2,1)S(1)}, u32[]{:S(2)}, u32[]{:S(2)}) collective-permute-start(bf16[2,2,192,384]{3,2,1,0:T(8,128)(2,1)S(1)} %pad_maximum_fusion.1.refs_7_.refs_8_), channel_id=1, source_target_pairs={{0,64},{16,80},{32,96},{48,112},{64,0},{80,16},{96,32},{112,48},{1... | collective-permute-start | bytes 1769480 | tf_op jit(solution)/shard_map/ppermute | solution.py:318
  67.8 25.9 %collective-permute-start.9 = (bf16[2,2,192,384]{3,2,1,0:T(8,128)(2,1)S(1)}, bf16[2,2,192,384]{3,2,1,0:T(8,128)(2,1)S(1)}, u32[]{:S(2)}, u32[]{:S(2)}) collective-permute-start(bf16[2,2,192,384]{3,2,1,0:T(8,128)(2,1)S(1)} %pad_maximum_fusion.1.refs_7_.refs_8_), channel_id=1, source_target_pairs={{0,96},{16,112},{32,0},{48,16},{64,32},{80,48},{96,64},{112,80},{1... | collective-permute-start | bytes 1769480 | tf_op jit(solution)/shard_map/ppermute | solution.py:318
  119.6 200.9 %reduce-scatter.5.cloned.1.call-start = ((), (), s32[]{:S(2)}) async-start(), calls=%async_computation.3 | async-start | bytes 6684672 | tf_op jit(solution)/shard_map/reduce_scatter | solution.py:434
  122.1 24.7 %collective-permute-start.10 = (bf16[4,128,192]{2,1,0:T(8,128)(2,1)S(1)}, bf16[4,128,192]{2,1,0:T(8,128)(2,1)S(1)}, u32[]{:S(2)}, u32[]{:S(2)}) collective-permute-start(bf16[4,128,192]{2,1,0:T(8,128)(2,1)S(1)} %copy-done.18), channel_id=1, source_target_pairs={{0,16},{16,0},{32,48},{48,32},{64,80},{80,64},{96,112},{112,96},{1... | collective-permute-start | bytes 589832 | tf_op jit(solution)/shard_map/ppermute | solution.py:322
  146.9 33.4 %collective-permute-start.12 = (bf16[2,4,128,192]{3,2,1,0:T(8,128)(2,1)S(1)}, bf16[2,4,128,192]{3,2,1,0:T(8,128)(2,1)S(1)}, u32[]{:S(2)}, u32[]{:S(2)}) collective-permute-start(bf16[2,4,128,192]{3,2,1,0:T(8,128)(2,1)S(1)} %pad_maximum_fusion.3.refs_0_.refs_1_), channel_id=1, source_target_pairs={{0,32},{16,48},{32,64},{48,80},{64,96},{80,112},{96,0},{112,16},{1... | collective-permute-start | bytes 1179656 | tf_op jit(solution)/shard_map/ppermute | solution.py:318
  147.5 36.5 %collective-permute-start.13 = (bf16[2,4,128,192]{3,2,1,0:T(8,128)(2,1)S(1)}, bf16[2,4,128,192]{3,2,1,0:T(8,128)(2,1)}, u32[]{:S(2)}, u32[]{:S(2)}) collective-permute-start(bf16[2,4,128,192]{3,2,1,0:T(8,128)(2,1)S(1)} %pad_maximum_fusion.3.refs_0_.refs_1_), channel_id=1, source_target_pairs={{0,64},{16,80},{32,96},{48,112},{64,0},{80,16},{96,32},{112,48},{1... | collective-permute-start | bytes 1179656 | tf_op jit(solution)/shard_map/ppermute | solution.py:318
  150.4 36.3 %collective-permute-start.14 = (bf16[2,4,128,192]{3,2,1,0:T(8,128)(2,1)S(1)}, bf16[2,4,128,192]{3,2,1,0:T(8,128)(2,1)}, u32[]{:S(2)}, u32[]{:S(2)}) collective-permute-start(bf16[2,4,128,192]{3,2,1,0:T(8,128)(2,1)S(1)} %pad_maximum_fusion.3.refs_0_.refs_1_), channel_id=1, source_target_pairs={{0,96},{16,112},{32,0},{48,16},{64,32},{80,48},{96,64},{112,80},{1... | collective-permute-start | bytes 1179656 | tf_op jit(solution)/shard_map/ppermute | solution.py:318
  152.1 34.6 %collective-permute-start.15 = (bf16[2,2,192,384]{3,2,1,0:T(8,128)(2,1)S(1)}, bf16[2,2,192,384]{3,2,1,0:T(8,128)(2,1)S(1)}, u32[]{:S(2)}, u32[]{:S(2)}) collective-permute-start(bf16[2,2,192,384]{3,2,1,0:T(8,128)(2,1)S(1)} %get-tuple-element.166), channel_id=1, source_target_pairs={{0,96},{16,112},{32,0},{48,16},{64,32},{80,48},{96,64},{112,80},{1... | collective-permute-start | bytes 1769480 | tf_op jit(solution)/shard_map/ppermute | solution.py:318
  153.4 33.3 %collective-permute-start.16 = (bf16[2,2,192,384]{3,2,1,0:T(8,128)(2,1)S(1)}, bf16[2,2,192,384]{3,2,1,0:T(8,128)(2,1)S(1)}, u32[]{:S(2)}, u32[]{:S(2)}) collective-permute-start(bf16[2,2,192,384]{3,2,1,0:T(8,128)(2,1)S(1)} %get-tuple-element.164), channel_id=1, source_target_pairs={{0,32},{16,48},{32,64},{48,80},{64,96},{80,112},{96,0},{112,16},{1... | collective-permute-start | bytes 1769480 | tf_op jit(solution)/shard_map/ppermute | solution.py:318
  184.0 35.8 %collective-permute-start.17 = (bf16[2,2,192,384]{3,2,1,0:T(8,128)(2,1)S(1)}, bf16[2,2,192,384]{3,2,1,0:T(8,128)(2,1)S(1)}, u32[]{:S(2)}, u32[]{:S(2)}) collective-permute-start(bf16[2,2,192,384]{3,2,1,0:T(8,128)(2,1)S(1)} %get-tuple-element.165), channel_id=1, source_target_pairs={{0,64},{16,80},{32,96},{48,112},{64,0},{80,16},{96,32},{112,48},{1... | collective-permute-start | bytes 1769480 | tf_op jit(solution)/shard_map/ppermute | solution.py:318
  202.5 25.7 %collective-permute-start.20 = (bf16[2,4,128,192]{3,2,1,0:T(8,128)(2,1)S(1)}, bf16[2,4,128,192]{3,2,1,0:T(8,128)(2,1)}, u32[]{:S(2)}, u32[]{:S(2)}) collective-permute-start(bf16[2,4,128,192]{3,2,1,0:T(8,128)(2,1)S(1)} %pad_maximum_fusion.4.refs_0_.refs_1_), channel_id=1, source_target_pairs={{0,64},{16,80},{32,96},{48,112},{64,0},{80,16},{96,32},{112,48},{1... | collective-permute-start | bytes 1179656 | tf_op jit(solution)/shard_map/ppermute | solution.py:318
  205.3 22.8 %collective-permute-start.21 = (bf16[2,4,128,192]{3,2,1,0:T(8,128)(2,1)S(1)}, bf16[2,4,128,192]{3,2,1,0:T(8,128)(2,1)}, u32[]{:S(2)}, u32[]{:S(2)}) collective-permute-start(bf16[2,4,128,192]{3,2,1,0:T(8,128)(2,1)S(1)} %pad_maximum_fusion.4.refs_0_.refs_1_), channel_id=1, source_target_pairs={{0,96},{16,112},{32,0},{48,16},{64,32},{80,48},{96,64},{112,80},{1... | collective-permute-start | bytes 1179656 | tf_op jit(solution)/shard_map/ppermute | solution.py:318
  205.5 22.6 %collective-permute-start.18 = (bf16[8,1,384,128]{3,2,1,0:T(8,128)(2,1)}, bf16[8,1,384,128]{3,2,1,0:T(8,128)(2,1)S(1)}, u32[]{:S(2)}, u32[]{:S(2)}) collective-permute-start(bf16[8,1,384,128]{3,2,1,0:T(8,128)(2,1)} %get-tuple-element.119), channel_id=1, source_target_pairs={{0,1},{1,0},{2,3},{3,2},{4,5},{5,4},{6,7},{7,6},{8,9},{9,8},{10,11... | collective-permute-start | bytes 2359304 | tf_op jit(solution)/shard_map/ppermute | solution.py:342
  231.0 25.5 %collective-permute-start.26 = (bf16[2,2,192,384]{3,2,1,0:T(8,128)(2,1)S(1)}, bf16[2,2,192,384]{3,2,1,0:T(8,128)(2,1)}, u32[]{:S(2)}, u32[]{:S(2)}) collective-permute-start(bf16[2,2,192,384]{3,2,1,0:T(8,128)(2,1)S(1)} %get-tuple-element.163), channel_id=1, source_target_pairs={{0,96},{16,112},{32,0},{48,16},{64,32},{80,48},{96,64},{112,80},{1... | collective-permute-start | bytes 1769480 | tf_op jit(solution)/shard_map/ppermute | solution.py:318
  233.2 23.3 %collective-permute-start.27 = (bf16[2,2,192,384]{3,2,1,0:T(8,128)(2,1)S(1)}, bf16[2,2,192,384]{3,2,1,0:T(8,128)(2,1)}, u32[]{:S(2)}, u32[]{:S(2)}) collective-permute-start(bf16[2,2,192,384]{3,2,1,0:T(8,128)(2,1)S(1)} %get-tuple-element.162), channel_id=1, source_target_pairs={{0,32},{16,48},{32,64},{48,80},{64,96},{80,112},{96,0},{112,16},{1... | collective-permute-start | bytes 1769480 | tf_op jit(solution)/shard_map/ppermute | solution.py:318
  234.5 22.0 %collective-permute-start.23 = (bf16[2,2,384,128]{3,2,1,0:T(8,128)(2,1)}, bf16[2,2,384,128]{3,2,1,0:T(8,128)(2,1)}, u32[]{:S(2)}, u32[]{:S(2)}) collective-permute-start(bf16[2,2,384,128]{3,2,1,0:T(8,128)(2,1)} %get-tuple-element.171), channel_id=1, source_target_pairs={{0,4},{1,5},{2,6},{3,7},{4,8},{5,9},{6,10},{7,11},{8,12},{9,13},{1... | collective-permute-start | bytes 1179656 | tf_op jit(solution)/shard_map/ppermute | solution.py:350
  (42 other events, 464.9 us)
Sparse Core Ops, SparseCore 0:
  10.3 50.1 all-gather.4
  62.8 41.5 all-gather.6
  119.7 78.7 reduce-scatter.2
  205.7 84.5 reduce-scatter.4

commit v5 on v4

--- a/solution.py
+++ b/solution.py
@@ -246,13 +246,12 @@
     )(order, *ops)
 
 
-def left_kernel(rows, order_ref, cols_ref, *refs):
+def left_kernel(order_ref, cols_ref, *refs):
     car = refs[:8]
     r_ref, keep_ref, send_ref, l_s, o_s = refs[8:]
     step = pl.program_id(0)
-    _, _, chan, cj = car[0].shape
+    _, ni, chan, cj = car[0].shape
     cb, _, kk = r_ref.shape
-    ni = len(rows)
     half = ni // 2
 
     @pl.when(step == 0)
@@ -260,7 +259,7 @@
         for s in range(8):
             for i in range(ni):
                 at = pl.ds(pl.multiple_of((order_ref[s] * ni + i) * chan, chan), chan)
-                x = car[s][0, rows[i]].astype(F32)
+                x = car[s][0, i].astype(F32)
                 l_s[0, at, :] = x[:, :128]
                 l_s[1, at, : cj - 128] = x[:, 128:]
 
@@ -282,21 +281,20 @@
                         ref[r, i, b * 128 : (b + 1) * 128, :] = o_s[b, at, :].T.astype(BF)
 
 
-def left_product(order, cols, pairs, right_t, rows, cb=16):
-    _, total, chan, cj = pairs[0].shape
-    ni = len(rows)
+def left_product(order, cols, pairs, right_t, cb=16):
+    _, ni, chan, cj = pairs[0].shape
     kk = right_t.shape[2]
 
     def whole(*shape):
         return pl.BlockSpec(shape, lambda t, *r: (0,) * len(shape), pipeline_mode=pl.Buffered(1))
 
     cars = [
-        pl.BlockSpec((1, total, chan, cj), lambda t, *r, z=z: (z, 0, 0, 0), pipeline_mode=pl.Buffered(1))
+        pl.BlockSpec((1, ni, chan, cj), lambda t, *r, z=z: (z, 0, 0, 0), pipeline_mode=pl.Buffered(1))
         for _ in pairs
         for z in range(2)
     ]
     return pl.pallas_call(
-        functools.partial(left_kernel, rows),
+        left_kernel,
         grid_spec=pltpu.PrefetchScalarGridSpec(
             num_scalar_prefetch=2,
             grid=(chan // cb,),
@@ -435,29 +433,29 @@
     pairs0, near0 = after((pairs0, bias0[1:4:2]), gq1)
     order_l, car1 = lax.optimization_barrier((order, car1))
     swap1 = row_swap(car1)
-    left_a = left_product(after(order_l, pairs0), cols, pairs0, right_t, (0, 2))
-    swap1, left_a = lax.optimization_barrier((swap1, left_a))
+    left0 = left_product(after(order_l, pairs0, near0), cols, pairs0, right_t)
+    swap1, far0, left0, sum0 = lax.optimization_barrier((swap1, bias0[2], left0, sum0))
     pair1 = jnp.stack([car1, swap1])
     pairs1 = [pair1] + row_shifts(pair1)
-    got_a = core_swap(left_a[1])
-    left_b = left_product(after(order_l, pair1, left_a, sum0), cols, pairs0, right_t, (1, 3))
-    far0, got_a, left_b, pairs1 = lax.optimization_barrier((bias0[2], got_a, left_b, pairs1))
+    part_l0 = add_pair(left0[0], core_swap(left0[1]))
+    near_l0 = [x_shift(part_l0, 1), x_shift(part_l0, 3)]
     bias0 = add_all([bias0[0], far0] + list(near0))
-    got_b = core_swap(left_b[1])
-    pairs1, got_b, bias1 = lax.optimization_barrier((pairs1, got_b, d[-1]))
-    part_l0 = jnp.concatenate([add_pair(left_a[0], got_a), add_pair(left_b[0], got_b)], axis=1)
-    shifts_l0 = [x_shift(part_l0, dx) for dx in (1, 3, 2)]
+    pairs1, near_l0, bias1, bias0 = lax.optimization_barrier((pairs1, near_l0, d[-1], bias0))
+    far_l0 = x_shift(part_l0, 2)
     bias1 = row_parts(bias1)
-    left_c = left_product(after(order, pairs1, part_l0), cols, pairs1, right_t, (0, 1, 2, 3))
-    shifts_l0, bias1[1], bias1[3], left_c = lax.optimization_barrier((shifts_l0, bias1[1], bias1[3], left_c))
-    got_c = core_swap(left_c[1])
-    sum_l0 = add_all([part_l0[0:2]] + shifts_l0)
-    part_l1 = add_pair(left_c[0], after(got_c, sum_l0))
-    sum_l1 = add_all([part_l1[0:2]] + [x_shift(part_l1, dx) for dx in (1, 3, 2)])
-    left = z_sum(jnp.concatenate([sum_l0, sum_l1], axis=1))
-    bias1 = add_all(after(bias1, part_l1))
+    left1 = left_product(after(order, pairs1, near_l0), cols, pairs1, right_t)
+    far_l0, bias1, left1 = lax.optimization_barrier((far_l0, bias1, left1))
+    part_l1 = add_pair(left1[0], core_swap(left1[1]))
+    shifts_l1 = [x_shift(part_l1, dx) for dx in (1, 3, 2)]
+    sum_l0 = add_all([part_l0[0:2], far_l0] + near_l0)
+    bias1 = add_all(bias1)
     bias_keep, bias_send = [jnp.concatenate([bias0[z], bias1[z]]) for z in range(2)]
-    grad_bias = bias_keep.astype(F32) + row_swap(bias_send).astype(F32)
+    got_l0, got_bias = z_swap(sum_l0), row_swap(bias_send)
+    sum_l1 = add_all([part_l1[0:2]] + shifts_l1)
+    got_l1 = z_swap(sum_l1)
+    left = jnp.concatenate([add_pair(sum_l0[0], got_l0), add_pair(sum_l1[0], got_l1)])
+    got_bias, bias_keep = after((got_bias, bias_keep), got_l1)
+    grad_bias = bias_keep.astype(F32) + got_bias.astype(F32)
     sum0, sum1 = after((sum0, sum1), left)
 
     def untake(a, b):

time: 336 us -> 337 us (level)
  waiting for transfers between devices: 55.7 us -> 73.5 us
  Pallas kernels: 144 us -> 133 us
  starting transfers between devices: 60.3 us -> 51.1 us
    reduce_scatter x1, waiting for transfers between devices: 0.01 us -> 15.8 us  [local(): sum0 = lax.psum_scatter(dkv, 'col', scatter_dimension=0)]
    pallas_call x3 -> x2, Pallas kernels: 45.2 us -> 34 us  [left_product(): pl.pallas_call(left_kernel, grid_spec=pltpu.PrefetchScalarGridSpec(num_sc...]
    ppermute x6, starting transfers between devices: 17 us -> 9.58 us  [x_shift(): lax.ppermute(part[2 * dx:2 * dx + 2], 'col', [(c, (c + 4 * dx) % 16) for...]
    ppermute x6, waiting for transfers between devices: 10.2 us -> 14.2 us  [x_shift(): lax.ppermute(part[2 * dx:2 * dx + 2], 'col', [(c, (c + 4 * dx) % 16) for...]
    ppermute x21, waiting for transfers between devices: 34.2 us -> 37.6 us  [row_shift(): lax.ppermute(x, 'row', [(2 * y + z, 2 * ((y + dy) % 4) + z) for y in rang...]
    ppermute x1 -> x2, waiting for transfers between devices: 7.49 us -> 5.82 us  [z_swap(): return lax.ppermute(total[1], 'col', [(c, c ^ 2) for c in range(16)])]
  transfers between devices with their start and end apart: 39 -> 39, of which waited for: 11 -> 12; matrix products, arithmetic and copies ran while one was open for 15% -> 16% of each run, Pallas kernels for 44% -> 40%
where the time goes in v5:
time: 337 us; the launch traced here: 331 us
  Pallas kernels  133 us (39%)
  waiting for transfers between devices  73.5 us (22%)
  starting transfers between devices  51.1 us (15%)
  local copies, waits for them, and re-layouts  39.1 us (12%)
  other arithmetic  20.3 us (6%)
  between operations  14.7 us (4%)
    pallas_call x4, Pallas kernels, attention(): pl.pallas_call(functools.partial(attention_kernel, h0, heads, total_heads...  98.7 us
    ppermute x21, waiting for transfers between devices, row_shift(): lax.ppermute(x, 'row', [(2 * y + z, 2 * ((y + dy) % 4) + z) for y in rang...  37.6 us
    pallas_call x2, Pallas kernels, left_product(): pl.pallas_call(left_kernel, grid_spec=pltpu.PrefetchScalarGridSpec(num_sc...  34 us
    ppermute x21, starting transfers between devices, row_shift(): lax.ppermute(x, 'row', [(2 * y + z, 2 * ((y + dy) % 4) + z) for y in rang...  29.5 us
    unnamed x55, local copies, waits for them, and re-layouts  27.2 us
    reduce_scatter x1, waiting for transfers between devices, local(): sum0 = lax.psum_scatter(dkv, 'col', scatter_dimension=0)  15.8 us
    ppermute x6, waiting for transfers between devices, x_shift(): lax.ppermute(part[2 * dx:2 * dx + 2], 'col', [(c, (c + 4 * dx) % 16) for...  14.2 us
    ppermute x4, starting transfers between devices, row_swap(): return lax.ppermute(x, 'row', [(r, r ^ 1) for r in range(8)])  10.7 us
  transfers between devices with their start and end apart: 39, of which 12 were waited for; matrix products, arithmetic and copies ran while one was open for 16% of the time, Pallas kernels for 40%

profile of v5, /device:TPU:0, one launch (start us, length us, event | category | flops | bytes accessed | tf_op | source)
XLA Modules:
  0.0 331.4 jit_solution(1357773986125895411)
XLA Ops:
  11.2 4.0 %collective-permute-start = (bf16[4,192,384]{2,1,0:T(8,128)(2,1)S(1)}, bf16[4,192,384]{2,1,0:T(8,128)(2,1)S(1)}, u32[]{:S(2)}, u32[]{:S(2)}) collective-permute-start(bf16[4,192,384]{2,1,0:T(8,128)(2,1)S(1)} %add_convert_fusion.4), channel_id=1, source_target_pairs={{0,16},{16,0},{32,48},{48,32},{64,80},{80,64},{96,112},{112,96},{1... | collective-permute-start | bytes 1769480 | tf_op jit(solution)/shard_map/ppermute | solution.py:320
  17.7 2.9 collective-permute-start.3
  22.1 24.6 %copy.17 = bf16[192,384,128]{1,0,2:T(8,128)(2,1)} copy(bf16[192,384,128]{2,1,0:T(8,128)(2,1)} %param.19) | data formatting | bytes 37748736 | tf_op args[9]
  53.3 9.3 %collective-permute-done.2 = bf16[2,192,384]{2,1,0:T(8,128)(2,1)S(1)} collective-permute-done((bf16[2,192,384]{2,1,0:T(8,128)(2,1)S(1)}, bf16[2,192,384]{2,1,0:T(8,128)(2,1)S(1)}, u32[]{:S(2)}, u32[]{:S(2)}) %collective-permute-start.2) | collective-permute-done | bytes 294944 | tf_op jit(solution)/shard_map/ppermute | solution.py:316
  64.0 3.5 %collective-permute-start.8 = (bf16[2,2,192,384]{3,2,1,0:T(8,128)(2,1)S(1)}, bf16[2,2,192,384]{3,2,1,0:T(8,128)(2,1)S(1)}, u32[]{:S(2)}, u32[]{:S(2)}) collective-permute-start(bf16[2,2,192,384]{3,2,1,0:T(8,128)(2,1)S(1)} %pad_maximum_fusion.refs_7_.refs_8_), channel_id=1, source_target_pairs={{0,64},{16,80},{32,96},{48,112},{64,0},{80,16},{96,32},{112,48},{1... | collective-permute-start | bytes 1769480 | tf_op jit(solution)/shard_map/ppermute | solution.py:316
  68.0 23.4 %attention_rows.4 = (bf16[4,192,128]{2,1,0:T(8,128)(2,1)}, bf16[4,192,128]{2,1,0:T(8,128)(2,1)}, bf16[4,64,3072]{2,1,0:T(8,128)(2,1)}, bf16[4,64,3072]{2,1,0:T(8,128)(2,1)}, f32[2,192,3072]{2,1,0:T(8,128)}) custom-call(s32[8]{0:T(128)} %stack.113.order_ref, bf16[4,192,128]{2,1,0:T(8,128)(2,1)} %get-tuple-element.211.refs_0_, ...), custom_call_target="tpu_custom_call" | custom-call | flops 9663676416 | bytes 30000000 | tf_op jit(solution)/shard_map/attention_rows/pallas_call | solution.py:235
  94.3 24.9 %attention_rows.5 = (bf16[4,192,128]{2,1,0:T(8,128)(2,1)}, bf16[4,192,128]{2,1,0:T(8,128)(2,1)}, bf16[16,8,192,128]{3,2,1,0:T(8,128)(2,1)}, bf16[4,128,192]{2,1,0:T(8,128)(2,1)}, f32[2,192,3072]{2,1,0:T(8,128)}) custom-call(s32[8]{0:T(128)} %stack.113.order_ref, bf16[4,192,128]{2,1,0:T(8,128)(2,1)} %get-tuple-element.211.refs_0_, ...), custom_call_target="tpu_custom_call" | custom-call | flops 9663676416 | bytes 30000000 | tf_op jit(solution)/shard_map/attention_rows/pallas_call | solution.py:235
  122.0 24.4 %attention_rows.6 = (bf16[4,192,128]{2,1,0:T(8,128)(2,1)}, bf16[4,192,128]{2,1,0:T(8,128)(2,1)}, bf16[4,64,3072]{2,1,0:T(8,128)(2,1)}, bf16[4,64,3072]{2,1,0:T(8,128)(2,1)}, bf16[8,2,192,384]{3,2,1,0:T(8,128)(2,1)}) custom-call(s32[8]{0:T(128)} %stack.113.order_ref, bf16[4,192,128]{2,1,0:T(8,128)(2,1)} %get-tuple-element.215.refs_0_, ...), custom_call_target="tpu_custom_call" | custom-call | flops 9663676416 | bytes 30000000 | tf_op jit(solution)/shard_map/attention_rows/pallas_call | solution.py:235
  146.7 3.3 collective-permute-start.14
  154.0 25.9 %attention_rows.7 = (bf16[4,192,128]{2,1,0:T(8,128)(2,1)}, bf16[4,192,128]{2,1,0:T(8,128)(2,1)}, bf16[16,8,192,128]{3,2,1,0:T(8,128)(2,1)}, bf16[4,128,192]{2,1,0:T(8,128)(2,1)}, bf16[8,2,192,384]{3,2,1,0:T(8,128)(2,1)}) custom-call(s32[8]{0:T(128)} %stack.113.order_ref, bf16[4,192,128]{2,1,0:T(8,128)(2,1)} %get-tuple-element.215.refs_0_, ...), custom_call_target="tpu_custom_call" | custom-call | flops 9663676416 | bytes 30000000 | tf_op jit(solution)/shard_map/attention_rows/pallas_call | solution.py:235
  180.0 3.6 %collective-permute-start.11 = (bf16[4,128,192]{2,1,0:T(8,128)(2,1)}, bf16[4,128,192]{2,1,0:T(8,128)(2,1)}, u32[]{:S(2)}, u32[]{:S(2)}) collective-permute-start(bf16[4,128,192]{2,1,0:T(8,128)(2,1)} %get-tuple-element.94), channel_id=1, source_target_pairs={{0,16},{16,0},{32,48},{48,32},{64,80},{80,64},{96,112},{112,96},{1... | collective-permute-start | bytes 589832 | tf_op jit(solution)/shard_map/ppermute | solution.py:320
  183.6 2.7 collective-permute-start.12
  186.3 15.8 %reduce-scatter.3.cloned.1.call-done = bf16[1,8,192,128]{3,2,1,0:T(8,128)(2,1)} async-done(((bf16[16,8,192,128]{3,2,1,0:T(8,128)(2,1)}), bf16[1,8,192,128]{3,2,1,0:T(8,128)(2,1)}) %reduce-scatter.3.cloned.1.call-update) | async-done | bytes 393232 | tf_op jit(solution)/shard_map/reduce_scatter | solution.py:423
  202.1 17.0 %left_product.2 = (bf16[8,2,384,128]{3,2,1,0:T(8,128)(2,1)}, bf16[8,2,384,128]{3,2,1,0:T(8,128)(2,1)}) custom-call(s32[8]{0:T(128)} %stack.113.order_ref, s32[16]{0:T(128)} %stack.136.cols_ref, bf16[2,4,128,192]{3,2,1,0:T(8,128)(2,1)} %copy-done.5, bf16[2,4,128,192]{3,2,1,0:T(8,128)(2,1)} %copy-done.5, ...), custom_call_target="tpu_custom_call" | custom-call | flops 40000000000 | bytes 30000000 | tf_op jit(solution)/shard_map/left_product/pallas_call | solution.py:296
  220.4 3.3 %collective-permute-start.21 = (bf16[2,4,128,192]{3,2,1,0:T(8,128)(2,1)S(1)}, bf16[2,4,128,192]{3,2,1,0:T(8,128)(2,1)S(1)}, u32[]{:S(2)}, u32[]{:S(2)}) collective-permute-start(bf16[2,4,128,192]{3,2,1,0:T(8,128)(2,1)S(1)} %pad_maximum_fusion.4.refs_0_.refs_1_), channel_id=1, source_target_pairs={{0,64},{16,80},{32,96},{48,112},{64,0},{80,16},{96,32},{112,48},{1... | collective-permute-start | bytes 1179656 | tf_op jit(solution)/shard_map/ppermute | solution.py:316
  227.8 2.7 collective-permute-start.24
  232.9 14.2 %collective-permute-done.20.refs_2_.refs_3_ = bf16[2,4,128,192]{3,2,1,0:T(8,128)(2,1)S(1)} collective-permute-done((bf16[2,4,128,192]{3,2,1,0:T(8,128)(2,1)S(1)}, bf16[2,4,128,192]{3,2,1,0:T(8,128)(2,1)S(1)}, u32[]{:S(2)}, u32[]{:S(2)}) %collective-permute-start.20) | collective-permute-done | bytes 393248 | tf_op jit(solution)/shard_map/ppermute | solution.py:316
  254.0 17.0 %left_product.3 = (bf16[8,2,384,128]{3,2,1,0:T(8,128)(2,1)}, bf16[8,2,384,128]{3,2,1,0:T(8,128)(2,1)}) custom-call(s32[8]{0:T(128)} %stack.113.order_ref, s32[16]{0:T(128)} %stack.136.cols_ref, bf16[2,4,128,192]{3,2,1,0:T(8,128)(2,1)} %copy-done.4, bf16[2,4,128,192]{3,2,1,0:T(8,128)(2,1)} %copy-done.4, bf16[2,4,128,192]{3,2,1,0:T(8,128)(2,1)} %copy-done.22, ...), custom_call_target="tpu_custom_call" | custom-call | flops 40000000000 | bytes 30000000 | tf_op jit(solution)/shard_map/left_product/pallas_call | solution.py:296
  270.9 7.6 %collective-permute-done.25 = bf16[2,2,192,384]{3,2,1,0:T(8,128)(2,1)} collective-permute-done((bf16[2,2,192,384]{3,2,1,0:T(8,128)(2,1)}, bf16[2,2,192,384]{3,2,1,0:T(8,128)(2,1)}, u32[]{:S(2)}, u32[]{:S(2)}) %collective-permute-start.25) | collective-permute-done | bytes 589856 | tf_op jit(solution)/shard_map/ppermute | solution.py:316
  278.5 3.3 collective-permute-done.27
  288.2 2.8 collective-permute-start.34
  299.1 5.0 %collective-permute-done.30 = bf16[2,2,384,128]{3,2,1,0:T(8,128)(2,1)S(1)} collective-permute-done((bf16[2,2,384,128]{3,2,1,0:T(8,128)(2,1)S(1)}, bf16[2,2,384,128]{3,2,1,0:T(8,128)(2,1)S(1)}, u32[]{:S(2)}, u32[]{:S(2)}) %collective-permute-start.30) | collective-permute-done | bytes 393248 | tf_op jit(solution)/shard_map/ppermute | solution.py:348
  304.9 8.4 %collective-permute-done.32 = bf16[2,2,384,128]{3,2,1,0:T(8,128)(2,1)S(1)} collective-permute-done((bf16[2,2,384,128]{3,2,1,0:T(8,128)(2,1)S(1)}, bf16[2,2,384,128]{3,2,1,0:T(8,128)(2,1)S(1)}, u32[]{:S(2)}, u32[]{:S(2)}) %collective-permute-start.32) | collective-permute-done | bytes 393248 | tf_op jit(solution)/shard_map/ppermute | solution.py:348
  314.0 5.8 %collective-permute-done.33 = bf16[2,384,128]{2,1,0:T(8,128)(2,1)S(1)} collective-permute-done((bf16[2,384,128]{2,1,0:T(8,128)(2,1)S(1)}, bf16[2,384,128]{2,1,0:T(8,128)(2,1)S(1)}, u32[]{:S(2)}, u32[]{:S(2)}) %collective-permute-start.33) | collective-permute-done | bytes 196640 | tf_op jit(solution)/shard_map/ppermute | solution.py:352
  (173 shorter events, 61.3 us)
Async XLA Ops:
  7.2 60.8 %all-gather.5.cloned.1.call-start = ((), (), s32[]{:S(2)}) async-start(), calls=%async_computation.4 | async-start | bytes 6684672 | tf_op jit(solution)/shard_map/all_gather | solution.py:409
  9.3 112.6 %all-gather.7.cloned.1.call-start = ((), (), s32[]{:S(2)}) async-start(), calls=%async_computation.5 | async-start | bytes 6684672 | tf_op jit(solution)/shard_map/all_gather | solution.py:409
  10.2 191.8 %reduce-scatter.3.cloned.1.call-start = ((), (), s32[]{:S(2)}) async-start(), calls=%async_computation.2 | async-start | bytes 6684672 | tf_op jit(solution)/shard_map/reduce_scatter | solution.py:423
  11.2 35.5 %collective-permute-start = (bf16[4,192,384]{2,1,0:T(8,128)(2,1)S(1)}, bf16[4,192,384]{2,1,0:T(8,128)(2,1)S(1)}, u32[]{:S(2)}, u32[]{:S(2)}) collective-permute-start(bf16[4,192,384]{2,1,0:T(8,128)(2,1)S(1)} %add_convert_fusion.4), channel_id=1, source_target_pairs={{0,16},{16,0},{32,48},{48,32},{64,80},{80,64},{96,112},{112,96},{1... | collective-permute-start | bytes 1769480 | tf_op jit(solution)/shard_map/ppermute | solution.py:320
  16.1 32.9 %collective-permute-start.1 = (bf16[2,192,384]{2,1,0:T(8,128)(2,1)}, bf16[2,192,384]{2,1,0:T(8,128)(2,1)}, u32[]{:S(2)}, u32[]{:S(2)}) collective-permute-start(bf16[2,192,384]{2,1,0:T(8,128)(2,1)} %get-tuple-element.161), channel_id=1, source_target_pairs={{0,32},{16,48},{32,64},{48,80},{64,96},{80,112},{96,0},{112,16},{1... | collective-permute-start | bytes 884744 | tf_op jit(solution)/shard_map/ppermute | solution.py:316
  17.7 35.6 %collective-permute-start.3 = (bf16[2,192,384]{2,1,0:T(8,128)(2,1)}, bf16[2,192,384]{2,1,0:T(8,128)(2,1)}, u32[]{:S(2)}, u32[]{:S(2)}) collective-permute-start(bf16[2,192,384]{2,1,0:T(8,128)(2,1)} %get-tuple-element.161), channel_id=1, source_target_pairs={{0,64},{16,80},{32,96},{48,112},{64,0},{80,16},{96,32},{112,48},{1... | collective-permute-start | bytes 884744 | tf_op jit(solution)/shard_map/ppermute | solution.py:316
  20.6 32.7 %collective-permute-start.5 = (bf16[2,192,384]{2,1,0:T(8,128)(2,1)}, bf16[2,192,384]{2,1,0:T(8,128)(2,1)}, u32[]{:S(2)}, u32[]{:S(2)}) collective-permute-start(bf16[2,192,384]{2,1,0:T(8,128)(2,1)} %get-tuple-element.161), channel_id=1, source_target_pairs={{0,96},{16,112},{32,0},{48,16},{64,32},{80,48},{96,64},{112,80},{1... | collective-permute-start | bytes 884744 | tf_op jit(solution)/shard_map/ppermute | solution.py:316
  63.3 28.1 %collective-permute-start.7 = (bf16[2,2,192,384]{3,2,1,0:T(8,128)(2,1)S(1)}, bf16[2,2,192,384]{3,2,1,0:T(8,128)(2,1)S(1)}, u32[]{:S(2)}, u32[]{:S(2)}) collective-permute-start(bf16[2,2,192,384]{3,2,1,0:T(8,128)(2,1)S(1)} %pad_maximum_fusion.refs_7_.refs_8_), channel_id=1, source_target_pairs={{0,32},{16,48},{32,64},{48,80},{64,96},{80,112},{96,0},{112,16},{1... | collective-permute-start | bytes 1769480 | tf_op jit(solution)/shard_map/ppermute | solution.py:316
  64.0 29.3 %collective-permute-start.8 = (bf16[2,2,192,384]{3,2,1,0:T(8,128)(2,1)S(1)}, bf16[2,2,192,384]{3,2,1,0:T(8,128)(2,1)S(1)}, u32[]{:S(2)}, u32[]{:S(2)}) collective-permute-start(bf16[2,2,192,384]{3,2,1,0:T(8,128)(2,1)S(1)} %pad_maximum_fusion.refs_7_.refs_8_), channel_id=1, source_target_pairs={{0,64},{16,80},{32,96},{48,112},{64,0},{80,16},{96,32},{112,48},{1... | collective-permute-start | bytes 1769480 | tf_op jit(solution)/shard_map/ppermute | solution.py:316
  67.4 25.9 %collective-permute-start.9 = (bf16[2,2,192,384]{3,2,1,0:T(8,128)(2,1)S(1)}, bf16[2,2,192,384]{3,2,1,0:T(8,128)(2,1)S(1)}, u32[]{:S(2)}, u32[]{:S(2)}) collective-permute-start(bf16[2,2,192,384]{3,2,1,0:T(8,128)(2,1)S(1)} %pad_maximum_fusion.refs_7_.refs_8_), channel_id=1, source_target_pairs={{0,96},{16,112},{32,0},{48,16},{64,32},{80,48},{96,64},{112,80},{1... | collective-permute-start | bytes 1769480 | tf_op jit(solution)/shard_map/ppermute | solution.py:316
  119.3 202.5 %reduce-scatter.5.cloned.1.call-start = ((), (), s32[]{:S(2)}) async-start(), calls=%async_computation.3 | async-start | bytes 6684672 | tf_op jit(solution)/shard_map/reduce_scatter | solution.py:432
  146.6 33.4 %collective-permute-start.13 = (bf16[2,4,128,192]{3,2,1,0:T(8,128)(2,1)S(1)}, bf16[2,4,128,192]{3,2,1,0:T(8,128)(2,1)}, u32[]{:S(2)}, u32[]{:S(2)}) collective-permute-start(bf16[2,4,128,192]{3,2,1,0:T(8,128)(2,1)S(1)} %pad_maximum_fusion.3.refs_0_.refs_1_), channel_id=1, source_target_pairs={{0,32},{16,48},{32,64},{48,80},{64,96},{80,112},{96,0},{112,16},{1... | collective-permute-start | bytes 1179656 | tf_op jit(solution)/shard_map/ppermute | solution.py:316
  146.7 36.9 %collective-permute-start.14 = (bf16[2,4,128,192]{3,2,1,0:T(8,128)(2,1)S(1)}, bf16[2,4,128,192]{3,2,1,0:T(8,128)(2,1)}, u32[]{:S(2)}, u32[]{:S(2)}) collective-permute-start(bf16[2,4,128,192]{3,2,1,0:T(8,128)(2,1)S(1)} %pad_maximum_fusion.3.refs_0_.refs_1_), channel_id=1, source_target_pairs={{0,64},{16,80},{32,96},{48,112},{64,0},{80,16},{96,32},{112,48},{1... | collective-permute-start | bytes 1179656 | tf_op jit(solution)/shard_map/ppermute | solution.py:316
  150.0 36.2 %collective-permute-start.15 = (bf16[2,4,128,192]{3,2,1,0:T(8,128)(2,1)S(1)}, bf16[2,4,128,192]{3,2,1,0:T(8,128)(2,1)}, u32[]{:S(2)}, u32[]{:S(2)}) collective-permute-start(bf16[2,4,128,192]{3,2,1,0:T(8,128)(2,1)S(1)} %pad_maximum_fusion.3.refs_0_.refs_1_), channel_id=1, source_target_pairs={{0,96},{16,112},{32,0},{48,16},{64,32},{80,48},{96,64},{112,80},{1... | collective-permute-start | bytes 1179656 | tf_op jit(solution)/shard_map/ppermute | solution.py:316
  151.7 34.6 %collective-permute-start.16 = (bf16[2,2,192,384]{3,2,1,0:T(8,128)(2,1)S(1)}, bf16[2,2,192,384]{3,2,1,0:T(8,128)(2,1)S(1)}, u32[]{:S(2)}, u32[]{:S(2)}) collective-permute-start(bf16[2,2,192,384]{3,2,1,0:T(8,128)(2,1)S(1)} %get-tuple-element.145), channel_id=1, source_target_pairs={{0,96},{16,112},{32,0},{48,16},{64,32},{80,48},{96,64},{112,80},{1... | collective-permute-start | bytes 1769480 | tf_op jit(solution)/shard_map/ppermute | solution.py:316
  152.6 33.7 %collective-permute-start.17 = (bf16[2,2,192,384]{3,2,1,0:T(8,128)(2,1)S(1)}, bf16[2,2,192,384]{3,2,1,0:T(8,128)(2,1)S(1)}, u32[]{:S(2)}, u32[]{:S(2)}) collective-permute-start(bf16[2,2,192,384]{3,2,1,0:T(8,128)(2,1)S(1)} %get-tuple-element.144), channel_id=1, source_target_pairs={{0,32},{16,48},{32,64},{48,80},{64,96},{80,112},{96,0},{112,16},{1... | collective-permute-start | bytes 1769480 | tf_op jit(solution)/shard_map/ppermute | solution.py:316
  180.0 39.1 %collective-permute-start.11 = (bf16[4,128,192]{2,1,0:T(8,128)(2,1)}, bf16[4,128,192]{2,1,0:T(8,128)(2,1)}, u32[]{:S(2)}, u32[]{:S(2)}) collective-permute-start(bf16[4,128,192]{2,1,0:T(8,128)(2,1)} %get-tuple-element.94), channel_id=1, source_target_pairs={{0,16},{16,0},{32,48},{48,32},{64,80},{80,64},{96,112},{112,96},{1... | collective-permute-start | bytes 589832 | tf_op jit(solution)/shard_map/ppermute | solution.py:320
  183.6 35.5 %collective-permute-start.12 = (bf16[2,2,192,384]{3,2,1,0:T(8,128)(2,1)S(1)}, bf16[2,2,192,384]{3,2,1,0:T(8,128)(2,1)}, u32[]{:S(2)}, u32[]{:S(2)}) collective-permute-start(bf16[2,2,192,384]{3,2,1,0:T(8,128)(2,1)S(1)} %get-tuple-element.146), channel_id=1, source_target_pairs={{0,64},{16,80},{32,96},{48,112},{64,0},{80,16},{96,32},{112,48},{1... | collective-permute-start | bytes 1769480 | tf_op jit(solution)/shard_map/ppermute | solution.py:316
  220.3 26.8 %collective-permute-start.20 = (bf16[2,4,128,192]{3,2,1,0:T(8,128)(2,1)S(1)}, bf16[2,4,128,192]{3,2,1,0:T(8,128)(2,1)S(1)}, u32[]{:S(2)}, u32[]{:S(2)}) collective-permute-start(bf16[2,4,128,192]{3,2,1,0:T(8,128)(2,1)S(1)} %pad_maximum_fusion.4.refs_0_.refs_1_), channel_id=1, source_target_pairs={{0,32},{16,48},{32,64},{48,80},{64,96},{80,112},{96,0},{112,16},{1... | collective-permute-start | bytes 1179656 | tf_op jit(solution)/shard_map/ppermute | solution.py:316
  220.4 26.7 %collective-permute-start.21 = (bf16[2,4,128,192]{3,2,1,0:T(8,128)(2,1)S(1)}, bf16[2,4,128,192]{3,2,1,0:T(8,128)(2,1)S(1)}, u32[]{:S(2)}, u32[]{:S(2)}) collective-permute-start(bf16[2,4,128,192]{3,2,1,0:T(8,128)(2,1)S(1)} %pad_maximum_fusion.4.refs_0_.refs_1_), channel_id=1, source_target_pairs={{0,64},{16,80},{32,96},{48,112},{64,0},{80,16},{96,32},{112,48},{1... | collective-permute-start | bytes 1179656 | tf_op jit(solution)/shard_map/ppermute | solution.py:316
  250.4 28.2 %collective-permute-start.25 = (bf16[2,2,192,384]{3,2,1,0:T(8,128)(2,1)}, bf16[2,2,192,384]{3,2,1,0:T(8,128)(2,1)}, u32[]{:S(2)}, u32[]{:S(2)}) collective-permute-start(bf16[2,2,192,384]{3,2,1,0:T(8,128)(2,1)} %get-tuple-element.142), channel_id=1, source_target_pairs={{0,96},{16,112},{32,0},{48,16},{64,32},{80,48},{96,64},{112,80},{1... | collective-permute-start | bytes 1769480 | tf_op jit(solution)/shard_map/ppermute | solution.py:316
  253.0 25.6 %collective-permute-start.26 = (bf16[2,2,192,384]{3,2,1,0:T(8,128)(2,1)S(1)}, bf16[2,2,192,384]{3,2,1,0:T(8,128)(2,1)}, u32[]{:S(2)}, u32[]{:S(2)}) collective-permute-start(bf16[2,2,192,384]{3,2,1,0:T(8,128)(2,1)S(1)} %get-tuple-element.141), channel_id=1, source_target_pairs={{0,64},{16,80},{32,96},{48,112},{64,0},{80,16},{96,32},{112,48},{1... | collective-permute-start | bytes 1769480 | tf_op jit(solution)/shard_map/ppermute | solution.py:316
  253.0 28.8 %collective-permute-start.27 = (bf16[2,2,192,384]{3,2,1,0:T(8,128)(2,1)S(1)}, bf16[2,2,192,384]{3,2,1,0:T(8,128)(2,1)}, u32[]{:S(2)}, u32[]{:S(2)}) collective-permute-start(bf16[2,2,192,384]{3,2,1,0:T(8,128)(2,1)S(1)} %get-tuple-element.140), channel_id=1, source_target_pairs={{0,32},{16,48},{32,64},{48,80},{64,96},{80,112},{96,0},{112,16},{1... | collective-permute-start | bytes 1769480 | tf_op jit(solution)/shard_map/ppermute | solution.py:316
  288.2 25.8 %collective-permute-start.34 = (bf16[4,192,384]{2,1,0:T(8,128)(2,1)S(1)}, bf16[4,192,384]{2,1,0:T(8,128)(2,1)S(1)}, u32[]{:S(2)}, u32[]{:S(2)}) collective-permute-start(bf16[4,192,384]{2,1,0:T(8,128)(2,1)S(1)} %pad_maximum_fusion.1), channel_id=1, source_target_pairs={{0,16},{16,0},{32,48},{48,32},{64,80},{80,64},{96,112},{112,96},{1... | collective-permute-start | bytes 1769480 | tf_op jit(solution)/shard_map/ppermute | solution.py:320
  (42 other events, 432.0 us)
Sparse Core Ops, SparseCore 0:
  10.3 50.1 all-gather.4
  62.8 41.5 all-gather.6
  119.4 82.5 reduce-scatter.2
  204.3 81.1 reduce-scatter.4

commit v6 on v5

--- a/solution.py
+++ b/solution.py
@@ -356,6 +356,14 @@
     return add_pair(total[0], z_swap(total))
 
 
+def z_first(part):
+    part = part.reshape((4, 2) + part.shape[1:])
+    got = lax.ppermute(part[:, 1], "col", [(c, c ^ 2) for c in range(16)])
+    half = add_pair(part[:, 0], got)
+    moved = [lax.ppermute(half[dx], "col", [(c, (c + 4 * dx) % 16) for c in range(16)]) for dx in (1, 3, 2)]
+    return add_all([half[0]] + moved)
+
+
 def after(x, *done):
     return lax.optimization_barrier((x, done))[0]
 
@@ -433,29 +441,32 @@
     pairs0, near0 = after((pairs0, bias0[1:4:2]), gq1)
     order_l, car1 = lax.optimization_barrier((order, car1))
     swap1 = row_swap(car1)
-    left0 = left_product(after(order_l, pairs0, near0), cols, pairs0, right_t)
-    swap1, far0, left0, sum0 = lax.optimization_barrier((swap1, bias0[2], left0, sum0))
+    swap1, sum0, pairs0, near0 = lax.optimization_barrier((swap1, sum0, pairs0, near0))
     pair1 = jnp.stack([car1, swap1])
     pairs1 = [pair1] + row_shifts(pair1)
-    part_l0 = add_pair(left0[0], core_swap(left0[1]))
-    near_l0 = [x_shift(part_l0, 1), x_shift(part_l0, 3)]
+    left0 = left_product(after(order_l, pair1), cols, pairs0, right_t)
+    pairs1, far0, left0, bias1 = lax.optimization_barrier((pairs1, bias0[2], left0, d[-1]))
     bias0 = add_all([bias0[0], far0] + list(near0))
-    pairs1, near_l0, bias1, bias0 = lax.optimization_barrier((pairs1, near_l0, d[-1], bias0))
-    far_l0 = x_shift(part_l0, 2)
+    got_l0 = core_swap(left0[1])
     bias1 = row_parts(bias1)
-    left1 = left_product(after(order, pairs1, near_l0), cols, pairs1, right_t)
-    far_l0, bias1, left1 = lax.optimization_barrier((far_l0, bias1, left1))
-    part_l1 = add_pair(left1[0], core_swap(left1[1]))
-    shifts_l1 = [x_shift(part_l1, dx) for dx in (1, 3, 2)]
-    sum_l0 = add_all([part_l0[0:2], far_l0] + near_l0)
-    bias1 = add_all(bias1)
-    bias_keep, bias_send = [jnp.concatenate([bias0[z], bias1[z]]) for z in range(2)]
-    got_l0, got_bias = z_swap(sum_l0), row_swap(bias_send)
-    sum_l1 = add_all([part_l1[0:2]] + shifts_l1)
-    got_l1 = z_swap(sum_l1)
-    left = jnp.concatenate([add_pair(sum_l0[0], got_l0), add_pair(sum_l1[0], got_l1)])
-    got_bias, bias_keep = after((got_bias, bias_keep), got_l1)
-    grad_bias = bias_keep.astype(F32) + got_bias.astype(F32)
+    got_bias0 = row_swap(bias0[1])
+    left1 = left_product(after(order, pairs1, bias0), cols, pairs1, right_t)
+    got_l0, bias1[1], bias1[3], got_bias0, left1, late1 = lax.optimization_barrier(
+        (got_l0, bias1[1], bias1[3], got_bias0, left1, d[-1])
+    )
+    bias1[2] = row_parts(late1)[2]
+    got_l1 = core_swap(left1[1])
+    part_l0 = add_pair(left0[0], got_l0)
+    shifts_l0 = [x_shift(part_l0, dx) for dx in (1, 3, 2)]
+    part_l1 = add_pair(left1[0], got_l1)
+    bias1 = add_all(after(bias1, part_l1))
+    sum_l1 = z_first(part_l1)
+    sum_l0 = z_sum(add_all([part_l0[0:2]] + shifts_l0))
+    left = jnp.concatenate([sum_l0, sum_l1])
+    got_bias1 = after(row_swap(bias1[1]), sum_l1)
+    grad_bias = jnp.concatenate(
+        [bias0[0].astype(F32) + got_bias0.astype(F32), bias1[0].astype(F32) + got_bias1.astype(F32)]
+    )
     sum0, sum1 = after((sum0, sum1), left)
 
     def untake(a, b):

time: 337 us -> 336 us (level)
  starting transfers between devices: 51.1 us -> 60.8 us
  waiting for transfers between devices: 73.5 us -> 64.4 us
    ppermute x21, waiting for transfers between devices: 37.6 us -> 18.5 us  [row_shift(): lax.ppermute(x, 'row', [(2 * y + z, 2 * ((y + dy) % 4) + z) for y in rang...]
    ppermute x0 -> x4, waiting for transfers between devices: none -> 18.2 us  [the longest x1 11.1 us: z_first(): got = lax.ppermute(part[:, 1], 'col', [(c, c ^ 2) for c in range(16)])]
    reduce_scatter x1, waiting for transfers between devices: 15.8 us -> 2.42 us  [local(): sum0 = lax.psum_scatter(dkv, 'col', scatter_dimension=0)]
    ppermute x4 -> x5, waiting for transfers between devices: 0.01 us -> 10.3 us  [row_swap(): return lax.ppermute(x, 'row', [(r, r ^ 1) for r in range(8)])]
    ppermute x2 -> x1, starting transfers between devices: 1.12 us -> 8.73 us  [z_swap(): return lax.ppermute(total[1], 'col', [(c, c ^ 2) for c in range(16)])]
    ppermute x2 -> x1, waiting for transfers between devices: 5.82 us -> 0.52 us  [z_swap(): return lax.ppermute(total[1], 'col', [(c, c ^ 2) for c in range(16)])]
    ppermute x6 -> x3, starting transfers between devices: 9.58 us -> 4.62 us  [x_shift(): lax.ppermute(part[2 * dx:2 * dx + 2], 'col', [(c, (c + 4 * dx) % 16) for...]
    ppermute x0 -> x4, starting transfers between devices: none -> 3.51 us  [the longest x3 3.43 us: z_first(): lax.ppermute(half[dx], 'col', [(c, (c + 4 * dx) % 16) for c in range(16)])]
  transfers between devices with their start and end apart: 39 -> 40, of which waited for: 12 -> 12; matrix products, arithmetic and copies ran while one was open for 16% -> 15% of each run, Pallas kernels for 40% -> 40%
where the time goes in v6:
time: 336 us; the launch traced here: 330 us
  Pallas kernels  133 us (40%)
  waiting for transfers between devices  64.4 us (19%)
  starting transfers between devices  60.8 us (18%)
  local copies, waits for them, and re-layouts  38.2 us (11%)
  other arithmetic  19.3 us (6%)
  between operations  14.8 us (4%)
    pallas_call x4, Pallas kernels, attention(): pl.pallas_call(functools.partial(attention_kernel, h0, heads, total_heads...  98.9 us
    pallas_call x2, Pallas kernels, left_product(): pl.pallas_call(left_kernel, grid_spec=pltpu.PrefetchScalarGridSpec(num_sc...  33.9 us
    ppermute x21, starting transfers between devices, row_shift(): lax.ppermute(x, 'row', [(2 * y + z, 2 * ((y + dy) % 4) + z) for y in rang...  29.8 us
    unnamed x49, local copies, waits for them, and re-layouts  26.6 us
    ppermute x21, waiting for transfers between devices, row_shift(): lax.ppermute(x, 'row', [(2 * y + z, 2 * ((y + dy) % 4) + z) for y in rang...  18.5 us
    ppermute x3, waiting for transfers between devices, x_shift(): lax.ppermute(part[2 * dx:2 * dx + 2], 'col', [(c, (c + 4 * dx) % 16) for...  14.3 us
    ppermute x5, starting transfers between devices, row_swap(): return lax.ppermute(x, 'row', [(r, r ^ 1) for r in range(8)])  13.2 us
    ppermute x1, waiting for transfers between devices, z_first(): got = lax.ppermute(part[:, 1], 'col', [(c, c ^ 2) for c in range(16)])  11.1 us
  transfers between devices with their start and end apart: 40, of which 12 were waited for; matrix products, arithmetic and copies ran while one was open for 15% of the time, Pallas kernels for 40%

profile of v6, /device:TPU:0, one launch (start us, length us, event | category | flops | bytes accessed | tf_op | source)
XLA Modules:
  0.0 330.3 jit_solution(18300694986516738071)
XLA Ops:
  11.2 4.0 %collective-permute-start = (bf16[4,192,384]{2,1,0:T(8,128)(2,1)S(1)}, bf16[4,192,384]{2,1,0:T(8,128)(2,1)S(1)}, u32[]{:S(2)}, u32[]{:S(2)}) collective-permute-start(bf16[4,192,384]{2,1,0:T(8,128)(2,1)S(1)} %add_convert_fusion.4), channel_id=1, source_target_pairs={{0,16},{16,0},{32,48},{48,32},{64,80},{80,64},{96,112},{112,96},{1... | collective-permute-start | bytes 1769480 | tf_op jit(solution)/shard_map/ppermute | solution.py:320
  22.1 24.7 %copy.19 = bf16[192,384,128]{1,0,2:T(8,128)(2,1)} copy(bf16[192,384,128]{2,1,0:T(8,128)(2,1)} %param.19) | data formatting | bytes 37748736 | tf_op args[9]
  53.4 9.3 %collective-permute-done.2 = bf16[2,192,384]{2,1,0:T(8,128)(2,1)S(1)} collective-permute-done((bf16[2,192,384]{2,1,0:T(8,128)(2,1)S(1)}, bf16[2,192,384]{2,1,0:T(8,128)(2,1)S(1)}, u32[]{:S(2)}, u32[]{:S(2)}) %collective-permute-start.2) | collective-permute-done | bytes 294944 | tf_op jit(solution)/shard_map/ppermute | solution.py:316
  64.0 3.5 %collective-permute-start.8 = (bf16[2,2,192,384]{3,2,1,0:T(8,128)(2,1)S(1)}, bf16[2,2,192,384]{3,2,1,0:T(8,128)(2,1)S(1)}, u32[]{:S(2)}, u32[]{:S(2)}) collective-permute-start(bf16[2,2,192,384]{3,2,1,0:T(8,128)(2,1)S(1)} %pad_maximum_fusion.1.refs_7_.refs_8_), channel_id=1, source_target_pairs={{0,64},{16,80},{32,96},{48,112},{64,0},{80,16},{96,32},{112,48},{1... | collective-permute-start | bytes 1769480 | tf_op jit(solution)/shard_map/ppermute | solution.py:316
  68.0 23.4 %attention_rows.4 = (bf16[4,192,128]{2,1,0:T(8,128)(2,1)}, bf16[4,192,128]{2,1,0:T(8,128)(2,1)}, bf16[4,64,3072]{2,1,0:T(8,128)(2,1)}, bf16[4,64,3072]{2,1,0:T(8,128)(2,1)}, f32[2,192,3072]{2,1,0:T(8,128)}) custom-call(s32[8]{0:T(128)} %stack.113.order_ref, bf16[4,192,128]{2,1,0:T(8,128)(2,1)} %get-tuple-element.218.refs_0_, ...), custom_call_target="tpu_custom_call" | custom-call | flops 9663676416 | bytes 30000000 | tf_op jit(solution)/shard_map/attention_rows/pallas_call | solution.py:235
  94.4 24.9 %attention_rows.5 = (bf16[4,192,128]{2,1,0:T(8,128)(2,1)}, bf16[4,192,128]{2,1,0:T(8,128)(2,1)}, bf16[16,8,192,128]{3,2,1,0:T(8,128)(2,1)}, bf16[4,128,192]{2,1,0:T(8,128)(2,1)}, f32[2,192,3072]{2,1,0:T(8,128)}) custom-call(s32[8]{0:T(128)} %stack.113.order_ref, bf16[4,192,128]{2,1,0:T(8,128)(2,1)} %get-tuple-element.218.refs_0_, ...), custom_call_target="tpu_custom_call" | custom-call | flops 9663676416 | bytes 30000000 | tf_op jit(solution)/shard_map/attention_rows/pallas_call | solution.py:235
  121.9 24.4 %attention_rows.6 = (bf16[4,192,128]{2,1,0:T(8,128)(2,1)}, bf16[4,192,128]{2,1,0:T(8,128)(2,1)}, bf16[4,64,3072]{2,1,0:T(8,128)(2,1)}, bf16[4,64,3072]{2,1,0:T(8,128)(2,1)}, bf16[8,2,192,384]{3,2,1,0:T(8,128)(2,1)}) custom-call(s32[8]{0:T(128)} %stack.113.order_ref, bf16[4,192,128]{2,1,0:T(8,128)(2,1)} %get-tuple-element.222.refs_0_, ...), custom_call_target="tpu_custom_call" | custom-call | flops 9663676416 | bytes 30000000 | tf_op jit(solution)/shard_map/attention_rows/pallas_call | solution.py:235
  146.8 3.1 collective-permute-start.13
  153.9 26.1 %attention_rows.7 = (bf16[4,192,128]{2,1,0:T(8,128)(2,1)}, bf16[4,192,128]{2,1,0:T(8,128)(2,1)}, bf16[16,8,192,128]{3,2,1,0:T(8,128)(2,1)}, bf16[4,128,192]{2,1,0:T(8,128)(2,1)}, bf16[8,2,192,384]{3,2,1,0:T(8,128)(2,1)}) custom-call(s32[8]{0:T(128)} %stack.113.order_ref, bf16[4,192,128]{2,1,0:T(8,128)(2,1)} %get-tuple-element.222.refs_0_, ...), custom_call_target="tpu_custom_call" | custom-call | flops 9663676416 | bytes 30000000 | tf_op jit(solution)/shard_map/attention_rows/pallas_call | solution.py:235
  180.1 3.6 %collective-permute-start.11 = (bf16[4,128,192]{2,1,0:T(8,128)(2,1)}, bf16[4,128,192]{2,1,0:T(8,128)(2,1)}, u32[]{:S(2)}, u32[]{:S(2)}) collective-permute-start(bf16[4,128,192]{2,1,0:T(8,128)(2,1)} %get-tuple-element.100), channel_id=1, source_target_pairs={{0,16},{16,0},{32,48},{48,32},{64,80},{80,64},{96,112},{112,96},{1... | collective-permute-start | bytes 589832 | tf_op jit(solution)/shard_map/ppermute | solution.py:320
  187.0 10.3 %collective-permute-done.11 = bf16[4,128,192]{2,1,0:T(8,128)(2,1)} collective-permute-done((bf16[4,128,192]{2,1,0:T(8,128)(2,1)}, bf16[4,128,192]{2,1,0:T(8,128)(2,1)}, u32[]{:S(2)}, u32[]{:S(2)}) %collective-permute-start.11) | collective-permute-done | bytes 196640 | tf_op jit(solution)/shard_map/ppermute | solution.py:320
  201.0 4.4 %collective-permute-start.18 = (bf16[2,4,128,192]{3,2,1,0:T(8,128)(2,1)S(1)}, bf16[2,4,128,192]{3,2,1,0:T(8,128)(2,1)S(1)}, u32[]{:S(2)}, u32[]{:S(2)}) collective-permute-start(bf16[2,4,128,192]{3,2,1,0:T(8,128)(2,1)S(1)} %pad_maximum_fusion.3.refs_0_.refs_1_), channel_id=1, source_target_pairs={{0,64},{16,80},{32,96},{48,112},{64,0},{80,16},{96,32},{112,48},{1... | collective-permute-start | bytes 1179656 | tf_op jit(solution)/shard_map/ppermute | solution.py:316
  205.4 16.9 %left_product.2 = (bf16[8,2,384,128]{3,2,1,0:T(8,128)(2,1)}, bf16[8,2,384,128]{3,2,1,0:T(8,128)(2,1)}) custom-call(s32[8]{0:T(128)} %stack.113.order_ref, s32[16]{0:T(128)} %stack.139.cols_ref, bf16[2,4,128,192]{3,2,1,0:T(8,128)(2,1)} %copy-done.5, bf16[2,4,128,192]{3,2,1,0:T(8,128)(2,1)} %copy-done.5, ...), custom_call_target="tpu_custom_call" | custom-call | flops 40000000000 | bytes 30000000 | tf_op jit(solution)/shard_map/left_product/pallas_call | solution.py:296
  222.3 6.6 %collective-permute-done.18.refs_4_.refs_5_ = bf16[2,4,128,192]{3,2,1,0:T(8,128)(2,1)S(1)} collective-permute-done((bf16[2,4,128,192]{3,2,1,0:T(8,128)(2,1)S(1)}, bf16[2,4,128,192]{3,2,1,0:T(8,128)(2,1)S(1)}, u32[]{:S(2)}, u32[]{:S(2)}) %collective-permute-start.18) | collective-permute-done | bytes 393248 | tf_op jit(solution)/shard_map/ppermute | solution.py:316
  232.2 3.6 %collective-permute-start.24 = (bf16[2,192,384]{2,1,0:T(8,128)(2,1)}, bf16[2,192,384]{2,1,0:T(8,128)(2,1)}, u32[]{:S(2)}, u32[]{:S(2)}) collective-permute-start(bf16[2,192,384]{2,1,0:T(8,128)(2,1)} %slice_bitcast_fusion.5), channel_id=1, source_target_pairs={{0,16},{16,0},{32,48},{48,32},{64,80},{80,64},{96,112},{112,96},{1... | collective-permute-start | bytes 884744 | tf_op jit(solution)/shard_map/ppermute | solution.py:320
  239.1 16.9 %left_product.3 = (bf16[8,2,384,128]{3,2,1,0:T(8,128)(2,1)}, bf16[8,2,384,128]{3,2,1,0:T(8,128)(2,1)}) custom-call(s32[8]{0:T(128)} %stack.113.order_ref, s32[16]{0:T(128)} %stack.139.cols_ref, bf16[2,4,128,192]{3,2,1,0:T(8,128)(2,1)} %copy-done.6, bf16[2,4,128,192]{3,2,1,0:T(8,128)(2,1)} %copy-done.6, bf16[2,4,128,192]{3,2,1,0:T(8,128)(2,1)} %copy-done.20, ...), custom_call_target="tpu_custom_call" | custom-call | flops 40000000000 | bytes 30000000 | tf_op jit(solution)/shard_map/left_product/pallas_call | solution.py:296
  263.4 3.1 collective-permute-start.26
  269.5 7.0 %collective-permute-done.25 = bf16[2,2,384,128]{3,2,1,0:T(8,128)(2,1)S(1)} collective-permute-done((bf16[2,2,384,128]{3,2,1,0:T(8,128)(2,1)S(1)}, bf16[2,2,384,128]{3,2,1,0:T(8,128)(2,1)S(1)}, u32[]{:S(2)}, u32[]{:S(2)}) %collective-permute-start.25) | collective-permute-done | bytes 393248 | tf_op jit(solution)/shard_map/ppermute | solution.py:348
  276.5 4.0 %collective-permute-done.26 = bf16[2,2,384,128]{3,2,1,0:T(8,128)(2,1)S(1)} collective-permute-done((bf16[2,2,384,128]{3,2,1,0:T(8,128)(2,1)S(1)}, bf16[2,2,384,128]{3,2,1,0:T(8,128)(2,1)S(1)}, u32[]{:S(2)}, u32[]{:S(2)}) %collective-permute-start.26) | collective-permute-done | bytes 393248 | tf_op jit(solution)/shard_map/ppermute | solution.py:348
  280.5 3.3 %collective-permute-done.27 = bf16[2,2,384,128]{3,2,1,0:T(8,128)(2,1)S(1)} collective-permute-done((bf16[2,2,384,128]{3,2,1,0:T(8,128)(2,1)S(1)}, bf16[2,2,384,128]{3,2,1,0:T(8,128)(2,1)S(1)}, u32[]{:S(2)}, u32[]{:S(2)}) %collective-permute-start.27) | collective-permute-done | bytes 393248 | tf_op jit(solution)/shard_map/ppermute | solution.py:348
  284.0 8.7 %collective-permute-start.28 = (bf16[2,384,128]{2,1,0:T(8,128)(2,1)S(1)}, bf16[2,384,128]{2,1,0:T(8,128)(2,1)S(1)}, u32[]{:S(2)}, u32[]{:S(2)}) collective-permute-start(bf16[2,384,128]{2,1,0:T(8,128)(2,1)S(1)} %slice_bitcast_fusion.12), channel_id=1, source_target_pairs={{0,2},{1,3},{2,0},{3,1},{4,6},{5,7},{6,4},{7,5},{8,10},{9,11},{10,... | collective-permute-start | bytes 589832 | tf_op jit(solution)/shard_map/ppermute | solution.py:352
  296.1 11.1 %collective-permute-done.30 = bf16[4,2,384,128]{3,2,1,0:T(8,128)(2,1)S(1)} collective-permute-done((bf16[4,2,384,128]{3,2,1,0:T(8,128)(2,1)S(1)}, bf16[4,2,384,128]{3,2,1,0:T(8,128)(2,1)S(1)}, u32[]{:S(2)}, u32[]{:S(2)}) %collective-permute-start.30) | collective-permute-done | bytes 786464 | tf_op jit(solution)/shard_map/ppermute | solution.py:361
  307.6 3.2 collective-permute-start.32
  311.5 7.1 %collective-permute-done.31 = bf16[2,384,128]{2,1,0:T(8,128)(2,1)S(1)} collective-permute-done((bf16[2,384,128]{2,1,0:T(8,128)(2,1)S(1)}, bf16[2,384,128]{2,1,0:T(8,128)(2,1)S(1)}, u32[]{:S(2)}, u32[]{:S(2)}) %collective-permute-start.31) | collective-permute-done | bytes 196640 | tf_op jit(solution)/shard_map/ppermute | solution.py:363
  (170 shorter events, 62.1 us)
Async XLA Ops:
  7.2 60.9 %all-gather.5.cloned.1.call-start = ((), (), s32[]{:S(2)}) async-start(), calls=%async_computation.4 | async-start | bytes 6684672 | tf_op jit(solution)/shard_map/all_gather | solution.py:417
  9.3 112.6 %all-gather.7.cloned.1.call-start = ((), (), s32[]{:S(2)}) async-start(), calls=%async_computation.5 | async-start | bytes 6684672 | tf_op jit(solution)/shard_map/all_gather | solution.py:417
  10.2 189.5 %reduce-scatter.3.cloned.1.call-start = ((), (), s32[]{:S(2)}) async-start(), calls=%async_computation.2 | async-start | bytes 6684672 | tf_op jit(solution)/shard_map/reduce_scatter | solution.py:431
  11.2 35.5 %collective-permute-start = (bf16[4,192,384]{2,1,0:T(8,128)(2,1)S(1)}, bf16[4,192,384]{2,1,0:T(8,128)(2,1)S(1)}, u32[]{:S(2)}, u32[]{:S(2)}) collective-permute-start(bf16[4,192,384]{2,1,0:T(8,128)(2,1)S(1)} %add_convert_fusion.4), channel_id=1, source_target_pairs={{0,16},{16,0},{32,48},{48,32},{64,80},{80,64},{96,112},{112,96},{1... | collective-permute-start | bytes 1769480 | tf_op jit(solution)/shard_map/ppermute | solution.py:320
  16.1 33.2 %collective-permute-start.1 = (bf16[2,192,384]{2,1,0:T(8,128)(2,1)S(1)}, bf16[2,192,384]{2,1,0:T(8,128)(2,1)}, u32[]{:S(2)}, u32[]{:S(2)}) collective-permute-start(bf16[2,192,384]{2,1,0:T(8,128)(2,1)S(1)} %get-tuple-element.168), channel_id=1, source_target_pairs={{0,32},{16,48},{32,64},{48,80},{64,96},{80,112},{96,0},{112,16},{1... | collective-permute-start | bytes 884744 | tf_op jit(solution)/shard_map/ppermute | solution.py:316
  17.6 35.7 %collective-permute-start.3 = (bf16[2,192,384]{2,1,0:T(8,128)(2,1)S(1)}, bf16[2,192,384]{2,1,0:T(8,128)(2,1)}, u32[]{:S(2)}, u32[]{:S(2)}) collective-permute-start(bf16[2,192,384]{2,1,0:T(8,128)(2,1)S(1)} %get-tuple-element.168), channel_id=1, source_target_pairs={{0,64},{16,80},{32,96},{48,112},{64,0},{80,16},{96,32},{112,48},{1... | collective-permute-start | bytes 884744 | tf_op jit(solution)/shard_map/ppermute | solution.py:316
  20.5 32.8 %collective-permute-start.5 = (bf16[2,192,384]{2,1,0:T(8,128)(2,1)S(1)}, bf16[2,192,384]{2,1,0:T(8,128)(2,1)}, u32[]{:S(2)}, u32[]{:S(2)}) collective-permute-start(bf16[2,192,384]{2,1,0:T(8,128)(2,1)S(1)} %get-tuple-element.168), channel_id=1, source_target_pairs={{0,96},{16,112},{32,0},{48,16},{64,32},{80,48},{96,64},{112,80},{1... | collective-permute-start | bytes 884744 | tf_op jit(solution)/shard_map/ppermute | solution.py:316
  63.4 28.1 %collective-permute-start.7 = (bf16[2,2,192,384]{3,2,1,0:T(8,128)(2,1)S(1)}, bf16[2,2,192,384]{3,2,1,0:T(8,128)(2,1)S(1)}, u32[]{:S(2)}, u32[]{:S(2)}) collective-permute-start(bf16[2,2,192,384]{3,2,1,0:T(8,128)(2,1)S(1)} %pad_maximum_fusion.1.refs_7_.refs_8_), channel_id=1, source_target_pairs={{0,32},{16,48},{32,64},{48,80},{64,96},{80,112},{96,0},{112,16},{1... | collective-permute-start | bytes 1769480 | tf_op jit(solution)/shard_map/ppermute | solution.py:316
  64.0 29.4 %collective-permute-start.8 = (bf16[2,2,192,384]{3,2,1,0:T(8,128)(2,1)S(1)}, bf16[2,2,192,384]{3,2,1,0:T(8,128)(2,1)S(1)}, u32[]{:S(2)}, u32[]{:S(2)}) collective-permute-start(bf16[2,2,192,384]{3,2,1,0:T(8,128)(2,1)S(1)} %pad_maximum_fusion.1.refs_7_.refs_8_), channel_id=1, source_target_pairs={{0,64},{16,80},{32,96},{48,112},{64,0},{80,16},{96,32},{112,48},{1... | collective-permute-start | bytes 1769480 | tf_op jit(solution)/shard_map/ppermute | solution.py:316
  67.5 25.9 %collective-permute-start.9 = (bf16[2,2,192,384]{3,2,1,0:T(8,128)(2,1)S(1)}, bf16[2,2,192,384]{3,2,1,0:T(8,128)(2,1)S(1)}, u32[]{:S(2)}, u32[]{:S(2)}) collective-permute-start(bf16[2,2,192,384]{3,2,1,0:T(8,128)(2,1)S(1)} %pad_maximum_fusion.1.refs_7_.refs_8_), channel_id=1, source_target_pairs={{0,96},{16,112},{32,0},{48,16},{64,32},{80,48},{96,64},{112,80},{1... | collective-permute-start | bytes 1769480 | tf_op jit(solution)/shard_map/ppermute | solution.py:316
  119.4 201.3 %reduce-scatter.5.cloned.1.call-start = ((), (), s32[]{:S(2)}) async-start(), calls=%async_computation.3 | async-start | bytes 6684672 | tf_op jit(solution)/shard_map/reduce_scatter | solution.py:440
  121.7 24.6 %collective-permute-start.10 = (bf16[4,128,192]{2,1,0:T(8,128)(2,1)S(1)}, bf16[4,128,192]{2,1,0:T(8,128)(2,1)S(1)}, u32[]{:S(2)}, u32[]{:S(2)}) collective-permute-start(bf16[4,128,192]{2,1,0:T(8,128)(2,1)S(1)} %copy-done.14), channel_id=1, source_target_pairs={{0,16},{16,0},{32,48},{48,32},{64,80},{80,64},{96,112},{112,96},{1... | collective-permute-start | bytes 589832 | tf_op jit(solution)/shard_map/ppermute | solution.py:320
  146.5 33.5 %collective-permute-start.12 = (bf16[2,4,128,192]{3,2,1,0:T(8,128)(2,1)S(1)}, bf16[2,4,128,192]{3,2,1,0:T(8,128)(2,1)}, u32[]{:S(2)}, u32[]{:S(2)}) collective-permute-start(bf16[2,4,128,192]{3,2,1,0:T(8,128)(2,1)S(1)} %pad_maximum_fusion.2.refs_0_.refs_1_), channel_id=1, source_target_pairs={{0,32},{16,48},{32,64},{48,80},{64,96},{80,112},{96,0},{112,16},{1... | collective-permute-start | bytes 1179656 | tf_op jit(solution)/shard_map/ppermute | solution.py:316
  146.8 37.6 %collective-permute-start.13 = (bf16[2,4,128,192]{3,2,1,0:T(8,128)(2,1)S(1)}, bf16[2,4,128,192]{3,2,1,0:T(8,128)(2,1)}, u32[]{:S(2)}, u32[]{:S(2)}) collective-permute-start(bf16[2,4,128,192]{3,2,1,0:T(8,128)(2,1)S(1)} %pad_maximum_fusion.2.refs_0_.refs_1_), channel_id=1, source_target_pairs={{0,64},{16,80},{32,96},{48,112},{64,0},{80,16},{96,32},{112,48},{1... | collective-permute-start | bytes 1179656 | tf_op jit(solution)/shard_map/ppermute | solution.py:316
  149.9 37.2 %collective-permute-start.14 = (bf16[2,4,128,192]{3,2,1,0:T(8,128)(2,1)S(1)}, bf16[2,4,128,192]{3,2,1,0:T(8,128)(2,1)}, u32[]{:S(2)}, u32[]{:S(2)}) collective-permute-start(bf16[2,4,128,192]{3,2,1,0:T(8,128)(2,1)S(1)} %pad_maximum_fusion.2.refs_0_.refs_1_), channel_id=1, source_target_pairs={{0,96},{16,112},{32,0},{48,16},{64,32},{80,48},{96,64},{112,80},{1... | collective-permute-start | bytes 1179656 | tf_op jit(solution)/shard_map/ppermute | solution.py:316
  151.5 35.5 %collective-permute-start.15 = (bf16[2,2,192,384]{3,2,1,0:T(8,128)(2,1)S(1)}, bf16[2,2,192,384]{3,2,1,0:T(8,128)(2,1)S(1)}, u32[]{:S(2)}, u32[]{:S(2)}) collective-permute-start(bf16[2,2,192,384]{3,2,1,0:T(8,128)(2,1)S(1)} %get-tuple-element.157), channel_id=1, source_target_pairs={{0,96},{16,112},{32,0},{48,16},{64,32},{80,48},{96,64},{112,80},{1... | collective-permute-start | bytes 1769480 | tf_op jit(solution)/shard_map/ppermute | solution.py:316
  152.6 34.4 %collective-permute-start.16 = (bf16[2,2,192,384]{3,2,1,0:T(8,128)(2,1)S(1)}, bf16[2,2,192,384]{3,2,1,0:T(8,128)(2,1)S(1)}, u32[]{:S(2)}, u32[]{:S(2)}) collective-permute-start(bf16[2,2,192,384]{3,2,1,0:T(8,128)(2,1)S(1)} %get-tuple-element.156), channel_id=1, source_target_pairs={{0,32},{16,48},{32,64},{48,80},{64,96},{80,112},{96,0},{112,16},{1... | collective-permute-start | bytes 1769480 | tf_op jit(solution)/shard_map/ppermute | solution.py:316
  184.3 38.0 %collective-permute-start.20 = (bf16[2,2,192,384]{3,2,1,0:T(8,128)(2,1)S(1)}, bf16[2,2,192,384]{3,2,1,0:T(8,128)(2,1)}, u32[]{:S(2)}, u32[]{:S(2)}) collective-permute-start(bf16[2,2,192,384]{3,2,1,0:T(8,128)(2,1)S(1)} %get-tuple-element.155), channel_id=1, source_target_pairs={{0,64},{16,80},{32,96},{48,112},{64,0},{80,16},{96,32},{112,48},{1... | collective-permute-start | bytes 1769480 | tf_op jit(solution)/shard_map/ppermute | solution.py:316
  201.0 27.9 %collective-permute-start.18 = (bf16[2,4,128,192]{3,2,1,0:T(8,128)(2,1)S(1)}, bf16[2,4,128,192]{3,2,1,0:T(8,128)(2,1)S(1)}, u32[]{:S(2)}, u32[]{:S(2)}) collective-permute-start(bf16[2,4,128,192]{3,2,1,0:T(8,128)(2,1)S(1)} %pad_maximum_fusion.3.refs_0_.refs_1_), channel_id=1, source_target_pairs={{0,64},{16,80},{32,96},{48,112},{64,0},{80,16},{96,32},{112,48},{1... | collective-permute-start | bytes 1179656 | tf_op jit(solution)/shard_map/ppermute | solution.py:316
  232.2 23.9 %collective-permute-start.24 = (bf16[2,192,384]{2,1,0:T(8,128)(2,1)}, bf16[2,192,384]{2,1,0:T(8,128)(2,1)}, u32[]{:S(2)}, u32[]{:S(2)}) collective-permute-start(bf16[2,192,384]{2,1,0:T(8,128)(2,1)} %slice_bitcast_fusion.5), channel_id=1, source_target_pairs={{0,16},{16,0},{32,48},{48,32},{64,80},{80,64},{96,112},{112,96},{1... | collective-permute-start | bytes 884744 | tf_op jit(solution)/shard_map/ppermute | solution.py:320
  260.3 32.5 %collective-permute-start.34 = (bf16[2,2,192,384]{3,2,1,0:T(8,128)(2,1)S(1)}, bf16[2,2,192,384]{3,2,1,0:T(8,128)(2,1)S(1)}, u32[]{:S(2)}, u32[]{:S(2)}) collective-permute-start(bf16[2,2,192,384]{3,2,1,0:T(8,128)(2,1)S(1)} %slice.287), channel_id=1, source_target_pairs={{0,64},{16,80},{32,96},{48,112},{64,0},{80,16},{96,32},{112,48},{1... | collective-permute-start | bytes 1769480 | tf_op jit(solution)/shard_map/ppermute | solution.py:316
  269.4 37.8 %collective-permute-start.30 = (bf16[4,2,384,128]{3,2,1,0:T(8,128)(2,1)S(1)}, bf16[4,2,384,128]{3,2,1,0:T(8,128)(2,1)S(1)}, u32[]{:S(2)}, u32[]{:S(2)}) collective-permute-start(bf16[4,2,384,128]{3,2,1,0:T(8,128)(2,1)S(1)} %slice_bitcast_fusion), channel_id=1, source_target_pairs={{0,2},{1,3},{2,0},{3,1},{4,6},{5,7},{6,4},{7,5},{8,10},{9,11},{10,... | collective-permute-start | bytes 2359304 | tf_op jit(solution)/shard_map/ppermute | solution.py:361
  284.0 27.4 %collective-permute-start.28 = (bf16[2,384,128]{2,1,0:T(8,128)(2,1)S(1)}, bf16[2,384,128]{2,1,0:T(8,128)(2,1)S(1)}, u32[]{:S(2)}, u32[]{:S(2)}) collective-permute-start(bf16[2,384,128]{2,1,0:T(8,128)(2,1)S(1)} %slice_bitcast_fusion.12), channel_id=1, source_target_pairs={{0,2},{1,3},{2,0},{3,1},{4,6},{5,7},{6,4},{7,5},{8,10},{9,11},{10,... | collective-permute-start | bytes 589832 | tf_op jit(solution)/shard_map/ppermute | solution.py:352
  294.4 24.4 %collective-permute-start.35 = (bf16[2,192,384]{2,1,0:T(8,128)(2,1)S(1)}, bf16[2,192,384]{2,1,0:T(8,128)(2,1)S(1)}, u32[]{:S(2)}, u32[]{:S(2)}) collective-permute-start(bf16[2,192,384]{2,1,0:T(8,128)(2,1)S(1)} %slice_bitcast_fusion.2), channel_id=1, source_target_pairs={{0,16},{16,0},{32,48},{48,32},{64,80},{80,64},{96,112},{112,96},{1... | collective-permute-start | bytes 884744 | tf_op jit(solution)/shard_map/ppermute | solution.py:320
  (40 other events, 420.1 us)
Sparse Core Ops, SparseCore 0:
  10.3 50.1 all-gather.4
  62.8 41.5 all-gather.6
  119.5 80.2 reduce-scatter.2
  205.5 99.8 reduce-scatter.4

commit v7 on v6

--- a/solution.py
+++ b/solution.py
@@ -352,10 +352,6 @@
     return lax.ppermute(total[1], "col", [(c, c ^ 2) for c in range(16)])
 
 
-def z_sum(total):
-    return add_pair(total[0], z_swap(total))
-
-
 def z_first(part):
     part = part.reshape((4, 2) + part.shape[1:])
     got = lax.ppermute(part[:, 1], "col", [(c, c ^ 2) for c in range(16)])
@@ -430,39 +426,37 @@
     gq0, gg0, dkv, car0 = b[:4]
     sum0 = lax.psum_scatter(dkv, "col", scatter_dimension=0)
     swap0 = row_swap(car0)
-    c = attend(1, 0, a[-1], None, after(order, gq0))
-    swap0, bias0 = lax.optimization_barrier((after(swap0, c[0]), c[-1]))
+    order_c, swap0 = lax.optimization_barrier((order, swap0))
     pair0 = jnp.stack([car0, swap0])
     pairs0 = [pair0] + row_shifts(pair0)
+    c = attend(1, 0, a[-1], None, after(order_c, pair0))
+    pairs0, bias0 = lax.optimization_barrier((pairs0, c[-1]))
     bias0 = row_parts(bias0)
-    d = attend(1, 1, b[-1], list(c[:4]), after(order, pair0, c[0]))
+    left0 = left_product(order, cols, pairs0, right_t)
+    bias0[1], bias0[3], left0 = lax.optimization_barrier((bias0[1], bias0[3], left0))
+    part_l0 = add_pair(left0[0], core_swap(left0[1]))
+    order_d, part_l0 = lax.optimization_barrier((order, part_l0))
+    shifts_l0 = [x_shift(part_l0, dx) for dx in (1, 3, 2)]
+    d = attend(1, 1, b[-1], list(c[:4]), order_d)
     gq1, gg1, dkv, car1 = d[:4]
     sum1 = lax.psum_scatter(after(dkv, sum0), "col", scatter_dimension=0)
-    pairs0, near0 = after((pairs0, bias0[1:4:2]), gq1)
-    order_l, car1 = lax.optimization_barrier((order, car1))
     swap1 = row_swap(car1)
-    swap1, sum0, pairs0, near0 = lax.optimization_barrier((swap1, sum0, pairs0, near0))
+    shifts_l0, far0, swap1, late1, sum0 = lax.optimization_barrier((shifts_l0, bias0[2], swap1, d[-1], sum0))
     pair1 = jnp.stack([car1, swap1])
     pairs1 = [pair1] + row_shifts(pair1)
-    left0 = left_product(after(order_l, pair1), cols, pairs0, right_t)
-    pairs1, far0, left0, bias1 = lax.optimization_barrier((pairs1, bias0[2], left0, d[-1]))
-    bias0 = add_all([bias0[0], far0] + list(near0))
-    got_l0 = core_swap(left0[1])
-    bias1 = row_parts(bias1)
-    got_bias0 = row_swap(bias0[1])
-    left1 = left_product(after(order, pairs1, bias0), cols, pairs1, right_t)
-    got_l0, bias1[1], bias1[3], got_bias0, left1, late1 = lax.optimization_barrier(
-        (got_l0, bias1[1], bias1[3], got_bias0, left1, d[-1])
+    sum_l0 = add_all([part_l0[0:2]] + shifts_l0)
+    bias0 = add_all([bias0[0], bias0[1], bias0[3], far0])
+    pairs1, sum_l0, bias0, late1 = lax.optimization_barrier((pairs1, sum_l0, bias0, late1))
+    bias1 = row_parts(late1)
+    got_l0, got_bias0 = z_swap(sum_l0), row_swap(bias0[1])
+    left1 = left_product(after(order, pairs1), cols, pairs1, right_t)
+    got_l0, got_bias0, bias1[1], bias1[3], left1 = lax.optimization_barrier(
+        (got_l0, got_bias0, bias1[1], bias1[3], left1)
     )
-    bias1[2] = row_parts(late1)[2]
-    got_l1 = core_swap(left1[1])
-    part_l0 = add_pair(left0[0], got_l0)
-    shifts_l0 = [x_shift(part_l0, dx) for dx in (1, 3, 2)]
-    part_l1 = add_pair(left1[0], got_l1)
+    part_l1 = add_pair(left1[0], core_swap(left1[1]))
     bias1 = add_all(after(bias1, part_l1))
     sum_l1 = z_first(part_l1)
-    sum_l0 = z_sum(add_all([part_l0[0:2]] + shifts_l0))
-    left = jnp.concatenate([sum_l0, sum_l1])
+    left = jnp.concatenate([add_pair(sum_l0[0], got_l0), sum_l1])
     got_bias1 = after(row_swap(bias1[1]), sum_l1)
     grad_bias = jnp.concatenate(
         [bias0[0].astype(F32) + got_bias0.astype(F32), bias1[0].astype(F32) + got_bias1.astype(F32)]

time: 336 us -> 357 us (1.062)
  waiting for transfers between devices: 64.4 us -> 93.2 us
  starting transfers between devices: 60.8 us -> 54.7 us
    ppermute x21, waiting for transfers between devices: 18.5 us -> 57.2 us  [row_shift(): lax.ppermute(x, 'row', [(2 * y + z, 2 * ((y + dy) % 4) + z) for y in rang...]
    ppermute x1, waiting for transfers between devices: 11.1 us -> 1.03 us  [z_first(): got = lax.ppermute(part[:, 1], 'col', [(c, c ^ 2) for c in range(16)])]
    ppermute x1, starting transfers between devices: 8.73 us -> 4.5 us  [z_swap(): return lax.ppermute(total[1], 'col', [(c, c ^ 2) for c in range(16)])]
    ppermute x2, waiting for transfers between devices: 0.01 us -> 3.61 us  [core_swap(): return lax.ppermute(send, 'col', [(c, c ^ 1) for c in range(16)])]
    unnamed x49 -> x53, local copies, waits for them, and re-layouts: 26.6 us -> 28.2 us
  transfers between devices with their start and end apart: 40 -> 40, of which waited for: 12 -> 17; matrix products, arithmetic and copies ran while one was open for 15% -> 14% of each run, Pallas kernels for 40% -> 38%
where the time goes in v7:
time: 357 us; the launch traced here: 351 us
  Pallas kernels  132 us (37%)
  waiting for transfers between devices  93.2 us (26%)
  starting transfers between devices  54.7 us (15%)
  local copies, waits for them, and re-layouts  38.5 us (11%)
  other arithmetic  18 us (5%)
  between operations  14.7 us (4%)
    pallas_call x4, Pallas kernels, attention(): pl.pallas_call(functools.partial(attention_kernel, h0, heads, total_heads...  98.4 us
    ppermute x21, waiting for transfers between devices, row_shift(): lax.ppermute(x, 'row', [(2 * y + z, 2 * ((y + dy) % 4) + z) for y in rang...  57.2 us
    pallas_call x2, Pallas kernels, left_product(): pl.pallas_call(left_kernel, grid_spec=pltpu.PrefetchScalarGridSpec(num_sc...  33.9 us
    unnamed x53, local copies, waits for them, and re-layouts  28.2 us
    ppermute x21, starting transfers between devices, row_shift(): lax.ppermute(x, 'row', [(2 * y + z, 2 * ((y + dy) % 4) + z) for y in rang...  27.9 us
    ppermute x3, waiting for transfers between devices, x_shift(): lax.ppermute(part[2 * dx:2 * dx + 2], 'col', [(c, (c + 4 * dx) % 16) for...  12.2 us
    ppermute x5, waiting for transfers between devices, row_swap(): return lax.ppermute(x, 'row', [(r, r ^ 1) for r in range(8)])  11.8 us
    ppermute x5, starting transfers between devices, row_swap(): return lax.ppermute(x, 'row', [(r, r ^ 1) for r in range(8)])  10.2 us
  transfers between devices with their start and end apart: 40, of which 17 were waited for; matrix products, arithmetic and copies ran while one was open for 14% of the time, Pallas kernels for 38%

profile of v7, /device:TPU:0, one launch (start us, length us, event | category | flops | bytes accessed | tf_op | source)
XLA Modules:
  0.0 351.3 jit_solution(14781228290013296221)
XLA Ops:
  11.2 4.0 %collective-permute-start = (bf16[4,192,384]{2,1,0:T(8,128)(2,1)S(1)}, bf16[4,192,384]{2,1,0:T(8,128)(2,1)S(1)}, u32[]{:S(2)}, u32[]{:S(2)}) collective-permute-start(bf16[4,192,384]{2,1,0:T(8,128)(2,1)S(1)} %add_convert_fusion.4), channel_id=1, source_target_pairs={{0,16},{16,0},{32,48},{48,32},{64,80},{80,64},{96,112},{112,96},{1... | collective-permute-start | bytes 1769480 | tf_op jit(solution)/shard_map/ppermute | solution.py:320
  16.1 3.0 collective-permute-start.5
  20.8 24.5 %copy.19 = bf16[192,384,128]{1,0,2:T(8,128)(2,1)} copy(bf16[192,384,128]{2,1,0:T(8,128)(2,1)} %param.19) | data formatting | bytes 37748736 | tf_op args[9]
  52.8 7.1 %collective-permute-done.6 = bf16[2,192,384]{2,1,0:T(8,128)(2,1)S(1)} collective-permute-done((bf16[2,192,384]{2,1,0:T(8,128)(2,1)S(1)}, bf16[2,192,384]{2,1,0:T(8,128)(2,1)S(1)}, u32[]{:S(2)}, u32[]{:S(2)}) %collective-permute-start.6) | collective-permute-done | bytes 294944 | tf_op jit(solution)/shard_map/ppermute | solution.py:316
  60.0 3.7 %collective-permute-done.2 = bf16[2,192,384]{2,1,0:T(8,128)(2,1)} collective-permute-done((bf16[2,192,384]{2,1,0:T(8,128)(2,1)S(1)}, bf16[2,192,384]{2,1,0:T(8,128)(2,1)}, u32[]{:S(2)}, u32[]{:S(2)}) %collective-permute-start.2) | collective-permute-done | bytes 294944 | tf_op jit(solution)/shard_map/ppermute | solution.py:316
  67.0 23.4 %attention_rows.4 = (bf16[4,192,128]{2,1,0:T(8,128)(2,1)}, bf16[4,192,128]{2,1,0:T(8,128)(2,1)}, bf16[4,64,3072]{2,1,0:T(8,128)(2,1)}, bf16[4,64,3072]{2,1,0:T(8,128)(2,1)}, f32[2,192,3072]{2,1,0:T(8,128)}) custom-call(s32[8]{0:T(128)} %stack.113.order_ref, bf16[4,192,128]{2,1,0:T(8,128)(2,1)} %get-tuple-element.213.refs_0_, ...), custom_call_target="tpu_custom_call" | custom-call | flops 9663676416 | bytes 30000000 | tf_op jit(solution)/shard_map/attention_rows/pallas_call | solution.py:235
  93.8 24.9 %attention_rows.5 = (bf16[4,192,128]{2,1,0:T(8,128)(2,1)}, bf16[4,192,128]{2,1,0:T(8,128)(2,1)}, bf16[16,8,192,128]{3,2,1,0:T(8,128)(2,1)}, bf16[4,128,192]{2,1,0:T(8,128)(2,1)}, f32[2,192,3072]{2,1,0:T(8,128)}) custom-call(s32[8]{0:T(128)} %stack.113.order_ref, bf16[4,192,128]{2,1,0:T(8,128)(2,1)} %get-tuple-element.213.refs_0_, ...), custom_call_target="tpu_custom_call" | custom-call | flops 9663676416 | bytes 30000000 | tf_op jit(solution)/shard_map/attention_rows/pallas_call | solution.py:235
  121.7 7.8 %collective-permute-done.10 = bf16[4,128,192]{2,1,0:T(8,128)(2,1)S(1)} collective-permute-done((bf16[4,128,192]{2,1,0:T(8,128)(2,1)S(1)}, bf16[4,128,192]{2,1,0:T(8,128)(2,1)S(1)}, u32[]{:S(2)}, u32[]{:S(2)}) %collective-permute-start.10) | collective-permute-done | bytes 196640 | tf_op jit(solution)/shard_map/ppermute | solution.py:320
  132.9 24.2 %attention_rows.6 = (bf16[4,192,128]{2,1,0:T(8,128)(2,1)}, bf16[4,192,128]{2,1,0:T(8,128)(2,1)}, bf16[4,64,3072]{2,1,0:T(8,128)(2,1)}, bf16[4,64,3072]{2,1,0:T(8,128)(2,1)}, bf16[8,2,192,384]{3,2,1,0:T(8,128)(2,1)}) custom-call(s32[8]{0:T(128)} %stack.113.order_ref, bf16[4,192,128]{2,1,0:T(8,128)(2,1)} %get-tuple-element.217.refs_0_, ...), custom_call_target="tpu_custom_call" | custom-call | flops 9663676416 | bytes 30000000 | tf_op jit(solution)/shard_map/attention_rows/pallas_call | solution.py:235
  163.8 17.0 %left_product.2 = (bf16[8,2,384,128]{3,2,1,0:T(8,128)(2,1)}, bf16[8,2,384,128]{3,2,1,0:T(8,128)(2,1)}) custom-call(s32[8]{0:T(128)} %stack.113.order_ref, s32[16]{0:T(128)} %stack.136.cols_ref, bf16[2,4,128,192]{3,2,1,0:T(8,128)(2,1)} %copy-done.5, bf16[2,4,128,192]{3,2,1,0:T(8,128)(2,1)} %copy-done.5, bf16[2,4,128,192]{3,2,1,0:T(8,128)(2,1)} %copy-done.23, ...), custom_call_target="tpu_custom_call" | custom-call | flops 40000000000 | bytes 30000000 | tf_op jit(solution)/shard_map/left_product/pallas_call | solution.py:296
  181.3 3.6 %collective-permute-done.16 = bf16[8,2,384,128]{3,2,1,0:T(8,128)(2,1)S(1)} collective-permute-done((bf16[8,2,384,128]{3,2,1,0:T(8,128)(2,1)}, bf16[8,2,384,128]{3,2,1,0:T(8,128)(2,1)S(1)}, u32[]{:S(2)}, u32[]{:S(2)}) %collective-permute-start.16) | collective-permute-done | bytes 1572896 | tf_op jit(solution)/shard_map/ppermute | solution.py:340
  186.8 25.9 %attention_rows.7 = (bf16[4,192,128]{2,1,0:T(8,128)(2,1)}, bf16[4,192,128]{2,1,0:T(8,128)(2,1)}, bf16[16,8,192,128]{3,2,1,0:T(8,128)(2,1)}, bf16[4,128,192]{2,1,0:T(8,128)(2,1)}, bf16[8,2,192,384]{3,2,1,0:T(8,128)(2,1)}) custom-call(s32[8]{0:T(128)} %stack.113.order_ref, bf16[4,192,128]{2,1,0:T(8,128)(2,1)} %get-tuple-element.217.refs_0_, ...), custom_call_target="tpu_custom_call" | custom-call | flops 9663676416 | bytes 30000000 | tf_op jit(solution)/shard_map/attention_rows/pallas_call | solution.py:235
  215.0 3.3 collective-permute-start.19
  221.8 8.0 %collective-permute-done.20 = bf16[2,2,192,384]{3,2,1,0:T(8,128)(2,1)S(1)} collective-permute-done((bf16[2,2,192,384]{3,2,1,0:T(8,128)(2,1)S(1)}, bf16[2,2,192,384]{3,2,1,0:T(8,128)(2,1)S(1)}, u32[]{:S(2)}, u32[]{:S(2)}) %collective-permute-start.20) | collective-permute-done | bytes 589856 | tf_op jit(solution)/shard_map/ppermute | solution.py:316
  231.9 12.2 %collective-permute-done.18 = bf16[2,2,384,128]{3,2,1,0:T(8,128)(2,1)S(1)} collective-permute-done((bf16[2,2,384,128]{3,2,1,0:T(8,128)(2,1)S(1)}, bf16[2,2,384,128]{3,2,1,0:T(8,128)(2,1)S(1)}, u32[]{:S(2)}, u32[]{:S(2)}) %collective-permute-start.18) | collective-permute-done | bytes 393248 | tf_op jit(solution)/shard_map/ppermute | solution.py:348
  248.2 11.1 %collective-permute-done.24.refs_6_.refs_7_ = bf16[2,4,128,192]{3,2,1,0:T(8,128)(2,1)S(1)} collective-permute-done((bf16[2,4,128,192]{3,2,1,0:T(8,128)(2,1)S(1)}, bf16[2,4,128,192]{3,2,1,0:T(8,128)(2,1)S(1)}, u32[]{:S(2)}, u32[]{:S(2)}) %collective-permute-start.24) | collective-permute-done | bytes 393248 | tf_op jit(solution)/shard_map/ppermute | solution.py:316
  260.8 8.3 %collective-permute-done.22.refs_2_.refs_3_ = bf16[2,4,128,192]{3,2,1,0:T(8,128)(2,1)S(1)} collective-permute-done((bf16[2,4,128,192]{3,2,1,0:T(8,128)(2,1)S(1)}, bf16[2,4,128,192]{3,2,1,0:T(8,128)(2,1)S(1)}, u32[]{:S(2)}, u32[]{:S(2)}) %collective-permute-start.22) | collective-permute-done | bytes 393248 | tf_op jit(solution)/shard_map/ppermute | solution.py:316
  269.9 4.5 %collective-permute-start.25 = (bf16[2,384,128]{2,1,0:T(8,128)(2,1)}, bf16[2,384,128]{2,1,0:T(8,128)(2,1)}, u32[]{:S(2)}, u32[]{:S(2)}) collective-permute-start(bf16[2,384,128]{2,1,0:T(8,128)(2,1)} %slice_bitcast_fusion.11), channel_id=1, source_target_pairs={{0,2},{1,3},{2,0},{3,1},{4,6},{5,7},{6,4},{7,5},{8,10},{9,11},{10,... | collective-permute-start | bytes 589832 | tf_op jit(solution)/shard_map/ppermute | solution.py:352
  274.9 3.4 collective-permute-start.27
  278.3 16.9 %left_product.3 = (bf16[8,2,384,128]{3,2,1,0:T(8,128)(2,1)}, bf16[8,2,384,128]{3,2,1,0:T(8,128)(2,1)}) custom-call(s32[8]{0:T(128)} %stack.113.order_ref, s32[16]{0:T(128)} %stack.136.cols_ref, bf16[2,4,128,192]{3,2,1,0:T(8,128)(2,1)} %copy-done.4, bf16[2,4,128,192]{3,2,1,0:T(8,128)(2,1)} %copy-done.4, bf16[2,4,128,192]{3,2,1,0:T(8,128)(2,1)} %copy-done.22, ...), custom_call_target="tpu_custom_call" | custom-call | flops 40000000000 | bytes 30000000 | tf_op jit(solution)/shard_map/left_product/pallas_call | solution.py:296
  304.0 14.9 %collective-permute-done.34 = bf16[2,2,192,384]{3,2,1,0:T(8,128)(2,1)S(1)} collective-permute-done((bf16[2,2,192,384]{3,2,1,0:T(8,128)(2,1)S(1)}, bf16[2,2,192,384]{3,2,1,0:T(8,128)(2,1)S(1)}, u32[]{:S(2)}, u32[]{:S(2)}) %collective-permute-start.34) | collective-permute-done | bytes 589856 | tf_op jit(solution)/shard_map/ppermute | solution.py:316
  320.4 4.6 %collective-permute-start.35 = (bf16[2,192,384]{2,1,0:T(8,128)(2,1)S(1)}, bf16[2,192,384]{2,1,0:T(8,128)(2,1)S(1)}, u32[]{:S(2)}, u32[]{:S(2)}) collective-permute-start(bf16[2,192,384]{2,1,0:T(8,128)(2,1)S(1)} %slice_bitcast_fusion.2), channel_id=1, source_target_pairs={{0,16},{16,0},{32,48},{48,32},{64,80},{80,64},{96,112},{112,96},{1... | collective-permute-start | bytes 884744 | tf_op jit(solution)/shard_map/ppermute | solution.py:320
  327.7 3.1 collective-permute-start.33
  334.5 5.4 %collective-permute-done.33 = bf16[2,384,128]{2,1,0:T(8,128)(2,1)S(1)} collective-permute-done((bf16[2,384,128]{2,1,0:T(8,128)(2,1)S(1)}, bf16[2,384,128]{2,1,0:T(8,128)(2,1)S(1)}, u32[]{:S(2)}, u32[]{:S(2)}) %collective-permute-start.33) | collective-permute-done | bytes 196640 | tf_op jit(solution)/shard_map/ppermute | solution.py:359
  (173 shorter events, 71.8 us)
Async XLA Ops:
  7.2 59.9 %all-gather.5.cloned.1.call-start = ((), (), s32[]{:S(2)}) async-start(), calls=%async_computation.4 | async-start | bytes 6684672 | tf_op jit(solution)/shard_map/all_gather | solution.py:413
  9.3 123.5 %all-gather.7.cloned.1.call-start = ((), (), s32[]{:S(2)}) async-start(), calls=%async_computation.5 | async-start | bytes 6684672 | tf_op jit(solution)/shard_map/all_gather | solution.py:413
  10.2 202.5 %reduce-scatter.3.cloned.1.call-start = ((), (), s32[]{:S(2)}) async-start(), calls=%async_computation.2 | async-start | bytes 6684672 | tf_op jit(solution)/shard_map/reduce_scatter | solution.py:427
  11.2 34.2 %collective-permute-start = (bf16[4,192,384]{2,1,0:T(8,128)(2,1)S(1)}, bf16[4,192,384]{2,1,0:T(8,128)(2,1)S(1)}, u32[]{:S(2)}, u32[]{:S(2)}) collective-permute-start(bf16[4,192,384]{2,1,0:T(8,128)(2,1)S(1)} %add_convert_fusion.4), channel_id=1, source_target_pairs={{0,16},{16,0},{32,48},{48,32},{64,80},{80,64},{96,112},{112,96},{1... | collective-permute-start | bytes 1769480 | tf_op jit(solution)/shard_map/ppermute | solution.py:320
  16.1 34.3 %collective-permute-start.5 = (bf16[2,192,384]{2,1,0:T(8,128)(2,1)S(1)}, bf16[2,192,384]{2,1,0:T(8,128)(2,1)}, u32[]{:S(2)}, u32[]{:S(2)}) collective-permute-start(bf16[2,192,384]{2,1,0:T(8,128)(2,1)S(1)} %get-tuple-element.163), channel_id=1, source_target_pairs={{0,96},{16,112},{32,0},{48,16},{64,32},{80,48},{96,64},{112,80},{1... | collective-permute-start | bytes 884744 | tf_op jit(solution)/shard_map/ppermute | solution.py:316
  19.1 33.7 %collective-permute-start.3 = (bf16[2,192,384]{2,1,0:T(8,128)(2,1)S(1)}, bf16[2,192,384]{2,1,0:T(8,128)(2,1)}, u32[]{:S(2)}, u32[]{:S(2)}) collective-permute-start(bf16[2,192,384]{2,1,0:T(8,128)(2,1)S(1)} %get-tuple-element.163), channel_id=1, source_target_pairs={{0,64},{16,80},{32,96},{48,112},{64,0},{80,16},{96,32},{112,48},{1... | collective-permute-start | bytes 884744 | tf_op jit(solution)/shard_map/ppermute | solution.py:316
  19.7 33.1 %collective-permute-start.1 = (bf16[2,192,384]{2,1,0:T(8,128)(2,1)S(1)}, bf16[2,192,384]{2,1,0:T(8,128)(2,1)}, u32[]{:S(2)}, u32[]{:S(2)}) collective-permute-start(bf16[2,192,384]{2,1,0:T(8,128)(2,1)S(1)} %get-tuple-element.163), channel_id=1, source_target_pairs={{0,32},{16,48},{32,64},{48,80},{64,96},{80,112},{96,0},{112,16},{1... | collective-permute-start | bytes 884744 | tf_op jit(solution)/shard_map/ppermute | solution.py:316
  63.7 26.7 %collective-permute-start.9 = (bf16[2,2,192,384]{3,2,1,0:T(8,128)(2,1)S(1)}, bf16[2,2,192,384]{3,2,1,0:T(8,128)(2,1)S(1)}, u32[]{:S(2)}, u32[]{:S(2)}) collective-permute-start(bf16[2,2,192,384]{3,2,1,0:T(8,128)(2,1)S(1)} %pad_maximum_fusion.1.refs_7_.refs_8_), channel_id=1, source_target_pairs={{0,96},{16,112},{32,0},{48,16},{64,32},{80,48},{96,64},{112,80},{1... | collective-permute-start | bytes 1769480 | tf_op jit(solution)/shard_map/ppermute | solution.py:316
  64.3 26.1 %collective-permute-start.8 = (bf16[2,2,192,384]{3,2,1,0:T(8,128)(2,1)S(1)}, bf16[2,2,192,384]{3,2,1,0:T(8,128)(2,1)S(1)}, u32[]{:S(2)}, u32[]{:S(2)}) collective-permute-start(bf16[2,2,192,384]{3,2,1,0:T(8,128)(2,1)S(1)} %pad_maximum_fusion.1.refs_7_.refs_8_), channel_id=1, source_target_pairs={{0,64},{16,80},{32,96},{48,112},{64,0},{80,16},{96,32},{112,48},{1... | collective-permute-start | bytes 1769480 | tf_op jit(solution)/shard_map/ppermute | solution.py:316
  66.3 26.6 %collective-permute-start.7 = (bf16[2,2,192,384]{3,2,1,0:T(8,128)(2,1)S(1)}, bf16[2,2,192,384]{3,2,1,0:T(8,128)(2,1)S(1)}, u32[]{:S(2)}, u32[]{:S(2)}) collective-permute-start(bf16[2,2,192,384]{3,2,1,0:T(8,128)(2,1)S(1)} %pad_maximum_fusion.1.refs_7_.refs_8_), channel_id=1, source_target_pairs={{0,32},{16,48},{32,64},{48,80},{64,96},{80,112},{96,0},{112,16},{1... | collective-permute-start | bytes 1769480 | tf_op jit(solution)/shard_map/ppermute | solution.py:316
  118.7 223.3 %reduce-scatter.5.cloned.1.call-start = ((), (), s32[]{:S(2)}) async-start(), calls=%async_computation.3 | async-start | bytes 6684672 | tf_op jit(solution)/shard_map/reduce_scatter | solution.py:442
  129.7 27.4 %collective-permute-start.13 = (bf16[2,4,128,192]{3,2,1,0:T(8,128)(2,1)S(1)}, bf16[2,4,128,192]{3,2,1,0:T(8,128)(2,1)S(1)}, u32[]{:S(2)}, u32[]{:S(2)}) collective-permute-start(bf16[2,4,128,192]{3,2,1,0:T(8,128)(2,1)S(1)} %pad_maximum_fusion.2.refs_0_.refs_1_), channel_id=1, source_target_pairs={{0,96},{16,112},{32,0},{48,16},{64,32},{80,48},{96,64},{112,80},{1... | collective-permute-start | bytes 1179656 | tf_op jit(solution)/shard_map/ppermute | solution.py:316
  129.8 27.3 %collective-permute-start.12 = (bf16[2,4,128,192]{3,2,1,0:T(8,128)(2,1)S(1)}, bf16[2,4,128,192]{3,2,1,0:T(8,128)(2,1)S(1)}, u32[]{:S(2)}, u32[]{:S(2)}) collective-permute-start(bf16[2,4,128,192]{3,2,1,0:T(8,128)(2,1)S(1)} %pad_maximum_fusion.2.refs_0_.refs_1_), channel_id=1, source_target_pairs={{0,64},{16,80},{32,96},{48,112},{64,0},{80,16},{96,32},{112,48},{1... | collective-permute-start | bytes 1179656 | tf_op jit(solution)/shard_map/ppermute | solution.py:316
  131.4 25.8 %collective-permute-start.11 = (bf16[2,4,128,192]{3,2,1,0:T(8,128)(2,1)S(1)}, bf16[2,4,128,192]{3,2,1,0:T(8,128)(2,1)S(1)}, u32[]{:S(2)}, u32[]{:S(2)}) collective-permute-start(bf16[2,4,128,192]{3,2,1,0:T(8,128)(2,1)S(1)} %pad_maximum_fusion.2.refs_0_.refs_1_), channel_id=1, source_target_pairs={{0,32},{16,48},{32,64},{48,80},{64,96},{80,112},{96,0},{112,16},{1... | collective-permute-start | bytes 1179656 | tf_op jit(solution)/shard_map/ppermute | solution.py:316
  160.5 20.3 %collective-permute-start.15 = (bf16[2,2,192,384]{3,2,1,0:T(8,128)(2,1)S(1)}, bf16[2,2,192,384]{3,2,1,0:T(8,128)(2,1)S(1)}, u32[]{:S(2)}, u32[]{:S(2)}) collective-permute-start(bf16[2,2,192,384]{3,2,1,0:T(8,128)(2,1)S(1)} %get-tuple-element.151), channel_id=1, source_target_pairs={{0,32},{16,48},{32,64},{48,80},{64,96},{80,112},{96,0},{112,16},{1... | collective-permute-start | bytes 1769480 | tf_op jit(solution)/shard_map/ppermute | solution.py:316
  161.3 19.6 %collective-permute-start.14 = (bf16[2,2,192,384]{3,2,1,0:T(8,128)(2,1)S(1)}, bf16[2,2,192,384]{3,2,1,0:T(8,128)(2,1)S(1)}, u32[]{:S(2)}, u32[]{:S(2)}) collective-permute-start(bf16[2,2,192,384]{3,2,1,0:T(8,128)(2,1)S(1)} %get-tuple-element.152), channel_id=1, source_target_pairs={{0,96},{16,112},{32,0},{48,16},{64,32},{80,48},{96,64},{112,80},{1... | collective-permute-start | bytes 1769480 | tf_op jit(solution)/shard_map/ppermute | solution.py:316
  218.3 25.9 %collective-permute-start.18 = (bf16[2,2,384,128]{3,2,1,0:T(8,128)(2,1)S(1)}, bf16[2,2,384,128]{3,2,1,0:T(8,128)(2,1)S(1)}, u32[]{:S(2)}, u32[]{:S(2)}) collective-permute-start(bf16[2,2,384,128]{3,2,1,0:T(8,128)(2,1)S(1)} %get-tuple-element.154), channel_id=1, source_target_pairs={{0,12},{1,13},{2,14},{3,15},{4,0},{5,1},{6,2},{7,3},{8,4},{9,5},{1... | collective-permute-start | bytes 1179656 | tf_op jit(solution)/shard_map/ppermute | solution.py:348
  220.1 24.1 %collective-permute-start.17 = (bf16[2,2,384,128]{3,2,1,0:T(8,128)(2,1)S(1)}, bf16[2,2,384,128]{3,2,1,0:T(8,128)(2,1)S(1)}, u32[]{:S(2)}, u32[]{:S(2)}) collective-permute-start(bf16[2,2,384,128]{3,2,1,0:T(8,128)(2,1)S(1)} %get-tuple-element.155), channel_id=1, source_target_pairs={{0,4},{1,5},{2,6},{3,7},{4,8},{5,9},{6,10},{7,11},{8,12},{9,13},{1... | collective-permute-start | bytes 1179656 | tf_op jit(solution)/shard_map/ppermute | solution.py:348
  245.4 23.8 %collective-permute-start.22 = (bf16[2,4,128,192]{3,2,1,0:T(8,128)(2,1)S(1)}, bf16[2,4,128,192]{3,2,1,0:T(8,128)(2,1)S(1)}, u32[]{:S(2)}, u32[]{:S(2)}) collective-permute-start(bf16[2,4,128,192]{3,2,1,0:T(8,128)(2,1)S(1)} %pad_maximum_fusion.3.refs_0_.refs_1_), channel_id=1, source_target_pairs={{0,32},{16,48},{32,64},{48,80},{64,96},{80,112},{96,0},{112,16},{1... | collective-permute-start | bytes 1179656 | tf_op jit(solution)/shard_map/ppermute | solution.py:316
  269.9 25.3 %collective-permute-start.25 = (bf16[2,384,128]{2,1,0:T(8,128)(2,1)}, bf16[2,384,128]{2,1,0:T(8,128)(2,1)}, u32[]{:S(2)}, u32[]{:S(2)}) collective-permute-start(bf16[2,384,128]{2,1,0:T(8,128)(2,1)} %slice_bitcast_fusion.11), channel_id=1, source_target_pairs={{0,2},{1,3},{2,0},{3,1},{4,6},{5,7},{6,4},{7,5},{8,10},{9,11},{10,... | collective-permute-start | bytes 589832 | tf_op jit(solution)/shard_map/ppermute | solution.py:352
  274.4 22.6 %collective-permute-start.26 = (bf16[2,192,384]{2,1,0:T(8,128)(2,1)S(1)}, bf16[2,192,384]{2,1,0:T(8,128)(2,1)S(1)}, u32[]{:S(2)}, u32[]{:S(2)}) collective-permute-start(bf16[2,192,384]{2,1,0:T(8,128)(2,1)S(1)} %slice_bitcast_fusion.5), channel_id=1, source_target_pairs={{0,16},{16,0},{32,48},{48,32},{64,80},{80,64},{96,112},{112,96},{1... | collective-permute-start | bytes 884744 | tf_op jit(solution)/shard_map/ppermute | solution.py:320
  274.8 22.2 %collective-permute-start.28 = (bf16[2,2,192,384]{3,2,1,0:T(8,128)(2,1)S(1)}, bf16[2,2,192,384]{3,2,1,0:T(8,128)(2,1)}, u32[]{:S(2)}, u32[]{:S(2)}) collective-permute-start(bf16[2,2,192,384]{3,2,1,0:T(8,128)(2,1)S(1)} %get-tuple-element.148), channel_id=1, source_target_pairs={{0,32},{16,48},{32,64},{48,80},{64,96},{80,112},{96,0},{112,16},{1... | collective-permute-start | bytes 1769480 | tf_op jit(solution)/shard_map/ppermute | solution.py:316
  274.9 22.1 %collective-permute-start.27 = (bf16[2,2,192,384]{3,2,1,0:T(8,128)(2,1)S(1)}, bf16[2,2,192,384]{3,2,1,0:T(8,128)(2,1)}, u32[]{:S(2)}, u32[]{:S(2)}) collective-permute-start(bf16[2,2,192,384]{3,2,1,0:T(8,128)(2,1)S(1)} %get-tuple-element.149), channel_id=1, source_target_pairs={{0,96},{16,112},{32,0},{48,16},{64,32},{80,48},{96,64},{112,80},{1... | collective-permute-start | bytes 1769480 | tf_op jit(solution)/shard_map/ppermute | solution.py:316
  303.7 22.4 %collective-permute-start.30 = (bf16[4,2,384,128]{3,2,1,0:T(8,128)(2,1)S(1)}, bf16[4,2,384,128]{3,2,1,0:T(8,128)(2,1)S(1)}, u32[]{:S(2)}, u32[]{:S(2)}) collective-permute-start(bf16[4,2,384,128]{3,2,1,0:T(8,128)(2,1)S(1)} %slice_bitcast_fusion), channel_id=1, source_target_pairs={{0,2},{1,3},{2,0},{3,1},{4,6},{5,7},{6,4},{7,5},{8,10},{9,11},{10,... | collective-permute-start | bytes 2359304 | tf_op jit(solution)/shard_map/ppermute | solution.py:357
  (42 other events, 416.5 us)
Sparse Core Ops, SparseCore 0:
  10.3 50.1 all-gather.4
  62.8 41.5 all-gather.6
  118.8 74.2 reduce-scatter.2
  212.9 96.0 reduce-scatter.4

commit v8 on v7

--- a/solution.py
+++ b/solution.py
@@ -438,10 +438,11 @@
     order_d, part_l0 = lax.optimization_barrier((order, part_l0))
     shifts_l0 = [x_shift(part_l0, dx) for dx in (1, 3, 2)]
     d = attend(1, 1, b[-1], list(c[:4]), order_d)
-    gq1, gg1, dkv, car1 = d[:4]
+    gq1, gg1 = d[:2]
+    shifts_l0, far0, dkv, car1, late1 = lax.optimization_barrier((shifts_l0, bias0[2], d[2], d[3], d[-1]))
     sum1 = lax.psum_scatter(after(dkv, sum0), "col", scatter_dimension=0)
     swap1 = row_swap(car1)
-    shifts_l0, far0, swap1, late1, sum0 = lax.optimization_barrier((shifts_l0, bias0[2], swap1, d[-1], sum0))
+    swap1, sum0 = lax.optimization_barrier((swap1, sum0))
     pair1 = jnp.stack([car1, swap1])
     pairs1 = [pair1] + row_shifts(pair1)
     sum_l0 = add_all([part_l0[0:2]] + shifts_l0)
@@ -450,11 +451,9 @@
     bias1 = row_parts(late1)
     got_l0, got_bias0 = z_swap(sum_l0), row_swap(bias0[1])
     left1 = left_product(after(order, pairs1), cols, pairs1, right_t)
-    got_l0, got_bias0, bias1[1], bias1[3], left1 = lax.optimization_barrier(
-        (got_l0, got_bias0, bias1[1], bias1[3], left1)
-    )
+    got_l0, got_bias0, bias1, left1 = lax.optimization_barrier((got_l0, got_bias0, bias1, left1))
     part_l1 = add_pair(left1[0], core_swap(left1[1]))
-    bias1 = add_all(after(bias1, part_l1))
+    bias1 = add_all(bias1)
     sum_l1 = z_first(part_l1)
     left = jnp.concatenate([add_pair(sum_l0[0], got_l0), sum_l1])
     got_bias1 = after(row_swap(bias1[1]), sum_l1)

time: 357 us -> 355 us (level)
  waiting for transfers between devices: 93.2 us -> 86.1 us
    ppermute x1, waiting for transfers between devices: 1.03 us -> 21.3 us  [z_first(): got = lax.ppermute(part[:, 1], 'col', [(c, c ^ 2) for c in range(16)])]
    ppermute x21, waiting for transfers between devices: 57.2 us -> 39.6 us  [row_shift(): lax.ppermute(x, 'row', [(2 * y + z, 2 * ((y + dy) % 4) + z) for y in rang...]
    ppermute x3, waiting for transfers between devices: 12.2 us -> 0.01 us  [x_shift(): lax.ppermute(part[2 * dx:2 * dx + 2], 'col', [(c, (c + 4 * dx) % 16) for...]
    ppermute x5, waiting for transfers between devices: 11.8 us -> 17.1 us  [row_swap(): return lax.ppermute(x, 'row', [(r, r ^ 1) for r in range(8)])]
  transfers between devices with their start and end apart: 40 -> 40, of which waited for: 17 -> 15; matrix products, arithmetic and copies ran while one was open for 14% -> 15% of each run, Pallas kernels for 38% -> 38%
where the time goes in v8:
time: 355 us; the launch traced here: 349 us
  Pallas kernels  132 us (37%)
  waiting for transfers between devices  86.1 us (24%)
  starting transfers between devices  55.8 us (16%)
  local copies, waits for them, and re-layouts  40.3 us (11%)
  other arithmetic  19.5 us (5%)
  between operations  14.7 us (4%)
    pallas_call x4, Pallas kernels, attention(): pl.pallas_call(functools.partial(attention_kernel, h0, heads, total_heads...  98.3 us
    ppermute x21, waiting for transfers between devices, row_shift(): lax.ppermute(x, 'row', [(2 * y + z, 2 * ((y + dy) % 4) + z) for y in rang...  39.6 us
    pallas_call x2, Pallas kernels, left_product(): pl.pallas_call(left_kernel, grid_spec=pltpu.PrefetchScalarGridSpec(num_sc...  33.9 us
    ppermute x21, starting transfers between devices, row_shift(): lax.ppermute(x, 'row', [(2 * y + z, 2 * ((y + dy) % 4) + z) for y in rang...  29.6 us
    unnamed x53, local copies, waits for them, and re-layouts  29.1 us
    ppermute x1, waiting for transfers between devices, z_first(): got = lax.ppermute(part[:, 1], 'col', [(c, c ^ 2) for c in range(16)])  21.3 us
    ppermute x5, waiting for transfers between devices, row_swap(): return lax.ppermute(x, 'row', [(r, r ^ 1) for r in range(8)])  17.1 us
    ppermute x5, starting transfers between devices, row_swap(): return lax.ppermute(x, 'row', [(r, r ^ 1) for r in range(8)])  10 us
  transfers between devices with their start and end apart: 40, of which 15 were waited for; matrix products, arithmetic and copies ran while one was open for 15% of the time, Pallas kernels for 38%

profile of v8, /device:TPU:0, one launch (start us, length us, event | category | flops | bytes accessed | tf_op | source)
XLA Modules:
  0.0 348.6 jit_solution(7328301126308756642)
XLA Ops:
  11.2 4.0 %collective-permute-start = (bf16[4,192,384]{2,1,0:T(8,128)(2,1)S(1)}, bf16[4,192,384]{2,1,0:T(8,128)(2,1)S(1)}, u32[]{:S(2)}, u32[]{:S(2)}) collective-permute-start(bf16[4,192,384]{2,1,0:T(8,128)(2,1)S(1)} %add_convert_fusion.4), channel_id=1, source_target_pairs={{0,16},{16,0},{32,48},{48,32},{64,80},{80,64},{96,112},{112,96},{1... | collective-permute-start | bytes 1769480 | tf_op jit(solution)/shard_map/ppermute | solution.py:320
  16.1 3.0 collective-permute-start.5
  20.8 24.5 %copy.19 = bf16[192,384,128]{1,0,2:T(8,128)(2,1)} copy(bf16[192,384,128]{2,1,0:T(8,128)(2,1)} %param.19) | data formatting | bytes 37748736 | tf_op args[9]
  52.7 7.2 %collective-permute-done.6 = bf16[2,192,384]{2,1,0:T(8,128)(2,1)S(1)} collective-permute-done((bf16[2,192,384]{2,1,0:T(8,128)(2,1)S(1)}, bf16[2,192,384]{2,1,0:T(8,128)(2,1)S(1)}, u32[]{:S(2)}, u32[]{:S(2)}) %collective-permute-start.6) | collective-permute-done | bytes 294944 | tf_op jit(solution)/shard_map/ppermute | solution.py:316
  60.0 3.7 %collective-permute-done.2 = bf16[2,192,384]{2,1,0:T(8,128)(2,1)} collective-permute-done((bf16[2,192,384]{2,1,0:T(8,128)(2,1)S(1)}, bf16[2,192,384]{2,1,0:T(8,128)(2,1)}, u32[]{:S(2)}, u32[]{:S(2)}) %collective-permute-start.2) | collective-permute-done | bytes 294944 | tf_op jit(solution)/shard_map/ppermute | solution.py:316
  67.0 23.4 %attention_rows.4 = (bf16[4,192,128]{2,1,0:T(8,128)(2,1)}, bf16[4,192,128]{2,1,0:T(8,128)(2,1)}, bf16[4,64,3072]{2,1,0:T(8,128)(2,1)}, bf16[4,64,3072]{2,1,0:T(8,128)(2,1)}, f32[2,192,3072]{2,1,0:T(8,128)}) custom-call(s32[8]{0:T(128)} %stack.113.order_ref, bf16[4,192,128]{2,1,0:T(8,128)(2,1)} %get-tuple-element.213.refs_0_, ...), custom_call_target="tpu_custom_call" | custom-call | flops 9663676416 | bytes 30000000 | tf_op jit(solution)/shard_map/attention_rows/pallas_call | solution.py:235
  90.5 2.4 collective-permute-done.7.refs_9_.refs_10_
  93.8 24.9 %attention_rows.5 = (bf16[4,192,128]{2,1,0:T(8,128)(2,1)}, bf16[4,192,128]{2,1,0:T(8,128)(2,1)}, bf16[16,8,192,128]{3,2,1,0:T(8,128)(2,1)}, bf16[4,128,192]{2,1,0:T(8,128)(2,1)}, f32[2,192,3072]{2,1,0:T(8,128)}) custom-call(s32[8]{0:T(128)} %stack.113.order_ref, bf16[4,192,128]{2,1,0:T(8,128)(2,1)} %get-tuple-element.213.refs_0_, ...), custom_call_target="tpu_custom_call" | custom-call | flops 9663676416 | bytes 30000000 | tf_op jit(solution)/shard_map/attention_rows/pallas_call | solution.py:235
  121.7 7.8 %collective-permute-done.10 = bf16[4,128,192]{2,1,0:T(8,128)(2,1)S(1)} collective-permute-done((bf16[4,128,192]{2,1,0:T(8,128)(2,1)S(1)}, bf16[4,128,192]{2,1,0:T(8,128)(2,1)S(1)}, u32[]{:S(2)}, u32[]{:S(2)}) %collective-permute-start.10) | collective-permute-done | bytes 196640 | tf_op jit(solution)/shard_map/ppermute | solution.py:320
  132.9 24.2 %attention_rows.6 = (bf16[4,192,128]{2,1,0:T(8,128)(2,1)}, bf16[4,192,128]{2,1,0:T(8,128)(2,1)}, bf16[4,64,3072]{2,1,0:T(8,128)(2,1)}, bf16[4,64,3072]{2,1,0:T(8,128)(2,1)}, bf16[8,2,192,384]{3,2,1,0:T(8,128)(2,1)}) custom-call(s32[8]{0:T(128)} %stack.113.order_ref, bf16[4,192,128]{2,1,0:T(8,128)(2,1)} %get-tuple-element.217.refs_0_, ...), custom_call_target="tpu_custom_call" | custom-call | flops 9663676416 | bytes 30000000 | tf_op jit(solution)/shard_map/attention_rows/pallas_call | solution.py:235
  161.3 2.6 collective-permute-start.14
  163.8 17.0 %left_product.2 = (bf16[8,2,384,128]{3,2,1,0:T(8,128)(2,1)}, bf16[8,2,384,128]{3,2,1,0:T(8,128)(2,1)}) custom-call(s32[8]{0:T(128)} %stack.113.order_ref, s32[16]{0:T(128)} %stack.136.cols_ref, bf16[2,4,128,192]{3,2,1,0:T(8,128)(2,1)} %copy-done.5, bf16[2,4,128,192]{3,2,1,0:T(8,128)(2,1)} %copy-done.5, bf16[2,4,128,192]{3,2,1,0:T(8,128)(2,1)} %copy-done.23, ...), custom_call_target="tpu_custom_call" | custom-call | flops 40000000000 | bytes 30000000 | tf_op jit(solution)/shard_map/left_product/pallas_call | solution.py:296
  187.4 3.1 collective-permute-start.19
  192.9 25.8 %attention_rows.7 = (bf16[4,192,128]{2,1,0:T(8,128)(2,1)}, bf16[4,192,128]{2,1,0:T(8,128)(2,1)}, bf16[16,8,192,128]{3,2,1,0:T(8,128)(2,1)}, bf16[4,128,192]{2,1,0:T(8,128)(2,1)}, bf16[8,2,192,384]{3,2,1,0:T(8,128)(2,1)}) custom-call(s32[8]{0:T(128)} %stack.113.order_ref, bf16[4,192,128]{2,1,0:T(8,128)(2,1)} %get-tuple-element.217.refs_0_, ...), custom_call_target="tpu_custom_call" | custom-call | flops 9663676416 | bytes 30000000 | tf_op jit(solution)/shard_map/attention_rows/pallas_call | solution.py:235
  220.6 8.3 %collective-permute-done.21 = bf16[4,128,192]{2,1,0:T(8,128)(2,1)S(1)} collective-permute-done((bf16[4,128,192]{2,1,0:T(8,128)(2,1)S(1)}, bf16[4,128,192]{2,1,0:T(8,128)(2,1)S(1)}, u32[]{:S(2)}, u32[]{:S(2)}) %collective-permute-start.21) | collective-permute-done | bytes 196640 | tf_op jit(solution)/shard_map/ppermute | solution.py:320
  236.6 15.4 %collective-permute-done.24.refs_6_.refs_7_ = bf16[2,4,128,192]{3,2,1,0:T(8,128)(2,1)S(1)} collective-permute-done((bf16[2,4,128,192]{3,2,1,0:T(8,128)(2,1)S(1)}, bf16[2,4,128,192]{3,2,1,0:T(8,128)(2,1)S(1)}, u32[]{:S(2)}, u32[]{:S(2)}) %collective-permute-start.24) | collective-permute-done | bytes 393248 | tf_op jit(solution)/shard_map/ppermute | solution.py:316
  252.0 3.7 %collective-permute-done.22.refs_2_.refs_3_ = bf16[2,4,128,192]{3,2,1,0:T(8,128)(2,1)S(1)} collective-permute-done((bf16[2,4,128,192]{3,2,1,0:T(8,128)(2,1)S(1)}, bf16[2,4,128,192]{3,2,1,0:T(8,128)(2,1)S(1)}, u32[]{:S(2)}, u32[]{:S(2)}) %collective-permute-start.22) | collective-permute-done | bytes 393248 | tf_op jit(solution)/shard_map/ppermute | solution.py:316
  256.4 4.6 %collective-permute-start.25 = (bf16[2,384,128]{2,1,0:T(8,128)(2,1)}, bf16[2,384,128]{2,1,0:T(8,128)(2,1)}, u32[]{:S(2)}, u32[]{:S(2)}) collective-permute-start(bf16[2,384,128]{2,1,0:T(8,128)(2,1)} %slice_bitcast_fusion.11), channel_id=1, source_target_pairs={{0,2},{1,3},{2,0},{3,1},{4,6},{5,7},{6,4},{7,5},{8,10},{9,11},{10,... | collective-permute-start | bytes 589832 | tf_op jit(solution)/shard_map/ppermute | solution.py:352
  267.1 16.9 %left_product.3 = (bf16[8,2,384,128]{3,2,1,0:T(8,128)(2,1)}, bf16[8,2,384,128]{3,2,1,0:T(8,128)(2,1)}) custom-call(s32[8]{0:T(128)} %stack.113.order_ref, s32[16]{0:T(128)} %stack.136.cols_ref, bf16[2,4,128,192]{3,2,1,0:T(8,128)(2,1)} %copy-done.4, bf16[2,4,128,192]{3,2,1,0:T(8,128)(2,1)} %copy-done.4, bf16[2,4,128,192]{3,2,1,0:T(8,128)(2,1)} %copy-done.20, ...), custom_call_target="tpu_custom_call" | custom-call | flops 40000000000 | bytes 30000000 | tf_op jit(solution)/shard_map/left_product/pallas_call | solution.py:296
  284.9 6.4 %collective-permute-done.29 = bf16[2,2,192,384]{3,2,1,0:T(8,128)(2,1)} collective-permute-done((bf16[2,2,192,384]{3,2,1,0:T(8,128)(2,1)S(1)}, bf16[2,2,192,384]{3,2,1,0:T(8,128)(2,1)}, u32[]{:S(2)}, u32[]{:S(2)}) %collective-permute-start.29) | collective-permute-done | bytes 589856 | tf_op jit(solution)/shard_map/ppermute | solution.py:316
  299.1 3.3 collective-permute-start.35
  302.5 21.3 %collective-permute-done.31 = bf16[4,2,384,128]{3,2,1,0:T(8,128)(2,1)S(1)} collective-permute-done((bf16[4,2,384,128]{3,2,1,0:T(8,128)(2,1)S(1)}, bf16[4,2,384,128]{3,2,1,0:T(8,128)(2,1)S(1)}, u32[]{:S(2)}, u32[]{:S(2)}) %collective-permute-start.31) | collective-permute-done | bytes 786464 | tf_op jit(solution)/shard_map/ppermute | solution.py:357
  325.7 2.8 collective-permute-start.34
  333.0 4.1 %collective-permute-done.34 = bf16[2,384,128]{2,1,0:T(8,128)(2,1)S(1)} collective-permute-done((bf16[2,384,128]{2,1,0:T(8,128)(2,1)S(1)}, bf16[2,384,128]{2,1,0:T(8,128)(2,1)S(1)}, u32[]{:S(2)}, u32[]{:S(2)}) %collective-permute-start.34) | collective-permute-done | bytes 196640 | tf_op jit(solution)/shard_map/ppermute | solution.py:359
  (173 shorter events, 73.3 us)
Async XLA Ops:
  7.2 59.9 %all-gather.5.cloned.1.call-start = ((), (), s32[]{:S(2)}) async-start(), calls=%async_computation.4 | async-start | bytes 6684672 | tf_op jit(solution)/shard_map/all_gather | solution.py:413
  9.3 123.5 %all-gather.7.cloned.1.call-start = ((), (), s32[]{:S(2)}) async-start(), calls=%async_computation.5 | async-start | bytes 6684672 | tf_op jit(solution)/shard_map/all_gather | solution.py:413
  10.2 208.6 %reduce-scatter.3.cloned.1.call-start = ((), (), s32[]{:S(2)}) async-start(), calls=%async_computation.2 | async-start | bytes 6684672 | tf_op jit(solution)/shard_map/reduce_scatter | solution.py:427
  11.2 34.2 %collective-permute-start = (bf16[4,192,384]{2,1,0:T(8,128)(2,1)S(1)}, bf16[4,192,384]{2,1,0:T(8,128)(2,1)S(1)}, u32[]{:S(2)}, u32[]{:S(2)}) collective-permute-start(bf16[4,192,384]{2,1,0:T(8,128)(2,1)S(1)} %add_convert_fusion.4), channel_id=1, source_target_pairs={{0,16},{16,0},{32,48},{48,32},{64,80},{80,64},{96,112},{112,96},{1... | collective-permute-start | bytes 1769480 | tf_op jit(solution)/shard_map/ppermute | solution.py:320
  16.1 34.3 %collective-permute-start.5 = (bf16[2,192,384]{2,1,0:T(8,128)(2,1)S(1)}, bf16[2,192,384]{2,1,0:T(8,128)(2,1)}, u32[]{:S(2)}, u32[]{:S(2)}) collective-permute-start(bf16[2,192,384]{2,1,0:T(8,128)(2,1)S(1)} %get-tuple-element.163), channel_id=1, source_target_pairs={{0,96},{16,112},{32,0},{48,16},{64,32},{80,48},{96,64},{112,80},{1... | collective-permute-start | bytes 884744 | tf_op jit(solution)/shard_map/ppermute | solution.py:316
  19.1 33.7 %collective-permute-start.3 = (bf16[2,192,384]{2,1,0:T(8,128)(2,1)S(1)}, bf16[2,192,384]{2,1,0:T(8,128)(2,1)}, u32[]{:S(2)}, u32[]{:S(2)}) collective-permute-start(bf16[2,192,384]{2,1,0:T(8,128)(2,1)S(1)} %get-tuple-element.163), channel_id=1, source_target_pairs={{0,64},{16,80},{32,96},{48,112},{64,0},{80,16},{96,32},{112,48},{1... | collective-permute-start | bytes 884744 | tf_op jit(solution)/shard_map/ppermute | solution.py:316
  19.7 33.0 %collective-permute-start.1 = (bf16[2,192,384]{2,1,0:T(8,128)(2,1)S(1)}, bf16[2,192,384]{2,1,0:T(8,128)(2,1)}, u32[]{:S(2)}, u32[]{:S(2)}) collective-permute-start(bf16[2,192,384]{2,1,0:T(8,128)(2,1)S(1)} %get-tuple-element.163), channel_id=1, source_target_pairs={{0,32},{16,48},{32,64},{48,80},{64,96},{80,112},{96,0},{112,16},{1... | collective-permute-start | bytes 884744 | tf_op jit(solution)/shard_map/ppermute | solution.py:316
  63.7 26.7 %collective-permute-start.9 = (bf16[2,2,192,384]{3,2,1,0:T(8,128)(2,1)S(1)}, bf16[2,2,192,384]{3,2,1,0:T(8,128)(2,1)S(1)}, u32[]{:S(2)}, u32[]{:S(2)}) collective-permute-start(bf16[2,2,192,384]{3,2,1,0:T(8,128)(2,1)S(1)} %pad_maximum_fusion.1.refs_7_.refs_8_), channel_id=1, source_target_pairs={{0,96},{16,112},{32,0},{48,16},{64,32},{80,48},{96,64},{112,80},{1... | collective-permute-start | bytes 1769480 | tf_op jit(solution)/shard_map/ppermute | solution.py:316
  64.3 26.1 %collective-permute-start.8 = (bf16[2,2,192,384]{3,2,1,0:T(8,128)(2,1)S(1)}, bf16[2,2,192,384]{3,2,1,0:T(8,128)(2,1)S(1)}, u32[]{:S(2)}, u32[]{:S(2)}) collective-permute-start(bf16[2,2,192,384]{3,2,1,0:T(8,128)(2,1)S(1)} %pad_maximum_fusion.1.refs_7_.refs_8_), channel_id=1, source_target_pairs={{0,64},{16,80},{32,96},{48,112},{64,0},{80,16},{96,32},{112,48},{1... | collective-permute-start | bytes 1769480 | tf_op jit(solution)/shard_map/ppermute | solution.py:316
  66.3 26.6 %collective-permute-start.7 = (bf16[2,2,192,384]{3,2,1,0:T(8,128)(2,1)S(1)}, bf16[2,2,192,384]{3,2,1,0:T(8,128)(2,1)S(1)}, u32[]{:S(2)}, u32[]{:S(2)}) collective-permute-start(bf16[2,2,192,384]{3,2,1,0:T(8,128)(2,1)S(1)} %pad_maximum_fusion.1.refs_7_.refs_8_), channel_id=1, source_target_pairs={{0,32},{16,48},{32,64},{48,80},{64,96},{80,112},{96,0},{112,16},{1... | collective-permute-start | bytes 1769480 | tf_op jit(solution)/shard_map/ppermute | solution.py:316
  118.7 220.5 %reduce-scatter.5.cloned.1.call-start = ((), (), s32[]{:S(2)}) async-start(), calls=%async_computation.3 | async-start | bytes 6684672 | tf_op jit(solution)/shard_map/reduce_scatter | solution.py:443
  129.7 27.4 %collective-permute-start.13 = (bf16[2,4,128,192]{3,2,1,0:T(8,128)(2,1)S(1)}, bf16[2,4,128,192]{3,2,1,0:T(8,128)(2,1)S(1)}, u32[]{:S(2)}, u32[]{:S(2)}) collective-permute-start(bf16[2,4,128,192]{3,2,1,0:T(8,128)(2,1)S(1)} %pad_maximum_fusion.2.refs_0_.refs_1_), channel_id=1, source_target_pairs={{0,96},{16,112},{32,0},{48,16},{64,32},{80,48},{96,64},{112,80},{1... | collective-permute-start | bytes 1179656 | tf_op jit(solution)/shard_map/ppermute | solution.py:316
  129.8 27.3 %collective-permute-start.12 = (bf16[2,4,128,192]{3,2,1,0:T(8,128)(2,1)S(1)}, bf16[2,4,128,192]{3,2,1,0:T(8,128)(2,1)S(1)}, u32[]{:S(2)}, u32[]{:S(2)}) collective-permute-start(bf16[2,4,128,192]{3,2,1,0:T(8,128)(2,1)S(1)} %pad_maximum_fusion.2.refs_0_.refs_1_), channel_id=1, source_target_pairs={{0,64},{16,80},{32,96},{48,112},{64,0},{80,16},{96,32},{112,48},{1... | collective-permute-start | bytes 1179656 | tf_op jit(solution)/shard_map/ppermute | solution.py:316
  131.4 25.8 %collective-permute-start.11 = (bf16[2,4,128,192]{3,2,1,0:T(8,128)(2,1)S(1)}, bf16[2,4,128,192]{3,2,1,0:T(8,128)(2,1)S(1)}, u32[]{:S(2)}, u32[]{:S(2)}) collective-permute-start(bf16[2,4,128,192]{3,2,1,0:T(8,128)(2,1)S(1)} %pad_maximum_fusion.2.refs_0_.refs_1_), channel_id=1, source_target_pairs={{0,32},{16,48},{32,64},{48,80},{64,96},{80,112},{96,0},{112,16},{1... | collective-permute-start | bytes 1179656 | tf_op jit(solution)/shard_map/ppermute | solution.py:316
  180.9 37.9 %collective-permute-start.20 = (bf16[2,2,192,384]{3,2,1,0:T(8,128)(2,1)S(1)}, bf16[2,2,192,384]{3,2,1,0:T(8,128)(2,1)}, u32[]{:S(2)}, u32[]{:S(2)}) collective-permute-start(bf16[2,2,192,384]{3,2,1,0:T(8,128)(2,1)S(1)} %get-tuple-element.150), channel_id=1, source_target_pairs={{0,64},{16,80},{32,96},{48,112},{64,0},{80,16},{96,32},{112,48},{1... | collective-permute-start | bytes 1769480 | tf_op jit(solution)/shard_map/ppermute | solution.py:316
  187.4 31.4 %collective-permute-start.19 = (bf16[2,2,384,128]{3,2,1,0:T(8,128)(2,1)}, bf16[2,2,384,128]{3,2,1,0:T(8,128)(2,1)}, u32[]{:S(2)}, u32[]{:S(2)}) collective-permute-start(bf16[2,2,384,128]{3,2,1,0:T(8,128)(2,1)} %get-tuple-element.153), channel_id=1, source_target_pairs={{0,8},{1,9},{2,10},{3,11},{4,12},{5,13},{6,14},{7,15},{8,0},{9,1},... | collective-permute-start | bytes 1179656 | tf_op jit(solution)/shard_map/ppermute | solution.py:348
  190.5 28.3 %collective-permute-start.18 = (bf16[2,2,384,128]{3,2,1,0:T(8,128)(2,1)}, bf16[2,2,384,128]{3,2,1,0:T(8,128)(2,1)}, u32[]{:S(2)}, u32[]{:S(2)}) collective-permute-start(bf16[2,2,384,128]{3,2,1,0:T(8,128)(2,1)} %get-tuple-element.154), channel_id=1, source_target_pairs={{0,12},{1,13},{2,14},{3,15},{4,0},{5,1},{6,2},{7,3},{8,4},{9,5},{1... | collective-permute-start | bytes 1179656 | tf_op jit(solution)/shard_map/ppermute | solution.py:348
  192.0 26.8 %collective-permute-start.17 = (bf16[2,2,384,128]{3,2,1,0:T(8,128)(2,1)S(1)}, bf16[2,2,384,128]{3,2,1,0:T(8,128)(2,1)}, u32[]{:S(2)}, u32[]{:S(2)}) collective-permute-start(bf16[2,2,384,128]{3,2,1,0:T(8,128)(2,1)S(1)} %get-tuple-element.155), channel_id=1, source_target_pairs={{0,4},{1,5},{2,6},{3,7},{4,8},{5,9},{6,10},{7,11},{8,12},{9,13},{1... | collective-permute-start | bytes 1179656 | tf_op jit(solution)/shard_map/ppermute | solution.py:348
  256.4 27.5 %collective-permute-start.25 = (bf16[2,384,128]{2,1,0:T(8,128)(2,1)}, bf16[2,384,128]{2,1,0:T(8,128)(2,1)}, u32[]{:S(2)}, u32[]{:S(2)}) collective-permute-start(bf16[2,384,128]{2,1,0:T(8,128)(2,1)} %slice_bitcast_fusion.11), channel_id=1, source_target_pairs={{0,2},{1,3},{2,0},{3,1},{4,6},{5,7},{6,4},{7,5},{8,10},{9,11},{10,... | collective-permute-start | bytes 589832 | tf_op jit(solution)/shard_map/ppermute | solution.py:352
  262.6 28.7 %collective-permute-start.29 = (bf16[2,2,192,384]{3,2,1,0:T(8,128)(2,1)S(1)}, bf16[2,2,192,384]{3,2,1,0:T(8,128)(2,1)}, u32[]{:S(2)}, u32[]{:S(2)}) collective-permute-start(bf16[2,2,192,384]{3,2,1,0:T(8,128)(2,1)S(1)} %get-tuple-element.146), channel_id=1, source_target_pairs={{0,32},{16,48},{32,64},{48,80},{64,96},{80,112},{96,0},{112,16},{1... | collective-permute-start | bytes 1769480 | tf_op jit(solution)/shard_map/ppermute | solution.py:316
  263.2 28.2 %collective-permute-start.28 = (bf16[2,2,192,384]{3,2,1,0:T(8,128)(2,1)S(1)}, bf16[2,2,192,384]{3,2,1,0:T(8,128)(2,1)}, u32[]{:S(2)}, u32[]{:S(2)}) collective-permute-start(bf16[2,2,192,384]{3,2,1,0:T(8,128)(2,1)S(1)} %get-tuple-element.147), channel_id=1, source_target_pairs={{0,64},{16,80},{32,96},{48,112},{64,0},{80,16},{96,32},{112,48},{1... | collective-permute-start | bytes 1769480 | tf_op jit(solution)/shard_map/ppermute | solution.py:316
  264.8 27.2 %collective-permute-start.27 = (bf16[2,2,192,384]{3,2,1,0:T(8,128)(2,1)S(1)}, bf16[2,2,192,384]{3,2,1,0:T(8,128)(2,1)}, u32[]{:S(2)}, u32[]{:S(2)}) collective-permute-start(bf16[2,2,192,384]{3,2,1,0:T(8,128)(2,1)S(1)} %get-tuple-element.148), channel_id=1, source_target_pairs={{0,96},{16,112},{32,0},{48,16},{64,32},{80,48},{96,64},{112,80},{1... | collective-permute-start | bytes 1769480 | tf_op jit(solution)/shard_map/ppermute | solution.py:316
  297.2 26.5 %collective-permute-start.31 = (bf16[4,2,384,128]{3,2,1,0:T(8,128)(2,1)S(1)}, bf16[4,2,384,128]{3,2,1,0:T(8,128)(2,1)S(1)}, u32[]{:S(2)}, u32[]{:S(2)}) collective-permute-start(bf16[4,2,384,128]{3,2,1,0:T(8,128)(2,1)S(1)} %slice_bitcast_fusion), channel_id=1, source_target_pairs={{0,2},{1,3},{2,0},{3,1},{4,6},{5,7},{6,4},{7,5},{8,10},{9,11},{10,... | collective-permute-start | bytes 2359304 | tf_op jit(solution)/shard_map/ppermute | solution.py:357
  299.1 38.1 %collective-permute-start.35 = (bf16[2,192,384]{2,1,0:T(8,128)(2,1)S(1)}, bf16[2,192,384]{2,1,0:T(8,128)(2,1)S(1)}, u32[]{:S(2)}, u32[]{:S(2)}) collective-permute-start(bf16[2,192,384]{2,1,0:T(8,128)(2,1)S(1)} %slice_bitcast_fusion.2), channel_id=1, source_target_pairs={{0,16},{16,0},{32,48},{48,32},{64,80},{80,64},{96,112},{112,96},{1... | collective-permute-start | bytes 884744 | tf_op jit(solution)/shard_map/ppermute | solution.py:320
  (42 other events, 432.2 us)
Sparse Core Ops, SparseCore 0:
  10.3 50.1 all-gather.4
  62.8 41.5 all-gather.6
  118.8 74.2 reduce-scatter.2
  219.0 95.2 reduce-scatter.4
